TPU v7x, 512 devices: a whole 4x4x16 slice. The times are simulated.
512 devices in a mesh: ctx: 16 (over z_lo, core), exp: 32 (over z_hi, x, y).
Axes of the slice: x: 4, y: 4, z: 16 (z_hi: 2, z_lo: 8; z = z_hi * 8 + z_lo), core: 2. Of those that a mesh axis runs over, the one named last changes fastest.
Arguments:
- residual: bfloat16 [32, 2048, 1024], P('exp', 'ctx'), may hold values from -6 to 6
- query_rows: bfloat16 [32, 2048, 1024], P('exp', 'ctx'), may hold values from -8 to 8
- key_rows: bfloat16 [32, 2048, 1024], P('exp', 'ctx'), may hold values from -4 to 4
- value_rows: bfloat16 [32, 2048, 1024], P('exp', 'ctx'), may hold values from -6 to 6
- out_proj: bfloat16 [1024, 1024], P('exp'), may hold values from -0.75 to 0.75
- router: bfloat16 [1024, 32], replicated, may hold values from -0.5 to 0.5
- expert_ids: int32 [32, 2048, 2], P('exp', 'ctx'), may hold values from 0 to 31, all different within a row; in each aligned block of 128 rows (0 to 127, 128 to 255, ..., all dimensions but the last counted through in order) at most 12 rows name the same one
- expert_gate_up: bfloat16 [32, 1024, 1536], P('exp', 'ctx'), may hold values from -0.1875 to 0.1875
- expert_down: bfloat16 [32, 768, 1024], P('exp', 'ctx'), may hold values from -0.21875 to 0.21875
Outputs:
- layer_out: bfloat16 [32, 2048, 1024], P('exp', 'ctx')
Inputs may be any that keep to these rules, and one draw needn't show every extreme that they name: `expert_ids`: the 2 ids of a token differ. Among the 128 tokens of one device (aligned blocks of 128 tokens of the flattened sequences) each expert is named at most 12 times, a bound that some block reaches.
All inputs are finite; a program needn't handle non-finite values.
Results may differ from a plain program's by a relative error of at most 0.017.
Values may be sent and summed in bfloat16 or wider, within the bound.
No kernel may reach another device: no remote copies, remote signals or barrier semaphores. Data moves between devices by JAX's collectives and lax.ppermute only.
A program may use at most 64 MiB of HBM per device.

v0:
```python
import jax
import jax.numpy as jnp
from jax import lax
from jax.sharding import PartitionSpec as P

HEADS = 8
HEAD_DIM = 128
TOP = 2


NEG_FILL = -1e30


def attend_moving_keys(query_heads, work_pos, key_rows, value_rows, scale_factor):
    token_count = query_heads.shape[0]
    latest = jnp.max(work_pos)
    initial = (
        jnp.full((token_count, HEADS), NEG_FILL, jnp.float32),
        jnp.zeros((token_count, HEADS), jnp.float32),
        jnp.zeros((token_count, HEADS, HEAD_DIM), jnp.float32),
    )
    key_piece = lax.all_gather(key_rows, "ctx", axis=1, tiled=True)
    value_piece = lax.all_gather(value_rows, "ctx", axis=1, tiled=True)
    piece_len = key_piece.shape[1]

    def update(state):
        run_max, run_sum, run_acc = state
        key_heads = key_piece[0].reshape(piece_len, HEADS, HEAD_DIM)
        value_heads = value_piece[0].reshape(piece_len, HEADS, HEAD_DIM)
        scores = (
            jnp.einsum("qhd,khd->qhk", query_heads, key_heads, preferred_element_type=jnp.float32)
            * scale_factor
        )
        key_pos = jnp.arange(piece_len, dtype=jnp.int32)
        allowed = key_pos[None, None, :] <= work_pos[:, None, None]
        new_max = jnp.maximum(run_max, jnp.max(jnp.where(allowed, scores, NEG_FILL), axis=2))
        weights = jnp.where(allowed, jnp.exp(scores - new_max[:, :, None]), 0.0)
        new_sum = jnp.sum(weights, axis=2)
        new_acc = jnp.einsum(
            "qhk,khd->qhd",
            weights.astype(jnp.bfloat16),
            value_heads,
            preferred_element_type=jnp.float32,
        )
        return (new_max, new_sum, new_acc)

    run_max, run_sum, run_acc = lax.cond(
        jnp.int32(0) > latest, lambda unchanged: unchanged, update, initial
    )
    return (
        (run_acc / run_sum[:, :, None]).reshape(token_count, HEADS * HEAD_DIM).astype(jnp.bfloat16)
    )


def on_device(
    residual,
    query_rows,
    key_rows,
    value_rows,
    out_proj,
    router,
    expert_ids,
    expert_gate_up,
    expert_down,
):
    token_count = residual.shape[1]
    model_width = residual.shape[2]
    cycle_index = lax.axis_index("ctx")
    scale_factor = HEAD_DIM ** (-0.5)
    local_queries = query_rows[0]
    offsets = jnp.arange(token_count, dtype=jnp.int32)
    work_pos = cycle_index * token_count + offsets
    query_heads = local_queries.reshape(token_count, HEADS, HEAD_DIM)
    context_rows = attend_moving_keys(query_heads, work_pos, key_rows, value_rows, scale_factor)
    attn_out = jnp.dot(
        context_rows,
        lax.all_gather(out_proj, "exp", axis=0, tiled=True),
        preferred_element_type=jnp.float32,
    )
    hidden_state = (residual[0].astype(jnp.float32) + attn_out).astype(jnp.bfloat16)
    hidden_wide = hidden_state.astype(jnp.float32)
    mean_square = jnp.mean(hidden_wide * hidden_wide, axis=1, keepdims=True)
    normed = (hidden_wide * lax.rsqrt(mean_square + 1e-06)).astype(jnp.bfloat16)
    affinity = jax.nn.sigmoid(jnp.dot(normed, router, preferred_element_type=jnp.float32))
    chosen_ids = expert_ids[0]
    picked = jnp.take_along_axis(affinity, chosen_ids, axis=1)
    gate_share = picked / jnp.sum(picked, axis=1, keepdims=True)
    expert_count = router.shape[1]
    capacity = min(token_count, 3 * token_count // lax.axis_size("exp"))
    pair_ids = chosen_ids.reshape(token_count * TOP)
    one_hot = (pair_ids[:, None] == jnp.arange(expert_count, dtype=jnp.int32)[None, :]).astype(
        jnp.int32
    )
    earlier = jnp.cumsum(one_hot, axis=0) - one_hot
    slot_index = jnp.sum(earlier * one_hot, axis=1)
    target = pair_ids * capacity + slot_index
    slot_grid = jnp.arange(expert_count * capacity, dtype=jnp.int32)
    dispatch = jnp.any(
        slot_grid[:, None, None] == target.reshape(token_count, TOP)[None], axis=2
    ).astype(jnp.bfloat16)
    outgoing = jnp.dot(dispatch, normed, preferred_element_type=jnp.float32).astype(jnp.bfloat16)
    outgoing = outgoing.reshape(expert_count, capacity, model_width)
    full_gate_up, full_down = (
        lax.all_gather(expert_gate_up, "ctx", axis=1, tiled=True),
        lax.all_gather(expert_down, "ctx", axis=1, tiled=True),
    )
    ff_width = full_down.shape[1]
    arrived = lax.all_to_all(outgoing, "exp", split_axis=0, concat_axis=0, tiled=True)
    flat_feats = arrived.reshape(-1, model_width)
    gate_up_out = jnp.dot(flat_feats, full_gate_up[0], preferred_element_type=jnp.float32)
    activation = (jax.nn.silu(gate_up_out[:, :ff_width]) * gate_up_out[:, ff_width:]).astype(
        jnp.bfloat16
    )
    produced = jnp.dot(activation, full_down[0], preferred_element_type=jnp.float32).astype(
        jnp.bfloat16
    )
    returned_rows = lax.all_to_all(
        produced.reshape(arrived.shape), "exp", split_axis=0, concat_axis=0, tiled=True
    )
    flat_back = returned_rows.reshape(expert_count * capacity, model_width)
    pair_out = (
        jnp.take(flat_back, target, axis=0)
        .reshape(token_count, TOP, model_width)
        .astype(jnp.float32)
    )
    moe_out = jnp.sum(gate_share[:, :, None] * pair_out, axis=1)
    return (hidden_wide + moe_out).astype(jnp.bfloat16)[None]


def solution(mesh):
    return jax.shard_map(
        on_device,
        mesh=mesh,
        in_specs=(
            P("exp", "ctx", None),
            P("exp", "ctx", None),
            P("exp", "ctx", None),
            P("exp", "ctx", None),
            P("exp", None),
            P(),
            P("exp", "ctx", None),
            P("exp", "ctx", None),
            P("exp", "ctx", None),
        ),
        out_specs=P("exp", "ctx", None),
        check_vma=False,
    )
```

profile of v0, /device:TPU:6, one launch (start us, length us, event | category | flops | bytes accessed | tf_op | source)
XLA Modules:
  0.0 662.5 jit_solution(16331421266565729832)
XLA Ops:
  6.5 0.7 all-gather.6.cloned.1.call-update
  7.3 0.7 all-gather.8.cloned.1.call-update
  8.1 0.7 all-gather.10.cloned.1.call-update
  8.8 0.5 all-gather.12.cloned.1.call-update
  9.3 0.8 copy.47
  10.1 0.1 eq.41
  10.2 0.1 reshape_squeeze.7
  10.4 0.6 fusion.49
  11.7 0.6 reduce-window.6
  12.3 0.2 slice_reduce_fusion
  12.6 0.1 reduce_sum.55
  12.9 107.8 %all-gather.6.cloned.1.call-done = bf16[1,2048,1024]{2,1,0:T(8,128)(2,1)} async-done(((bf16[1,128,1024]{2,1,0:T(8,128)(2,1)}), bf16[1,2048,1024]{2,1,0:T(8,128)(2,1)}) %all-gather.6.cloned.1.call-update) | async-done | bytes 4194320 | tf_op jit(solution)/shard_map/all_gather | solution.py:22
  120.8 106.9 %all-gather.8.cloned.1.call-done = bf16[1,2048,1024]{2,1,0:T(8,128)(2,1)} async-done(((bf16[1,128,1024]{2,1,0:T(8,128)(2,1)}), bf16[1,2048,1024]{2,1,0:T(8,128)(2,1)}) %all-gather.8.cloned.1.call-update) | async-done | bytes 4194320 | tf_op jit(solution)/shard_map/all_gather | solution.py:23
  227.7 12.0 %conditional.1 = (f32[128,8]{0,1:T(8,128)S(1)}, f32[128,8,128]{0,2,1:T(8,128)S(1)}) conditional(s32[]{:T(128)} %convert_element_type.52, (s32[128]{0:T(128)S(1)}, bf16[1,2048,1024]{2,1,0:T(8,128)(2,1)}, bf16[1,128,1024]{2,1,0:T(8,128)(2,1)}, bf16[1,2048,1024]{2,1,0:T(8,128)(2,1)}) %tuple.13, () %tuple.14), branch_computations={%region_1.4_spmd, %region_4.5_spmd} | conditional | flops 1097071616 | bytes 71590472 | solution.py:47
  227.7 3.3 copy.57
  231.0 0.2 iota_compare_fusion
  231.3 1.7 fusion
  233.0 1.7 fusion.4
  234.7 0.5 copy-done.1
  235.1 1.1 copy.59
  236.2 3.2 fusion.14
  239.5 0.2 copy.55
  239.7 120.6 %all-gather.10.cloned.1.call-done = bf16[1024,1024]{1,0:T(8,128)(2,1)} async-done(((bf16[32,1024]{1,0:T(8,128)(2,1)}), bf16[1024,1024]{1,0:T(8,128)(2,1)}) %all-gather.10.cloned.1.call-update) | async-done | bytes 2097168 | tf_op jit(solution)/shard_map/all_gather | solution.py:77
  360.3 2.1 multiply_reduce_fusion.1
  362.5 0.4 convolution_convert_fusion
  362.9 1.2 reshape.176
  364.1 6.8 %all-to-all-start = ((bf16[32,12,1024]{2,1,0:T(8,128)(2,1)}), bf16[32,12,1024]{2,1,0:T(8,128)(2,1)S(1)}, u32[]{:S(2)}, u32[]{:S(2)}) async-start(bf16[32,12,1024]{2,1,0:T(8,128)(2,1)} %reshape.176), calls=%async_computation | async-start | bytes 2097152 | tf_op jit(solution)/shard_map/all_to_all | solution.py:108
  370.9 0.2 all-gather.14.cloned.1.call-start
  371.1 0.4 all-gather.14.cloned.1.call-update
  371.5 63.7 %all-to-all-done = bf16[32,12,1024]{2,1,0:T(8,128)(2,1)S(1)} async-done(((bf16[32,12,1024]{2,1,0:T(8,128)(2,1)}), bf16[32,12,1024]{2,1,0:T(8,128)(2,1)S(1)}, u32[]{:S(2)}, u32[]{:S(2)}) %all-to-all-start) | async-done | bytes 786464 | tf_op jit(solution)/shard_map/all_to_all | solution.py:108
  435.2 0.2 reshape.177
  435.3 47.1 %all-gather.12.cloned.1.call-done = bf16[1,1024,1536]{2,1,0:T(8,128)(2,1)} async-done(((bf16[1,64,1536]{2,1,0:T(8,128)(2,1)}), bf16[1,1024,1536]{2,1,0:T(8,128)(2,1)}) %all-gather.12.cloned.1.call-update) | async-done | bytes 3145744 | tf_op jit(solution)/shard_map/all_gather | solution.py:104
  482.5 4.7 fusion.22
  487.2 98.0 %all-gather.14.cloned.1.call-done = bf16[1,768,1024]{2,1,0:T(8,128)(2,1)} async-done(((bf16[1,48,1024]{2,1,0:T(8,128)(2,1)}), bf16[1,768,1024]{2,1,0:T(8,128)(2,1)}) %all-gather.14.cloned.1.call-update) | async-done | bytes 1572880 | tf_op jit(solution)/shard_map/all_gather | solution.py:105
  585.1 2.9 fusion.26
  588.1 1.2 reshape.178
  589.2 42.7 %all-to-all-start.1 = ((bf16[32,12,1024]{2,1,0:T(8,128)(2,1)}), bf16[32,12,1024]{2,1,0:T(8,128)(2,1)S(1)}, u32[]{:S(2)}, u32[]{:S(2)}) async-start(bf16[32,12,1024]{2,1,0:T(8,128)(2,1)} %reshape.178), calls=%async_computation.1 | async-start | bytes 2097152 | tf_op jit(solution)/shard_map/all_to_all | solution.py:117
  631.9 0.1 reduce_sum.54
  632.2 0.1 reshape.189
  632.3 0.1 mul.74
  632.5 0.3 fusion.34
  632.8 2.0 gather_fusion.1
  635.2 16.9 %all-to-all-done.1 = bf16[32,12,1024]{2,1,0:T(8,128)(2,1)S(1)} async-done(((bf16[32,12,1024]{2,1,0:T(8,128)(2,1)}), bf16[32,12,1024]{2,1,0:T(8,128)(2,1)S(1)}, u32[]{:S(2)}, u32[]{:S(2)}) %all-to-all-start.1) | async-done | bytes 786464 | tf_op jit(solution)/shard_map/all_to_all | solution.py:117
  652.0 0.2 reshape.179
  652.2 1.2 gather_fusion
  653.4 0.2 gather.12
  653.6 1.7 multiply_reduce_fusion
  655.2 0.8 fusion.38
  (33 shorter events, 1.0 us)
Async XLA Ops:
  6.5 626.0 %copy-start = (bf16[1024,32]{0,1:T(8,128)(2,1)S(1)}, bf16[1024,32]{0,1:T(8,128)(2,1)}, u32[]{:S(2)}) copy-start(bf16[1024,32]{0,1:T(8,128)(2,1)} %param.16) | copy-start | bytes 196612
  6.5 114.2 %all-gather.6.cloned.1.call-start = ((), (), s32[]{:S(2)}) async-start(), calls=%async_computation.2 | async-start | bytes 4456448 | tf_op jit(solution)/shard_map/all_gather | solution.py:22
  7.3 220.4 %all-gather.8.cloned.1.call-start = ((), (), s32[]{:S(2)}) async-start(), calls=%async_computation.3 | async-start | bytes 4456448 | tf_op jit(solution)/shard_map/all_gather | solution.py:23
  8.0 352.3 %all-gather.10.cloned.1.call-start = ((), (), s32[]{:S(2)}) async-start(), calls=%async_computation.4 | async-start | bytes 2162688 | tf_op jit(solution)/shard_map/all_gather | solution.py:77
  8.7 473.7 %all-gather.12.cloned.1.call-start = ((), (), s32[]{:S(2)}) async-start(), calls=%async_computation.5 | async-start | bytes 3342336 | tf_op jit(solution)/shard_map/all_gather | solution.py:104
  227.7 132.6 %copy-start.3 = (bf16[1,128,1024]{2,1,0:T(8,128)(2,1)S(1)}, bf16[1,128,1024]{2,1,0:T(8,128)(2,1)}, u32[]{:S(2)}) copy-start(bf16[1,128,1024]{2,1,0:T(8,128)(2,1)} %param.11) | copy-start | bytes 786436
  227.7 3.5 copy-start.2
  233.0 2.2 copy-start.1
  364.1 71.1 %all-to-all-start = ((bf16[32,12,1024]{2,1,0:T(8,128)(2,1)}), bf16[32,12,1024]{2,1,0:T(8,128)(2,1)S(1)}, u32[]{:S(2)}, u32[]{:S(2)}) async-start(bf16[32,12,1024]{2,1,0:T(8,128)(2,1)} %reshape.176), calls=%async_computation | async-start | bytes 2097152 | tf_op jit(solution)/shard_map/all_to_all | solution.py:108
  370.9 214.3 %all-gather.14.cloned.1.call-start = ((), (), s32[]{:S(2)}) async-start(), calls=%async_computation.6 | async-start | bytes 1671168 | tf_op jit(solution)/shard_map/all_gather | solution.py:105
  487.2 144.9 %copy-start.4 = (s32[1,128,2]{1,2,0:T(2,128)S(1)}, s32[1,128,2]{1,2,0:T(2,128)}, u32[]{:S(2)}) copy-start(s32[1,128,2]{1,2,0:T(2,128)} %param.17) | copy-start | bytes 3076
  589.2 62.8 %all-to-all-start.1 = ((bf16[32,12,1024]{2,1,0:T(8,128)(2,1)}), bf16[32,12,1024]{2,1,0:T(8,128)(2,1)S(1)}, u32[]{:S(2)}, u32[]{:S(2)}) async-start(bf16[32,12,1024]{2,1,0:T(8,128)(2,1)} %reshape.178), calls=%async_computation.1 | async-start | bytes 2097152 | tf_op jit(solution)/shard_map/all_to_all | solution.py:117
Sparse Core Ops, SparseCore 0:
  9.4 111.2 all-gather.5
  122.8 104.8 all-gather.7
  232.1 128.1 all-gather.9
  362.3 120.1 all-gather.11
  484.4 100.6 all-gather.13
where the time goes:
time: 663 us
  waiting for transfers between devices  564 us (85%)
  starting transfers between devices  49.8 us (8%)
  matrix products  15.3 us (2%)
  between operations  14 us (2%)
  local copies, waits for them, and re-layouts  13.3 us (2%)
    all_gather x1, waiting for transfers between devices, on_device(): lax.all_gather(out_proj, 'exp', axis=0, tiled=True)  121 us
    all_gather x1, waiting for transfers between devices, attend_moving_keys(): key_piece = lax.all_gather(key_rows, 'ctx', axis=1, tiled=True)  108 us
    all_gather x1, waiting for transfers between devices, attend_moving_keys(): value_piece = lax.all_gather(value_rows, 'ctx', axis=1, tiled=True)  107 us
    all_gather x1, waiting for transfers between devices, on_device(): lax.all_gather(expert_down, 'ctx', axis=1, tiled=True)  98 us
    all_to_all x1, waiting for transfers between devices, on_device(): lax.all_to_all(outgoing, 'exp', split_axis=0, concat_axis=0, tiled=True)  63.7 us
    all_gather x1, waiting for transfers between devices, on_device(): lax.all_gather(expert_gate_up, 'ctx', axis=1, tiled=True)  47.1 us
    all_to_all x1, starting transfers between devices, on_device(): lax.all_to_all(produced.reshape(arrived.shape), 'exp', split_axis=0, conc...  42.7 us
    all_to_all x1, waiting for transfers between devices, on_device(): lax.all_to_all(produced.reshape(arrived.shape), 'exp', split_axis=0, conc...  16.9 us
  transfers between devices with their start and end apart: 7, of which 7 were waited for; matrix products, arithmetic and copies ran while one was open for 4% of the time, Pallas kernels for 0%

commit v1 on v0

v1 whole, which is shorter than its diff:
```python
import functools

import jax
import jax.numpy as jnp
from jax import lax
from jax.experimental import pallas as pl
from jax.experimental.pallas import tpu as pltpu
from jax.sharding import Mesh, PartitionSpec as P

HEADS = 8
HEAD_DIM = 128
TOP = 2
SLOT = 16
NEG_FILL = -1e30
LOG2E = 1.4426950408889634
BF = jnp.bfloat16
F32 = jnp.float32
ALL = ("zlo", "core", "zhi", "xy")

VMEM = pl.BlockSpec(memory_space=pltpu.VMEM)
SMEM = pl.BlockSpec(memory_space=pltpu.SMEM)
ANY = pl.BlockSpec(memory_space=pl.ANY)


def linear(zlo, core, zhi, xy):
    return ((zlo * 2 + core) * 2 + zhi) * 16 + xy


def all_pairs(move):
    pairs = []
    for zlo in range(8):
        for core in range(2):
            for zhi in range(2):
                for xy in range(16):
                    target = move(zlo, core, zhi, xy)
                    if target is not None:
                        pairs.append((linear(zlo, core, zhi, xy), linear(*target)))
    return pairs


CORE_SWAP = all_pairs(lambda zlo, core, zhi, xy: (zlo, 1 - core, zhi, xy))
HALF_MOVE = all_pairs(lambda zlo, core, zhi, xy: (zlo, core, 1 - zhi, xy) if zhi == core else None)


def params(mib):
    return pltpu.CompilerParams(vmem_limit_bytes=mib << 20)


def pack_weights_kernel(up_ref, down_ref, out_ref):
    out_ref[0:64, :] = up_ref[0, :, 0:1024]
    out_ref[64:96, 0:512] = up_ref[0, 0:32, 1024:1536]
    out_ref[64:96, 512:1024] = up_ref[0, 32:64, 1024:1536]
    out_ref[96:144, :] = down_ref[0]


def pack_weights(gate_up, down):
    return pl.pallas_call(
        pack_weights_kernel,
        out_shape=jax.ShapeDtypeStruct((144, 1024), BF),
        in_specs=[VMEM, VMEM],
        out_specs=VMEM,
        compiler_params=params(8),
    )(gate_up, down)


def pack_heads_kernel(q_ref, k_ref, v_ref, out_ref):
    for h in range(HEADS):
        for c in range(2):
            for j, ref in enumerate((q_ref, k_ref, v_ref)):
                out_ref[h * 2 + c, j * 64 : (j + 1) * 64, :] = ref[
                    0, c * 64 : (c + 1) * 64, h * 128 : (h + 1) * 128
                ]


def pack_heads(q, k, v):
    return pl.pallas_call(
        pack_heads_kernel,
        out_shape=jax.ShapeDtypeStruct((16, 192, 128), BF),
        in_specs=[VMEM] * 3,
        out_specs=VMEM,
        compiler_params=params(8),
    )(q, k, v)


def attention_kernel(core_ref, own_ref, oth_ref, out_ref):
    core = core_ref[0]
    queries = own_ref[:, 0:64, :].reshape(1024, 128)
    own_keys = own_ref[:, 64:128, :].reshape(1024, 128)
    own_values = own_ref[:, 128:192, :].reshape(1024, 128)
    oth_keys = oth_ref[:, 0:64, :].reshape(1024, 128)
    oth_values = oth_ref[:, 64:128, :].reshape(1024, 128)
    scale = (HEAD_DIM ** (-0.5)) * LOG2E
    rows = 256
    row = lax.broadcasted_iota(jnp.int32, (rows, rows), 0)
    col = lax.broadcasted_iota(jnp.int32, (rows, rows), 1)
    own_allowed = col <= row
    oth_allowed = (col // 64) < (row // 64) + core
    contract = (((1,), (1,)), ((), ()))
    for j in range(1024 // rows):
        q = queries[j * rows : (j + 1) * rows]
        n = j * rows
        pieces = []
        for keys, values, allowed in (
            (own_keys, own_values, own_allowed),
            (oth_keys, oth_values, oth_allowed),
        ):
            if n:
                s = lax.dot_general(q, keys[:n], contract, preferred_element_type=F32) * scale
                pieces.append((s, values[:n]))
            s = lax.dot_general(q, keys[n : n + rows], contract, preferred_element_type=F32) * scale
            pieces.append((jnp.where(allowed, s, NEG_FILL), values[n : n + rows]))
        top = functools.reduce(jnp.maximum, [jnp.max(s, axis=1, keepdims=True) for s, _ in pieces])
        acc = jnp.zeros((rows, HEAD_DIM), F32)
        total = jnp.zeros((rows, 1), F32)
        for s, values in pieces:
            e = jnp.exp2(s - top)
            total = total + jnp.sum(e, axis=1, keepdims=True)
            acc = acc + jnp.dot(e.astype(BF), values, preferred_element_type=F32)
        out_ref[j * (rows // 64) : (j + 1) * (rows // 64)] = (
            (acc / total).astype(BF).reshape(rows // 64, 64, HEAD_DIM)
        )


def attention(core, own, oth):
    return pl.pallas_call(
        attention_kernel,
        out_shape=jax.ShapeDtypeStruct((16, 64, 128), BF),
        in_specs=[SMEM, VMEM, VMEM],
        out_specs=VMEM,
        compiler_params=params(32),
        cost_estimate=pl.CostEstimate(
            flops=2 * 2 * 1024 * 1280 * 128, bytes_accessed=2 << 20, transcendentals=1024 * 1280
        ),
    )(core, own, oth)


def middle_kernel(
    core_ref, ctx_ref, own_ref, oth_ref, res_ref, router_ref, ids_ref,
    hidden_ref, out_ref, gate_ref, target_ref, halves,
):
    core = core_ref[0]
    for h in range(HEADS):
        for c in range(2):
            halves[h // 4, c * 64 : (c + 1) * 64, (h % 4) * 128 : (h % 4 + 1) * 128] = ctx_ref[h * 2 + c]
    attn = jnp.dot(halves[core], own_ref[...], preferred_element_type=F32)
    attn = attn + jnp.dot(halves[1 - core], oth_ref[...], preferred_element_type=F32)
    hidden = (res_ref[0].astype(F32) + attn).astype(BF)
    hidden_ref[...] = hidden
    wide = hidden.astype(F32)
    mean_square = jnp.mean(wide * wide, axis=1, keepdims=True)
    normed = (wide * lax.rsqrt(mean_square + 1e-06)).astype(BF)
    affinity = jax.nn.sigmoid(jnp.dot(normed, router_ref[...], preferred_element_type=F32))
    tokens, experts = affinity.shape
    ids = ids_ref[0]
    lane = lax.broadcasted_iota(jnp.int32, (tokens, experts), 1)
    hot = [lane == ids[:, k : k + 1] for k in range(TOP)]
    picked = [jnp.sum(jnp.where(m, affinity, 0.0), axis=1, keepdims=True) for m in hot]
    whole = picked[0] + picked[1]
    below = (
        lax.broadcasted_iota(jnp.int32, (tokens, tokens), 1)
        < lax.broadcasted_iota(jnp.int32, (tokens, tokens), 0)
    ).astype(F32).astype(BF)
    counts = jnp.zeros((1, experts), F32)
    slot_lane = lax.broadcasted_iota(jnp.int32, (tokens, experts * SLOT), 1)
    dispatch = jnp.zeros((tokens, experts * SLOT), F32)
    for k in range(TOP):
        one = hot[k].astype(F32)
        rank = jnp.dot(below, one.astype(BF), preferred_element_type=F32) + counts
        slot = jnp.sum(rank * one, axis=1, keepdims=True).astype(jnp.int32)
        counts = counts + jnp.sum(one, axis=0, keepdims=True)
        target = ids[:, k : k + 1] * SLOT + slot
        dispatch = dispatch + (slot_lane == target).astype(F32)
        gate_ref[:, k : k + 1] = picked[k] / whole
        target_ref[:, k : k + 1] = target
    out_ref[...] = lax.dot_general(
        dispatch.astype(BF), normed, (((0,), (0,)), ((), ())), preferred_element_type=F32
    ).astype(BF)


def middle(core, ctx, own, oth, residual, router, ids):
    tokens, width = residual.shape[1:]
    experts = router.shape[1]
    return pl.pallas_call(
        middle_kernel,
        out_shape=(
            jax.ShapeDtypeStruct((tokens, width), BF),
            jax.ShapeDtypeStruct((experts * SLOT, width), BF),
            jax.ShapeDtypeStruct((tokens, TOP), F32),
            jax.ShapeDtypeStruct((tokens, TOP), jnp.int32),
        ),
        in_specs=[SMEM] + [VMEM] * 6,
        out_specs=(VMEM,) * 4,
        scratch_shapes=[pltpu.VMEM((2, 128, 512), BF)],
        compiler_params=params(32),
        cost_estimate=pl.CostEstimate(
            flops=2 * 128 * 1024 * 1600, bytes_accessed=4 << 20, transcendentals=4096
        ),
    )(core, ctx, own, oth, residual, router, ids)


def expert_kernel(core_ref, x_ref, own_ref, oth_ref, out_ref, up, down, sems):
    core = core_ref[0]
    copies = []
    for which in range(2):
        if which == 0:
            source, place = own_ref.at[pl.ds(core * 8, 8)], core
        else:
            source, place = oth_ref, 1 - core
        parts = (
            (source.at[:, 0:64, :], up.at[:, place, :, 0:1024]),
            (source.at[:, 64:96, 0:512], up.at[:, place, 0:32, 1024:1536]),
            (source.at[:, 64:96, 512:1024], up.at[:, place, 32:64, 1024:1536]),
            (source.at[:, 96:144, :], down.at[:, place]),
        )
        for j, (src, dst) in enumerate(parts):
            copies.append(pltpu.make_async_copy(src, dst, sems.at[which * 4 + j]))
    for copy in copies:
        copy.start()
    for j in (0, 1, 2, 4, 5, 6):
        copies[j].wait()
    ff = down.shape[0] * 2 * down.shape[2]
    up_all = up[...].reshape(1024, 2 * ff)
    inner = jnp.dot(x_ref[...], up_all, preferred_element_type=F32)
    activation = (jax.nn.silu(inner[:, :ff]) * inner[:, ff:]).astype(BF)
    for j in (3, 7):
        copies[j].wait()
    out_ref[...] = jnp.dot(
        activation, down[...].reshape(ff, 1024), preferred_element_type=F32
    ).astype(BF)


def experts(core, x, own, oth):
    rows = x.shape[0]
    return pl.pallas_call(
        expert_kernel,
        out_shape=jax.ShapeDtypeStruct((rows, 1024), BF),
        in_specs=[SMEM, VMEM, ANY, ANY],
        out_specs=VMEM,
        scratch_shapes=[
            pltpu.VMEM((8, 2, 64, 1536), BF),
            pltpu.VMEM((8, 2, 48, 1024), BF),
            pltpu.SemaphoreType.DMA((8,)),
        ],
        compiler_params=params(40),
        cost_estimate=pl.CostEstimate(
            flops=2 * rows * 1024 * 2304, bytes_accessed=7 << 20, transcendentals=rows * 768
        ),
    )(core, x, own, oth)


def combine_kernel(back_ref, hidden_ref, gate_ref, target_ref, out_ref):
    tokens = hidden_ref.shape[0]
    lane = lax.broadcasted_iota(jnp.int32, (tokens, back_ref.shape[0]), 1)
    total = hidden_ref[...].astype(F32)
    moe = None
    for k in range(TOP):
        pick = (lane == target_ref[:, k : k + 1]).astype(F32).astype(BF)
        pair = jnp.dot(pick, back_ref[...], preferred_element_type=F32) * gate_ref[:, k : k + 1]
        moe = pair if moe is None else moe + pair
    out_ref[0] = (total + moe).astype(BF)


def combine(back, hidden, gate, target):
    return pl.pallas_call(
        combine_kernel,
        out_shape=jax.ShapeDtypeStruct((1,) + hidden.shape, BF),
        in_specs=[VMEM] * 4,
        out_specs=VMEM,
        compiler_params=params(16),
    )(back, hidden, gate, target)


def on_device(
    residual, query_rows, key_rows, value_rows, out_proj, router, expert_ids,
    expert_gate_up, expert_down,
):
    core_index = lax.axis_index("core")
    core = core_index.astype(jnp.int32).reshape(1)
    packed = pack_weights(expert_gate_up, expert_down)
    weights = lax.all_gather(packed, ("zhi", "zlo"), axis=0, tiled=False)

    moved = lax.ppermute(out_proj, ALL, HALF_MOVE)
    shard = jnp.where(lax.axis_index("zhi") == core_index, out_proj, moved)
    proj_own = lax.all_to_all(
        jnp.broadcast_to(shard[None], (16,) + shard.shape), "xy", split_axis=0, concat_axis=0, tiled=True
    ).reshape(512, 1024)
    proj_oth = lax.ppermute(proj_own, ALL, CORE_SWAP)

    heads = pack_heads(query_rows, key_rows, value_rows)
    heads = lax.all_to_all(heads, ("zlo", "core"), split_axis=0, concat_axis=0, tiled=True)
    oth_heads = lax.ppermute(heads[:, 64:192, :], ALL, CORE_SWAP)
    context = attention(core, heads, oth_heads)
    context = lax.all_to_all(context, ("zlo", "core"), split_axis=0, concat_axis=0, tiled=True)

    hidden, outgoing, gate, target = middle(
        core, context, proj_own, proj_oth, residual, router, expert_ids
    )
    arrived = lax.all_to_all(
        outgoing.reshape(32, SLOT, 1024), ("core", "xy"), split_axis=0, concat_axis=0, tiled=True
    )
    to_send = lax.dynamic_slice_in_dim(weights, (1 - core_index) * 8, 8, axis=0)
    oth_weights = lax.ppermute(to_send, ALL, CORE_SWAP)
    produced = experts(core, arrived.reshape(32 * SLOT, 1024), weights, oth_weights)
    back = lax.all_to_all(
        produced.reshape(32, SLOT, 1024), ("core", "xy"), split_axis=0, concat_axis=0, tiled=True
    )
    return combine(back.reshape(32 * SLOT, 1024), hidden, gate, target)


def solution(mesh):
    fine = Mesh(mesh.devices.reshape(8, 2, 2, 16), ALL)
    rows = P(("zhi", "xy"), ("zlo", "core"), None)
    return jax.shard_map(
        on_device,
        mesh=fine,
        in_specs=(rows, rows, rows, rows, P(("zhi", "xy"), None), P(), rows, rows, rows),
        out_specs=rows,
        check_vma=False,
    )
```

time: 663 us -> 222 us (0.33)
  waiting for transfers between devices: 564 us -> 88.5 us
  blocking collectives: 0 us -> 45.9 us
  matrix products: 15.3 us -> 0 us
  Pallas kernels: 0 us -> 12.7 us
    all_gather x5 -> x1, waiting for transfers between devices: 481 us -> 45.1 us  [on_device(): weights = lax.all_gather(packed, ('zhi', 'zlo'), axis=0, tiled=False)]
    all_to_all x2 -> x3, waiting for transfers between devices: 80.5 us -> 25.1 us  [the longest x1 14.2 us: on_device(): lax.all_to_all(context, ('zlo', 'core'), split_axis=0, concat_axis=0, til...]
    all_to_all x0 -> x2, blocking collectives: none -> 45.9 us  [the longest x1 25.2 us: on_device(): lax.all_to_all(outgoing.reshape(32, SLOT, 1024), ('core', 'xy'), split_ax...]
    all_to_all x2 -> x3, starting transfers between devices: 49.4 us -> 26.1 us  [the longest x1 12.6 us: on_device(): lax.all_to_all(heads, ('zlo', 'core'), split_axis=0, concat_axis=0, tiled...]
    ppermute x0 -> x4, waiting for transfers between devices: none -> 18.3 us  [the longest x1 18.3 us: on_device(): moved = lax.ppermute(out_proj, ALL, HALF_MOVE)]
    ppermute x0 -> x4, starting transfers between devices: none -> 17.9 us  [the longest x1 8.22 us: on_device(): moved = lax.ppermute(out_proj, ALL, HALF_MOVE)]
    dot_general x7 -> x0, matrix products: 15.3 us -> none  [the longest x1 4.68 us: on_device(): jnp.dot(flat_feats, full_gate_up[0], preferred_element_type=jnp.float32)]
    pallas_call x0 -> x6, Pallas kernels: none -> 12.7 us  [the longest x1 3.52 us: attention(): pl.pallas_call(attention_kernel, out_shape=jax.ShapeDtypeStruct((16, 64,...]
  transfers between devices with their start and end apart: 7 -> 8, of which waited for: 7 -> 4; matrix products, arithmetic and copies ran while one was open for 4% -> 3% of each run, Pallas kernels for 0% -> 3%
where the time goes in v1:
time: 222 us; the launch traced here: 219 us
  waiting for transfers between devices  88.5 us (40%)
  blocking collectives  45.9 us (21%)
  starting transfers between devices  44 us (20%)
  local copies, waits for them, and re-layouts  14.8 us (7%)
  between operations  13.5 us (6%)
  Pallas kernels  12.7 us (6%)
    all_gather x1, waiting for transfers between devices, on_device(): weights = lax.all_gather(packed, ('zhi', 'zlo'), axis=0, tiled=False)  45.1 us
    all_to_all x1, blocking collectives, on_device(): lax.all_to_all(outgoing.reshape(32, SLOT, 1024), ('core', 'xy'), split_ax...  25.2 us
    all_to_all x1, blocking collectives, on_device(): lax.all_to_all(produced.reshape(32, SLOT, 1024), ('core', 'xy'), split_ax...  20.7 us
    ppermute x1, waiting for transfers between devices, on_device(): moved = lax.ppermute(out_proj, ALL, HALF_MOVE)  18.3 us
    all_to_all x1, waiting for transfers between devices, on_device(): lax.all_to_all(context, ('zlo', 'core'), split_axis=0, concat_axis=0, til...  14.2 us
    all_to_all x1, starting transfers between devices, on_device(): lax.all_to_all(heads, ('zlo', 'core'), split_axis=0, concat_axis=0, tiled...  12.6 us
    all_to_all x1, waiting for transfers between devices, on_device(): lax.all_to_all(heads, ('zlo', 'core'), split_axis=0, concat_axis=0, tiled...  11 us
    unnamed x30, local copies, waits for them, and re-layouts  9.38 us
  transfers between devices with their start and end apart: 8, of which 4 were waited for; matrix products, arithmetic and copies ran while one was open for 3% of the time, Pallas kernels for 3%

profile of v1, /device:TPU:6, one launch (start us, length us, event | category | flops | bytes accessed | tf_op | source)
XLA Modules:
  0.0 219.4 jit_solution(16814895237872757789)
XLA Ops:
  6.5 0.0 all-gather.3.cloned.1.call-start
  6.5 0.0 copy-start.9
  6.5 0.9 copy-done.9
  7.5 0.9 copy-done.10
  8.4 0.7 shard_map.94
  9.1 0.0 all-gather.3.cloned.1.call-update
  9.1 0.0 copy-start.6
  9.1 0.9 copy-done.6
  10.1 0.9 copy-done.7
  11.0 0.9 copy-done.8
  12.0 1.0 shard_map.91
  13.0 12.6 %all-to-all-start = ((bf16[16,192,128]{2,1,0:T(8,128)(2,1)}), bf16[16,192,128]{2,1,0:T(8,128)(2,1)S(1)}, u32[]{:S(2)}, u32[]{:S(2)}) async-start(bf16[16,192,128]{2,1,0:T(8,128)(2,1)} %shard_map.91), calls=%async_computation | async-start | bytes 1572864 | tf_op jit(solution)/shard_map/all_to_all | solution.py:290
  25.7 0.0 copy-done.11
  25.7 8.2 %collective-permute-start.1 = (bf16[32,1024]{1,0:T(8,128)(2,1)S(1)}, bf16[32,1024]{1,0:T(8,128)(2,1)S(1)}, u32[]{:S(2)}, u32[]{:S(2)}) collective-permute-start(bf16[32,1024]{1,0:T(8,128)(2,1)S(1)} %copy-done.11), channel_id=1, source_target_pairs={{0,16},{1,17},{2,18},{3,19},{4,20},{5,21},{6,22},{7,23},{8,24},{9,... | collective-permute-start | bytes 196616 | tf_op jit(solution)/shard_map/ppermute | solution.py:282
  33.9 18.3 %collective-permute-done.1 = bf16[32,1024]{1,0:T(8,128)(2,1)S(1)} collective-permute-done((bf16[32,1024]{1,0:T(8,128)(2,1)S(1)}, bf16[32,1024]{1,0:T(8,128)(2,1)S(1)}, u32[]{:S(2)}, u32[]{:S(2)}) %collective-permute-start.1) | collective-permute-done | bytes 65568 | tf_op jit(solution)/shard_map/ppermute | solution.py:282
  52.2 11.0 %all-to-all-done.own_ref = bf16[16,192,128]{2,1,0:T(8,128)(2,1)S(1)} async-done(((bf16[16,192,128]{2,1,0:T(8,128)(2,1)}), bf16[16,192,128]{2,1,0:T(8,128)(2,1)S(1)}, u32[]{:S(2)}, u32[]{:S(2)}) %all-to-all-start) | async-done | bytes 786464 | tf_op jit(solution)/shard_map/all_to_all | solution.py:290
  63.2 1.2 broadcast_in_dim.2
  64.4 7.4 %all-to-all-start.2 = ((bf16[16,32,1024]{2,1,0:T(8,128)(2,1)}), bf16[16,32,1024]{2,1,0:T(8,128)(2,1)S(1)}, u32[]{:S(2)}, u32[]{:S(2)}) async-start(bf16[16,32,1024]{2,1,0:T(8,128)(2,1)} %broadcast_in_dim.2), calls=%async_computation.2 | async-start | bytes 2097152 | tf_op jit(solution)/shard_map/all_to_all | solution.py:284
  71.9 0.8 slice.4
  72.7 5.2 %collective-permute-start = (bf16[16,128,128]{2,1,0:T(8,128)(2,1)}, bf16[16,128,128]{2,1,0:T(8,128)(2,1)}, u32[]{:S(2)}, u32[]{:S(2)}) collective-permute-start(bf16[16,128,128]{2,1,0:T(8,128)(2,1)} %slice.4), channel_id=1, source_target_pairs={{0,32},{1,33},{2,34},{3,35},{4,36},{5,37},{6,38},{7,39},{8,40},{9,... | collective-permute-start | bytes 1572872 | tf_op jit(solution)/shard_map/ppermute | solution.py:291
  77.9 45.1 %all-gather.3.cloned.1.call-done = bf16[2304,1024]{1,0:T(8,128)(2,1)} async-done(((bf16[144,1024]{1,0:T(8,128)(2,1)}), bf16[2304,1024]{1,0:T(8,128)(2,1)}) %all-gather.3.cloned.1.call-update) | async-done | bytes 4718608 | tf_op jit(solution)/shard_map/all_gather | solution.py:280
  123.0 0.0 copy-done.1
  123.0 3.3 %constant_dynamic-slice_fusion = bf16[8,144,1024]{2,1,0:T(8,128)(2,1)} fusion(bf16[16,144,1024]{2,1,0:T(8,128)(2,1)} %bitcast.7, s32[]{:T(128)S(6)} %select_n.13), kind=kLoop, calls=%fused_computation.1 | loop fusion | bytes 4718596 | tf_op jit(solution)/shard_map/dynamic_slice | solution.py:301
  126.4 2.0 collective-permute-start.3
  128.4 0.0 all-to-all-done.2
  128.4 2.4 %collective-permute-start.2 = (bf16[512,1024]{1,0:T(8,128)(2,1)S(1)}, bf16[512,1024]{1,0:T(8,128)(2,1)}, u32[]{:S(2)}, u32[]{:S(2)}) collective-permute-start(bf16[512,1024]{1,0:T(8,128)(2,1)S(1)} %bitcast.9), channel_id=1, source_target_pairs={{0,32},{1,33},{2,34},{3,35},{4,36},{5,37},{6,38},{7,39},{8,40},{9,... | collective-permute-start | bytes 3145736 | tf_op jit(solution)/shard_map/ppermute | solution.py:287
  130.8 0.0 collective-permute-done.oth_ref
  130.9 0.0 copy-start.2
  130.9 1.1 copy-done.2
  132.0 3.5 %shard_map.92 = bf16[16,64,128]{2,1,0:T(8,128)(2,1)S(1)} custom-call(s32[1]{0:T(128)} %bitcast.core_ref, bf16[16,192,128]{2,1,0:T(8,128)(2,1)S(1)} %copy-done.2, bf16[16,128,128]{2,1,0:T(8,128)(2,1)} %collective-permute-done.oth_ref), custom_call_target="tpu_custom_call" | custom-call | flops 671088640 | bytes 2097152 | tf_op jit(solution)/shard_map/pallas_call | solution.py:125
  135.5 0.0 copy-start.5
  135.5 0.7 copy-done.5
  136.2 6.0 %all-to-all-start.1 = ((bf16[16,64,128]{2,1,0:T(8,128)(2,1)}), bf16[16,64,128]{2,1,0:T(8,128)(2,1)}, u32[]{:S(2)}, u32[]{:S(2)}) async-start(bf16[16,64,128]{2,1,0:T(8,128)(2,1)} %copy-done.5), calls=%async_computation.1 | async-start | bytes 524288 | tf_op jit(solution)/shard_map/all_to_all | solution.py:293
  142.2 0.0 copy-done.13
  142.2 0.1 copy.11.ids_ref
  142.3 0.0 copy-done.12
  142.3 0.9 copy.10.router_ref
  143.2 0.0 collective-permute-done.2.oth_ref
  143.2 14.2 %all-to-all-done.1.ctx_ref = bf16[16,64,128]{2,1,0:T(8,128)(2,1)} async-done(((bf16[16,64,128]{2,1,0:T(8,128)(2,1)}), bf16[16,64,128]{2,1,0:T(8,128)(2,1)}, u32[]{:S(2)}, u32[]{:S(2)}) %all-to-all-start.1) | async-done | bytes 262176 | tf_op jit(solution)/shard_map/all_to_all | solution.py:293
  157.4 0.9 copy-done.3
  158.3 0.9 copy-done.4
  159.3 2.9 %shard_map.93 = (bf16[128,1024]{1,0:T(8,128)(2,1)S(1)}, bf16[512,1024]{1,0:T(8,128)(2,1)S(1)}, f32[128,2]{1,0:T(8,128)S(1)}, s32[128,2]{1,0:T(8,128)S(1)}) custom-call(s32[1]{0:T(128)} %bitcast.core_ref, bf16[16,64,128]{2,1,0:T(8,128)(2,1)} %all-to-all-done.1.ctx_ref, bf16[512,1024]{1,0:T(8,128)(2,1)S(1)} %bitcast.10, ...), custom_call_target="tpu_custom_call" | custom-call | flops 419430400 | bytes 4194304 | tf_op jit(solution)/shard_map/pallas_call | solution.py:183
  162.1 25.2 %all_to_all.25 = bf16[32,16,1024]{2,1,0:T(8,128)(2,1)S(1)} all-to-all(bf16[32,16,1024]{2,1,0:T(8,128)(2,1)S(1)} %bitcast.14), channel_id=1, replica_groups=mesh['zlo'=8,'core'=2,'zhi'=2,'xy'=16] {'core','xy'}, dimensions={0} | all-to-all | bytes 2097152 | tf_op jit(solution)/shard_map/all_to_all | solution.py:298
  187.3 0.0 collective-permute-done.3.oth_ref
  187.3 0.0 copy-done
  187.3 3.3 %shard_map.95 = bf16[512,1024]{1,0:T(8,128)(2,1)S(1)} custom-call(s32[1]{0:T(128)} %bitcast.core_ref, bf16[512,1024]{1,0:T(8,128)(2,1)S(1)} %bitcast.11, bf16[16,144,1024]{2,1,0:T(8,128)(2,1)S(1)} %bitcast.8, bf16[8,144,1024]{2,1,0:T(8,128)(2,1)S(1)} %collective-permute-done.3.oth_ref), custom_call_target="tpu_custom_call" | custom-call | flops 2415919104 | bytes 7340032 | tf_op jit(solution)/shard_map/pallas_call | solution.py:234
  190.6 20.7 %all_to_all.26 = bf16[32,16,1024]{2,1,0:T(8,128)(2,1)S(1)} all-to-all(bf16[32,16,1024]{2,1,0:T(8,128)(2,1)S(1)} %bitcast.12), channel_id=1, replica_groups=mesh['zlo'=8,'core'=2,'zhi'=2,'xy'=16] {'core','xy'}, dimensions={0} | all-to-all | bytes 2097152 | tf_op jit(solution)/shard_map/all_to_all | solution.py:304
  211.4 1.2 shard_map.96
  (11 shorter events, 0.0 us)
Async XLA Ops:
  6.5 116.5 %all-gather.3.cloned.1.call-start = ((), (), s32[]{:S(2)}) async-start(), calls=%async_computation.5 | async-start | bytes 5013504 | tf_op jit(solution)/shard_map/all_gather | solution.py:280
  6.5 0.9 copy-start.9
  7.5 0.9 copy-start.10
  8.4 17.3 %copy-start.11 = (bf16[32,1024]{1,0:T(8,128)(2,1)S(1)}, bf16[32,1024]{1,0:T(8,128)(2,1)}, u32[]{:S(2)}) copy-start(bf16[32,1024]{1,0:T(8,128)(2,1)} %param.13) | copy-start | bytes 196612
  9.1 1.0 copy-start.6
  10.1 0.9 copy-start.7
  11.0 0.9 copy-start.8
  13.0 50.1 %all-to-all-start = ((bf16[16,192,128]{2,1,0:T(8,128)(2,1)}), bf16[16,192,128]{2,1,0:T(8,128)(2,1)S(1)}, u32[]{:S(2)}, u32[]{:S(2)}) async-start(bf16[16,192,128]{2,1,0:T(8,128)(2,1)} %shard_map.91), calls=%async_computation | async-start | bytes 1572864 | tf_op jit(solution)/shard_map/all_to_all | solution.py:290
  25.7 26.5 %collective-permute-start.1 = (bf16[32,1024]{1,0:T(8,128)(2,1)S(1)}, bf16[32,1024]{1,0:T(8,128)(2,1)S(1)}, u32[]{:S(2)}, u32[]{:S(2)}) collective-permute-start(bf16[32,1024]{1,0:T(8,128)(2,1)S(1)} %copy-done.11), channel_id=1, source_target_pairs={{0,16},{1,17},{2,18},{3,19},{4,20},{5,21},{6,22},{7,23},{8,24},{9,... | collective-permute-start | bytes 196616 | tf_op jit(solution)/shard_map/ppermute | solution.py:282
  63.2 59.8 %copy-start.1 = (bf16[16,192,128]{2,1,0:T(8,128)(2,1)}, bf16[16,192,128]{2,1,0:T(8,128)(2,1)S(1)}, u32[]{:S(2)}) copy-start(bf16[16,192,128]{2,1,0:T(8,128)(2,1)S(1)} %all-to-all-done.own_ref) | copy-start | bytes 2359300
  64.4 64.0 %all-to-all-start.2 = ((bf16[16,32,1024]{2,1,0:T(8,128)(2,1)}), bf16[16,32,1024]{2,1,0:T(8,128)(2,1)S(1)}, u32[]{:S(2)}, u32[]{:S(2)}) async-start(bf16[16,32,1024]{2,1,0:T(8,128)(2,1)} %broadcast_in_dim.2), calls=%async_computation.2 | async-start | bytes 2097152 | tf_op jit(solution)/shard_map/all_to_all | solution.py:284
  72.7 58.1 %collective-permute-start = (bf16[16,128,128]{2,1,0:T(8,128)(2,1)}, bf16[16,128,128]{2,1,0:T(8,128)(2,1)}, u32[]{:S(2)}, u32[]{:S(2)}) collective-permute-start(bf16[16,128,128]{2,1,0:T(8,128)(2,1)} %slice.4), channel_id=1, source_target_pairs={{0,32},{1,33},{2,34},{3,35},{4,36},{5,37},{6,38},{7,39},{8,40},{9,... | collective-permute-start | bytes 1572872 | tf_op jit(solution)/shard_map/ppermute | solution.py:291
  123.0 19.3 %copy-start.12 = (bf16[1024,32]{0,1:T(8,128)(2,1)S(1)}, bf16[1024,32]{0,1:T(8,128)(2,1)}, u32[]{:S(2)}) copy-start(bf16[1024,32]{0,1:T(8,128)(2,1)} %param.14) | copy-start | bytes 196612
  126.4 15.9 %copy-start.13 = (s32[1,128,2]{1,2,0:T(2,128)S(1)}, s32[1,128,2]{1,2,0:T(2,128)}, u32[]{:S(2)}) copy-start(s32[1,128,2]{1,2,0:T(2,128)} %param.15) | copy-start | bytes 3076
  126.4 60.9 %collective-permute-start.3 = (bf16[8,144,1024]{2,1,0:T(8,128)(2,1)}, bf16[8,144,1024]{2,1,0:T(8,128)(2,1)S(1)}, u32[]{:S(2)}, u32[]{:S(2)}) collective-permute-start(bf16[8,144,1024]{2,1,0:T(8,128)(2,1)} %constant_dynamic-slice_fusion), channel_id=1, source_target_pairs={{0,32},{1,33},{2,34},{3,35},{4,36},{5,37},{6,38},{7,39},{8,40},{9,... | collective-permute-start | bytes 7077896 | tf_op jit(solution)/shard_map/ppermute | solution.py:302
  128.4 14.8 %collective-permute-start.2 = (bf16[512,1024]{1,0:T(8,128)(2,1)S(1)}, bf16[512,1024]{1,0:T(8,128)(2,1)}, u32[]{:S(2)}, u32[]{:S(2)}) collective-permute-start(bf16[512,1024]{1,0:T(8,128)(2,1)S(1)} %bitcast.9), channel_id=1, source_target_pairs={{0,32},{1,33},{2,34},{3,35},{4,36},{5,37},{6,38},{7,39},{8,40},{9,... | collective-permute-start | bytes 3145736 | tf_op jit(solution)/shard_map/ppermute | solution.py:287
  130.9 1.1 copy-start.2
  135.5 0.7 copy-start.5
  136.2 21.1 %all-to-all-start.1 = ((bf16[16,64,128]{2,1,0:T(8,128)(2,1)}), bf16[16,64,128]{2,1,0:T(8,128)(2,1)}, u32[]{:S(2)}, u32[]{:S(2)}) async-start(bf16[16,64,128]{2,1,0:T(8,128)(2,1)} %copy-done.5), calls=%async_computation.1 | async-start | bytes 524288 | tf_op jit(solution)/shard_map/all_to_all | solution.py:293
  157.4 1.0 copy-start.3
  158.3 0.9 copy-start.4
  159.3 28.1 %copy-start = (bf16[2304,1024]{1,0:T(8,128)(2,1)S(1)}, bf16[2304,1024]{1,0:T(8,128)(2,1)}, u32[]{:S(2)}) copy-start(bf16[2304,1024]{1,0:T(8,128)(2,1)} %all-gather.3.cloned.1.call-done) | copy-start | bytes 14155780
Sparse Core Ops, SparseCore 0:
  9.4 113.5 all-gather.2

commit v2 on v1

v2 whole, which is shorter than its diff:
```python
import functools

import jax
import jax.numpy as jnp
from jax import lax
from jax.experimental import pallas as pl
from jax.experimental.pallas import tpu as pltpu
from jax.sharding import Mesh, PartitionSpec as P

HEADS = 8
HEAD_DIM = 128
TOP = 2
SLOT = 16
PART = 2
NEG_FILL = -1e30
LOG2E = 1.4426950408889634
BF = jnp.bfloat16
F32 = jnp.float32
ALL = ("zlo", "core", "zhi", "xy")

VMEM = pl.BlockSpec(memory_space=pltpu.VMEM)
SMEM = pl.BlockSpec(memory_space=pltpu.SMEM)
ANY = pl.BlockSpec(memory_space=pl.ANY)
HBM = pl.BlockSpec(memory_space=pltpu.HBM)


def linear(zlo, core, zhi, xy):
    return ((zlo * 2 + core) * 2 + zhi) * 16 + xy


def all_pairs(move):
    pairs = []
    for zlo in range(8):
        for core in range(2):
            for zhi in range(2):
                for xy in range(16):
                    target = move(zlo, core, zhi, xy)
                    if target is not None:
                        pairs.append((linear(zlo, core, zhi, xy), linear(*target)))
    return pairs


CORE_SWAP = all_pairs(lambda zlo, core, zhi, xy: (zlo, 1 - core, zhi, xy))
HALF_MOVE = all_pairs(lambda zlo, core, zhi, xy: (zlo, core, 1 - zhi, xy) if zhi == core else None)


def plane_pairs(phase, step):
    def move(zlo, core, zhi, xy):
        x, y = divmod(xy, 4)
        if (phase + core) % 2 == 0:
            x = (x - step) % 4
        else:
            y = (y - step) % 4
        return zlo, core, zhi, x * 4 + y

    return all_pairs(move)


def params(mib):
    return pltpu.CompilerParams(vmem_limit_bytes=mib << 20)


def copy_kernel(plan, n_in, n_out, *refs):
    ins, outs, sems = refs[:n_in], refs[n_in : n_in + n_out], refs[-1]
    copies = [pltpu.make_async_copy(a, b, sems.at[n]) for n, (a, b) in enumerate(plan(ins, outs))]
    for copy in copies:
        copy.start()
    for copy in copies:
        copy.wait()


def copies_call(plan, count, outs, *operands, order=(), mib=56, bytes_accessed=2 << 20):
    many = isinstance(outs, tuple)
    return pl.pallas_call(
        functools.partial(copy_kernel, plan, len(operands) + len(order), len(outs) if many else 1),
        out_shape=outs,
        in_specs=[HBM] * len(operands) + [ANY] * len(order),
        out_specs=(HBM,) * len(outs) if many else HBM,
        scratch_shapes=[pltpu.SemaphoreType.DMA((count,))],
        compiler_params=params(mib),
        cost_estimate=pl.CostEstimate(flops=0, bytes_accessed=bytes_accessed, transcendentals=0),
    )(*operands, *order)


def heads_plan(ins, outs):
    return [
        (ref.at[:, :, h * 128 : (h + 1) * 128], outs[0].at[h, :, j * 64 : (j + 1) * 64, :])
        for h in range(HEADS)
        for j, ref in enumerate(ins[:3])
    ]


def weights_plan(ins, outs):
    up, down = ins
    return [
        (up.at[:, 0:1024], outs[0].at[0:64, :]),
        (up.at[0:32, 1024:1536], outs[0].at[64:96, 0:512]),
        (up.at[32:64, 1024:1536], outs[0].at[64:96, 512:1024]),
        (down, outs[0].at[96:144, :]),
    ]


def keys_plan(ins, outs):
    return [(ins[0].at[:, 64:192, :], outs[0])]


def attention_kernel(core_ref, own_ref, oth_ref, out_ref):
    core = core_ref[0]
    queries = own_ref[:, 0:64, :].reshape(1024, 128)
    own_keys = own_ref[:, 64:128, :].reshape(1024, 128)
    own_values = own_ref[:, 128:192, :].reshape(1024, 128)
    oth_keys = oth_ref[:, 0:64, :].reshape(1024, 128)
    oth_values = oth_ref[:, 64:128, :].reshape(1024, 128)
    scale = (HEAD_DIM ** (-0.5)) * LOG2E
    rows = 256
    row = lax.broadcasted_iota(jnp.int32, (rows, rows), 0)
    col = lax.broadcasted_iota(jnp.int32, (rows, rows), 1)
    own_allowed = col <= row
    oth_allowed = (col // 64) < (row // 64) + core
    contract = (((1,), (1,)), ((), ()))
    for j in range(1024 // rows):
        q = queries[j * rows : (j + 1) * rows]
        n = j * rows
        pieces = []
        for keys, values, allowed in (
            (own_keys, own_values, own_allowed),
            (oth_keys, oth_values, oth_allowed),
        ):
            if n:
                s = lax.dot_general(q, keys[:n], contract, preferred_element_type=F32) * scale
                pieces.append((s, values[:n]))
            s = lax.dot_general(q, keys[n : n + rows], contract, preferred_element_type=F32) * scale
            pieces.append((jnp.where(allowed, s, NEG_FILL), values[n : n + rows]))
        top = functools.reduce(jnp.maximum, [jnp.max(s, axis=1, keepdims=True) for s, _ in pieces])
        acc = jnp.zeros((rows, HEAD_DIM), F32)
        total = jnp.zeros((rows, 1), F32)
        for s, values in pieces:
            e = jnp.exp2(s - top)
            total = total + jnp.sum(e, axis=1, keepdims=True)
            acc = acc + jnp.dot(e.astype(BF), values, preferred_element_type=F32)
        out_ref[j * (rows // 64) : (j + 1) * (rows // 64)] = (
            (acc / total).astype(BF).reshape(rows // 64, 64, HEAD_DIM)
        )


def attention(core, own, oth):
    return pl.pallas_call(
        attention_kernel,
        out_shape=jax.ShapeDtypeStruct((16, 64, 128), BF),
        in_specs=[SMEM, VMEM, VMEM],
        out_specs=VMEM,
        compiler_params=params(20),
        cost_estimate=pl.CostEstimate(
            flops=2 * 2 * 1024 * 1280 * 128, bytes_accessed=2 << 20, transcendentals=1024 * 1280
        ),
    )(core, own, oth)


def middle_kernel(where_ref, ctx_ref, *refs):
    pieces, refs = refs[:8], refs[8:]
    res_ref, router_ref, ids_ref, hidden_ref, out_ref, gate_ref, target_ref = refs[:7]
    halves, proj, res, sems = refs[7:]
    own, place = where_ref[0], (where_ref[1], where_ref[2])
    copies = [pltpu.make_async_copy(res_ref.at[0], res, sems.at[32])]
    for n in range(8):
        core = own if n < 4 else 1 - own
        for first in range(4):
            along = (place[0] + jnp.where(core == 0, first, n % 4)) % 4
            across = (place[1] + jnp.where(core == 0, n % 4, first)) % 4
            copies.append(
                pltpu.make_async_copy(
                    pieces[n].at[first], proj.at[core, along * 4 + across], sems.at[n * 4 + first]
                )
            )
    for copy in copies:
        copy.start()
    for h in range(HEADS):
        for c in range(2):
            halves[c * 64 : (c + 1) * 64, h * 128 : (h + 1) * 128] = ctx_ref[h * 2 + c]
    for copy in copies:
        copy.wait()
    attn = jnp.dot(halves[...], proj[...].reshape(1024, 1024), preferred_element_type=F32)
    hidden = (res[...].astype(F32) + attn).astype(BF)
    hidden_ref[...] = hidden
    wide = hidden.astype(F32)
    mean_square = jnp.mean(wide * wide, axis=1, keepdims=True)
    normed = (wide * lax.rsqrt(mean_square + 1e-06)).astype(BF)
    affinity = jax.nn.sigmoid(
        lax.dot_general(
            router_ref[...], normed, (((1,), (1,)), ((), ())), preferred_element_type=F32
        )
    )
    experts, tokens = affinity.shape
    expert = lax.broadcasted_iota(jnp.int32, (experts, tokens), 0)
    hot = [expert == ids_ref[k : k + 1, :] for k in range(TOP)]
    picked = [jnp.sum(jnp.where(m, affinity, 0.0), axis=0, keepdims=True) for m in hot]
    whole = picked[0] + picked[1]
    before = (
        lax.broadcasted_iota(jnp.int32, (tokens, tokens), 0)
        < lax.broadcasted_iota(jnp.int32, (tokens, tokens), 1)
    ).astype(F32).astype(BF)
    counts = jnp.zeros((experts, 1), F32)
    slot_row = lax.broadcasted_iota(jnp.int32, (experts * SLOT, tokens), 0)
    dispatch = jnp.zeros((experts * SLOT, tokens), F32)
    for k in range(TOP):
        one = hot[k].astype(F32)
        rank = jnp.dot(one.astype(BF), before, preferred_element_type=F32) + counts
        slot = jnp.sum(rank * one, axis=0, keepdims=True).astype(jnp.int32)
        counts = counts + jnp.sum(one, axis=1, keepdims=True)
        target = ids_ref[k : k + 1, :] * SLOT + slot
        dispatch = dispatch + (slot_row == target).astype(F32)
        gate_ref[k : k + 1, :] = picked[k] / whole
        target_ref[k : k + 1, :] = target
    out_ref[...] = jnp.dot(dispatch.astype(BF), normed, preferred_element_type=F32).astype(BF)


def middle(where, ctx, own, oth, residual, router, ids):
    tokens, width = residual.shape[1:]
    experts = router.shape[1]
    return pl.pallas_call(
        middle_kernel,
        out_shape=(
            jax.ShapeDtypeStruct((tokens, width), BF),
            jax.ShapeDtypeStruct((experts * SLOT, width), BF),
            jax.ShapeDtypeStruct((TOP, tokens), F32),
            jax.ShapeDtypeStruct((TOP, tokens), jnp.int32),
        ),
        in_specs=[SMEM, VMEM] + [ANY] * 9 + [VMEM, VMEM],
        out_specs=(VMEM,) * 4,
        scratch_shapes=[
            pltpu.VMEM((128, 1024), BF),
            pltpu.VMEM((2, 16, 32, 1024), BF),
            pltpu.VMEM((128, 1024), BF),
            pltpu.SemaphoreType.DMA((33,)),
        ],
        compiler_params=params(16),
        cost_estimate=pl.CostEstimate(
            flops=2 * 128 * 1024 * 1600, bytes_accessed=4 << 20, transcendentals=4096
        ),
    )(where, ctx, *own, *oth, residual, router.T, ids[0].T)


def pick_kernel(core_ref, weights_ref, after_ref, *refs):
    sems = refs[-1]
    core = core_ref[0]
    copies = [
        pltpu.make_async_copy(
            weights_ref.at[pl.ds((1 - core) * 8 + n * PART, PART)], ref, sems.at[n]
        )
        for n, ref in enumerate(refs[:-2])
    ]
    copies.append(
        pltpu.make_async_copy(weights_ref.at[pl.ds(core * 8, 8)], refs[-2], sems.at[8 // PART])
    )
    for copy in copies:
        copy.start()
    for copy in copies:
        copy.wait()


def pick(core, weights, after):
    parts = 8 // PART
    one = weights.shape[1:]
    return pl.pallas_call(
        pick_kernel,
        out_shape=(jax.ShapeDtypeStruct((PART,) + one, BF),) * parts
        + (jax.ShapeDtypeStruct((8,) + one, BF),),
        in_specs=[SMEM, HBM, ANY],
        out_specs=(ANY,) * (parts + 1),
        scratch_shapes=[pltpu.SemaphoreType.DMA((parts + 1,))],
        compiler_params=params(52),
        cost_estimate=pl.CostEstimate(flops=0, bytes_accessed=8 << 20, transcendentals=0),
    )(core, weights, after)


def expert_kernel(core_ref, x_ref, own_ref, *refs):
    oth_refs, (out_ref, up, down, sems) = refs[: 8 // PART], refs[8 // PART :]
    core = core_ref[0]
    pieces = [(own_ref, slice(0, 8), core)]
    pieces += [
        (ref, slice(n * PART, (n + 1) * PART), 1 - core) for n, ref in enumerate(oth_refs)
    ]
    early, late = [], []
    for source, z, place in pieces:
        early += [
            (source.at[:, 0:64, :], up.at[z, place, :, 0:1024]),
            (source.at[:, 64:96, 0:512], up.at[z, place, 0:32, 1024:1536]),
            (source.at[:, 64:96, 512:1024], up.at[z, place, 32:64, 1024:1536]),
        ]
        late.append((source.at[:, 96:144, :], down.at[z, place]))
    copies = [
        pltpu.make_async_copy(src, dst, sems.at[n]) for n, (src, dst) in enumerate(early + late)
    ]
    for copy in copies:
        copy.start()
    for copy in copies[: len(early)]:
        copy.wait()
    ff = down.shape[0] * 2 * down.shape[2]
    up_all = up[...].reshape(1024, 2 * ff)
    inner = jnp.dot(x_ref[...], up_all, preferred_element_type=F32)
    activation = (jax.nn.silu(inner[:, :ff]) * inner[:, ff:]).astype(BF)
    for copy in copies[len(early) :]:
        copy.wait()
    out_ref[...] = jnp.dot(
        activation, down[...].reshape(ff, 1024), preferred_element_type=F32
    ).astype(BF)


def experts(core, x, own, oth):
    rows = x.shape[0]
    return pl.pallas_call(
        expert_kernel,
        out_shape=jax.ShapeDtypeStruct((rows, 1024), BF),
        in_specs=[SMEM, VMEM, ANY] + [ANY] * len(oth),
        out_specs=VMEM,
        scratch_shapes=[
            pltpu.VMEM((8, 2, 64, 1536), BF),
            pltpu.VMEM((8, 2, 48, 1024), BF),
            pltpu.SemaphoreType.DMA((4 * (1 + len(oth)),)),
        ],
        compiler_params=params(24),
        cost_estimate=pl.CostEstimate(
            flops=2 * rows * 1024 * 2304, bytes_accessed=7 << 20, transcendentals=rows * 768
        ),
    )(core, x, own, *oth)


def combine_kernel(back_ref, hidden_ref, gate_ref, target_ref, out_ref):
    tokens = hidden_ref.shape[0]
    slot_row = lax.broadcasted_iota(jnp.int32, (back_ref.shape[0], tokens), 0)
    pad = jnp.zeros((8 - TOP, tokens), F32)
    gates = jnp.transpose(jnp.concatenate([gate_ref[...], pad], axis=0))
    total = hidden_ref[...].astype(F32)
    moe = None
    for k in range(TOP):
        choose = (slot_row == target_ref[k : k + 1, :]).astype(F32).astype(BF)
        pair = lax.dot_general(
            choose, back_ref[...], (((0,), (0,)), ((), ())), preferred_element_type=F32
        ) * gates[:, k : k + 1]
        moe = pair if moe is None else moe + pair
    out_ref[0] = (total + moe).astype(BF)


def combine(back, hidden, gate, target):
    return pl.pallas_call(
        combine_kernel,
        out_shape=jax.ShapeDtypeStruct((1,) + hidden.shape, BF),
        in_specs=[VMEM] * 4,
        out_specs=VMEM,
        compiler_params=params(16),
    )(back, hidden, gate, target)


def on_device(
    residual, query_rows, key_rows, value_rows, out_proj, router, expert_ids,
    expert_gate_up, expert_down,
):
    core_index = lax.axis_index("core")
    core = core_index.astype(jnp.int32).reshape(1)
    packed = copies_call(
        weights_plan, 4, jax.ShapeDtypeStruct((144, 1024), BF), expert_gate_up[0], expert_down[0]
    )
    weights = lax.all_gather(packed, ("zhi", "zlo"), axis=0, tiled=False)

    moved = lax.ppermute(out_proj, ALL, HALF_MOVE)
    shard = jnp.where(lax.axis_index("zhi") == core_index, out_proj, moved)
    line = jnp.stack([shard] + [lax.ppermute(shard, ALL, plane_pairs(0, d)) for d in (1, 2, 3)])
    proj_own = [line] + [lax.ppermute(line, ALL, plane_pairs(1, d)) for d in (1, 2, 3)]

    halves = (2, 64, 1024)
    heads = copies_call(
        heads_plan, 24, jax.ShapeDtypeStruct((8, 2, 192, 128), BF),
        query_rows.reshape(halves), key_rows.reshape(halves), value_rows.reshape(halves),
        order=(moved,),
    )
    heads = lax.all_to_all(
        heads.reshape(16, 192, 128), ("zlo", "core"), split_axis=0, concat_axis=0, tiled=True
    )
    keys = copies_call(
        keys_plan, 1, jax.ShapeDtypeStruct((16, 128, 128), BF), heads, order=tuple(proj_own),
        mib=2,
    )
    oth_keys = lax.ppermute(keys, ALL, CORE_SWAP)
    proj_oth = [lax.ppermute(p, ALL, CORE_SWAP) for p in proj_own]
    context = attention(core, heads, oth_keys)
    context = lax.all_to_all(context, ("zlo", "core"), split_axis=0, concat_axis=0, tiled=True)

    xy = lax.axis_index("xy").astype(jnp.int32).reshape(1)
    where = jnp.concatenate([core, xy // 4, xy % 4])
    hidden, outgoing, gate, target = middle(
        where, context, proj_own, proj_oth, residual, router, expert_ids
    )
    arrived = lax.all_to_all(
        outgoing.reshape(32, SLOT, 1024), ("core", "xy"), split_axis=0, concat_axis=0, tiled=True
    )
    *to_send, own_weights = pick(core, weights, target)
    oth_weights = [lax.ppermute(w, ALL, CORE_SWAP) for w in to_send]
    produced = experts(core, arrived.reshape(32 * SLOT, 1024), own_weights, oth_weights)
    back = lax.all_to_all(
        produced.reshape(32, SLOT, 1024), ("core", "xy"), split_axis=0, concat_axis=0, tiled=True
    )
    return combine(back.reshape(32 * SLOT, 1024), hidden, gate, target)


def solution(mesh):
    fine = Mesh(mesh.devices.reshape(8, 2, 2, 16), ALL)
    rows = P(("zhi", "xy"), ("zlo", "core"), None)
    return jax.shard_map(
        on_device,
        mesh=fine,
        in_specs=(rows, rows, rows, rows, P(("zhi", "xy"), None), P(), rows, rows, rows),
        out_specs=rows,
        check_vma=False,
    )
```

time: 222 us -> 336 us (1.51)
  Pallas kernels: 12.7 us -> 177 us
  waiting for transfers between devices: 88.5 us -> 28.9 us
  starting transfers between devices: 44 us -> 87 us
  blocking collectives: 45.9 us -> 22.7 us
  local copies, waits for them, and re-layouts: 14.8 us -> 2.31 us
    pallas_call x2 -> x4, Pallas kernels: 1.8 us -> 161 us  [the longest x1 126 us: pick(): pl.pallas_call(pick_kernel, out_shape=(jax.ShapeDtypeStruct((PART,) + one...]
    all_gather x1, waiting for transfers between devices: 45.1 us -> 0.02 us  [on_device(): weights = lax.all_gather(packed, ('zhi', 'zlo'), axis=0, tiled=False)]
    ppermute x3 -> x15, starting transfers between devices: 9.69 us -> 40.3 us  [the longest x3 11.6 us: on_device(): lax.ppermute(line, ALL, plane_pairs(1, d))]
    all_to_all x1 -> x0, blocking collectives: 25.2 us -> none  [on_device(): lax.all_to_all(outgoing.reshape(32, SLOT, 1024), ('core', 'xy'), split_ax...]
    ppermute x1, waiting for transfers between devices: 18.3 us -> 2.2 us  [on_device(): moved = lax.ppermute(out_proj, ALL, HALF_MOVE)]
    ppermute x3 -> x15, waiting for transfers between devices: 0.01 us -> 15.2 us  [the longest x3 5.43 us: on_device(): lax.ppermute(shard, ALL, plane_pairs(0, d))]
    all_to_all x1, waiting for transfers between devices: 14.2 us -> 5 us  [on_device(): lax.all_to_all(context, ('zlo', 'core'), split_axis=0, concat_axis=0, til...]
    ppermute x1, starting transfers between devices: 8.22 us -> 15.9 us  [on_device(): moved = lax.ppermute(out_proj, ALL, HALF_MOVE)]
  transfers between devices with their start and end apart: 8 -> 20, of which waited for: 4 -> 10; matrix products, arithmetic and copies ran while one was open for 3% -> 0% of each run, Pallas kernels for 3% -> 48%
where the time goes in v2:
time: 336 us; the launch traced here: 332 us
  Pallas kernels  177 us (53%)
  starting transfers between devices  87 us (26%)
  waiting for transfers between devices  28.9 us (9%)
  blocking collectives  22.7 us (7%)
  between operations  13.7 us (4%)
    pallas_call x1, Pallas kernels, pick(): pl.pallas_call(pick_kernel, out_shape=(jax.ShapeDtypeStruct((PART,) + one...  126 us
    pallas_call x3, Pallas kernels, copies_call(): pl.pallas_call(functools.partial(copy_kernel, plan, len(operands) + len(o...  35.3 us
    all_to_all x1, blocking collectives, on_device(): lax.all_to_all(produced.reshape(32, SLOT, 1024), ('core', 'xy'), split_ax...  22.7 us
    ppermute x1, starting transfers between devices, on_device(): moved = lax.ppermute(out_proj, ALL, HALF_MOVE)  15.9 us
    all_to_all x1, starting transfers between devices, on_device(): lax.all_to_all(context, ('zlo', 'core'), split_axis=0, concat_axis=0, til...  13.2 us
    ppermute x3, starting transfers between devices, on_device(): lax.ppermute(line, ALL, plane_pairs(1, d))  11.6 us
    all_to_all x1, starting transfers between devices, on_device(): lax.all_to_all(outgoing.reshape(32, SLOT, 1024), ('core', 'xy'), split_ax...  9.58 us
    ppermute x4, starting transfers between devices, on_device(): oth_weights = [lax.ppermute(w, ALL, CORE_SWAP) for w in to_send]  8.65 us
  transfers between devices with their start and end apart: 20, of which 10 were waited for; matrix products, arithmetic and copies ran while one was open for 0% of the time, Pallas kernels for 48%

profile of v2, /device:TPU:6, one launch (start us, length us, event | category | flops | bytes accessed | tf_op | source)
XLA Modules:
  0.0 332.5 jit_solution(49686333488619263)
XLA Ops:
  6.5 10.1 %shard_map.95 = bf16[144,1024]{1,0:T(8,128)(2,1)} custom-call(bf16[64,1536]{1,0:T(8,128)(2,1)} %bitcast.32, bf16[48,1024]{1,0:T(8,128)(2,1)} %bitcast.33), custom_call_target="tpu_custom_call" | custom-call | bytes 2097152 | tf_op jit(solution)/shard_map/pallas_call | solution.py:74
  16.6 0.0 all-gather.3.cloned.1.call-update
  16.6 0.0 copy-start
  16.6 0.0 copy-start.1
  16.7 0.0 copy-start.2
  16.7 15.9 %collective-permute-start = (bf16[32,1024]{1,0:T(8,128)(2,1)}, bf16[32,1024]{1,0:T(8,128)(2,1)S(1)}, u32[]{:S(2)}, u32[]{:S(2)}) collective-permute-start(bf16[32,1024]{1,0:T(8,128)(2,1)} %param.13), channel_id=1, source_target_pairs={{0,16},{1,17},{2,18},{3,19},{4,20},{5,21},{6,22},{7,23},{8,24},{9,... | collective-permute-start | bytes 196616 | tf_op jit(solution)/shard_map/ppermute | solution.py:365
  32.5 2.2 collective-permute-done.refs_3_
  34.7 0.6 copy-done.4
  35.4 25.1 %shard_map.91 = bf16[8,2,192,128]{3,2,1,0:T(8,128)(2,1)} custom-call(bf16[2,64,1024]{2,1,0:T(8,128)(2,1)} %bitcast.28, bf16[2,64,1024]{2,1,0:T(8,128)(2,1)} %bitcast.29, bf16[2,64,1024]{2,1,0:T(8,128)(2,1)} %bitcast.30, bf16[32,1024]{1,0:T(8,128)(2,1)} %copy-done.4), custom_call_target="tpu_custom_call" | custom-call | bytes 2097152 | tf_op jit(solution)/shard_map/pallas_call | solution.py:74
  60.5 8.1 %all-to-all-start = ((bf16[16,192,128]{2,1,0:T(8,128)(2,1)}), bf16[16,192,128]{2,1,0:T(8,128)(2,1)S(1)}, u32[]{:S(2)}, u32[]{:S(2)}) async-start(bf16[16,192,128]{2,1,0:T(8,128)(2,1)} %bitcast.27), calls=%async_computation | async-start | bytes 1572864 | tf_op jit(solution)/shard_map/all_to_all | solution.py:376
  68.6 0.9 broadcast_select_fusion
  69.5 2.4 collective-permute-start.3
  71.9 4.3 %collective-permute-start.2 = (bf16[32,1024]{1,0:T(8,128)(2,1)S(1)}, bf16[32,1024]{1,0:T(8,128)(2,1)S(1)}, u32[]{:S(2)}, u32[]{:S(2)}) collective-permute-start(bf16[32,1024]{1,0:T(8,128)(2,1)S(1)} %broadcast_select_fusion), channel_id=1, source_target_pairs={{0,8},{1,9},{2,10},{3,11},{4,12},{5,13},{6,14},{7,15},{8,0},{9,1},... | collective-permute-start | bytes 196616 | tf_op jit(solution)/shard_map/ppermute | solution.py:367
  76.2 1.9 collective-permute-start.1
  78.1 0.0 collective-permute-done.3
  78.1 1.4 collective-permute-done.2
  79.5 4.0 %collective-permute-done.1 = bf16[32,1024]{1,0:T(8,128)(2,1)S(1)} collective-permute-done((bf16[32,1024]{1,0:T(8,128)(2,1)S(1)}, bf16[32,1024]{1,0:T(8,128)(2,1)S(1)}, u32[]{:S(2)}, u32[]{:S(2)}) %collective-permute-start.1) | collective-permute-done | bytes 65568 | tf_op jit(solution)/shard_map/ppermute | solution.py:367
  83.6 3.5 %collective-permute-start.6 = (bf16[4,32,1024]{2,1,0:T(8,128)(2,1)S(1)}, bf16[4,32,1024]{2,1,0:T(8,128)(2,1)S(1)}, u32[]{:S(2)}, u32[]{:S(2)}) collective-permute-start(bf16[4,32,1024]{2,1,0:T(8,128)(2,1)S(1)} %pad_maximum_fusion.refs_1_.refs_0_), channel_id=1, source_target_pairs={{0,1},{1,2},{2,3},{3,0},{4,5},{5,6},{6,7},{7,4},{8,9},{9,10},{10,1... | collective-permute-start | bytes 786440 | tf_op jit(solution)/shard_map/ppermute | solution.py:368
  87.1 4.8 %collective-permute-start.5 = (bf16[4,32,1024]{2,1,0:T(8,128)(2,1)S(1)}, bf16[4,32,1024]{2,1,0:T(8,128)(2,1)S(1)}, u32[]{:S(2)}, u32[]{:S(2)}) collective-permute-start(bf16[4,32,1024]{2,1,0:T(8,128)(2,1)S(1)} %pad_maximum_fusion.refs_1_.refs_0_), channel_id=1, source_target_pairs={{0,2},{1,3},{2,0},{3,1},{4,6},{5,7},{6,4},{7,5},{8,10},{9,11},{10,... | collective-permute-start | bytes 786440 | tf_op jit(solution)/shard_map/ppermute | solution.py:368
  91.9 3.3 collective-permute-start.4
  95.2 0.0 collective-permute-done.6.refs_4_.refs_3_
  95.2 1.9 collective-permute-done.5.refs_3_.refs_2_
  97.1 3.0 collective-permute-done.4.refs_2_.refs_1_
  100.2 6.5 %all-to-all-done.refs_0_.own_ref = bf16[16,192,128]{2,1,0:T(8,128)(2,1)S(1)} async-done(((bf16[16,192,128]{2,1,0:T(8,128)(2,1)}), bf16[16,192,128]{2,1,0:T(8,128)(2,1)S(1)}, u32[]{:S(2)}, u32[]{:S(2)}) %all-to-all-start) | async-done | bytes 786464 | tf_op jit(solution)/shard_map/all_to_all | solution.py:376
  106.7 2.8 collective-permute-start.7
  109.5 1.5 collective-permute-done.7.oth_ref
  111.1 3.2 shard_map.93
  114.2 13.2 %all-to-all-start.1 = ((bf16[16,64,128]{2,1,0:T(8,128)(2,1)}), bf16[16,64,128]{2,1,0:T(8,128)(2,1)S(1)}, u32[]{:S(2)}, u32[]{:S(2)}) async-start(bf16[16,64,128]{2,1,0:T(8,128)(2,1)} %shard_map.93), calls=%async_computation.1 | async-start | bytes 524288 | tf_op jit(solution)/shard_map/all_to_all | solution.py:386
  127.5 2.3 collective-permute-start.8
  129.8 2.0 collective-permute-start.11
  131.8 2.3 collective-permute-start.10
  134.1 2.0 collective-permute-start.9
  136.2 0.1 pad_add_fusion.where_ref
  136.3 1.3 collective-permute-done.9.refs_5_
  137.5 5.0 %all-to-all-done.1.ctx_ref = bf16[16,64,128]{2,1,0:T(8,128)(2,1)S(1)} async-done(((bf16[16,64,128]{2,1,0:T(8,128)(2,1)}), bf16[16,64,128]{2,1,0:T(8,128)(2,1)S(1)}, u32[]{:S(2)}, u32[]{:S(2)}) %all-to-all-start.1) | async-done | bytes 262176 | tf_op jit(solution)/shard_map/all_to_all | solution.py:386
  142.6 6.6 %shard_map.94 = (bf16[128,1024]{1,0:T(8,128)(2,1)S(1)}, bf16[512,1024]{1,0:T(8,128)(2,1)}, f32[2,128]{1,0:T(2,128)S(1)}, s32[2,128]{1,0:T(2,128)S(1)}) custom-call(s32[3]{0:T(128)S(1)} %pad_add_fusion.where_ref, bf16[16,64,128]{2,1,0:T(8,128)(2,1)S(1)} %all-to-all-done.1.ctx_ref, bf16[4,32,1024]{2,1,0:T(8,128)(2,1)S(1)} %pad_maximum_fusion.refs_1_.refs_0_, ...), custom_call_target="tpu_custom_call" | custom-call | flops 419430400 | bytes 4194304 | tf_op jit(solution)/shard_map/pallas_call | solution.py:220
  149.2 9.6 %all-to-all-start.2 = ((bf16[32,16,1024]{2,1,0:T(8,128)(2,1)}), bf16[32,16,1024]{2,1,0:T(8,128)(2,1)S(1)}, u32[]{:S(2)}, u32[]{:S(2)}) async-start(bf16[32,16,1024]{2,1,0:T(8,128)(2,1)} %bitcast.13), calls=%async_computation.2 | async-start | bytes 2097152 | tf_op jit(solution)/shard_map/all_to_all | solution.py:393
  158.8 0.0 all-gather.3.cloned.1.call-done
  158.8 126.2 %shard_map.96 = (bf16[2,144,1024]{2,1,0:T(8,128)(2,1)}, bf16[2,144,1024]{2,1,0:T(8,128)(2,1)}, bf16[2,144,1024]{2,1,0:T(8,128)(2,1)S(1)}, bf16[2,144,1024]{2,1,0:T(8,128)(2,1)}, bf16[8,144,1024]{2,1,0:T(8,128)(2,1)}) custom-call(s32[1]{0:T(128)} %bitcast.core_ref, bf16[16,144,1024]{2,1,0:T(8,128)(2,1)} %bitcast.26, ...), custom_call_target="tpu_custom_call" | custom-call | bytes 8388608 | tf_op jit(solution)/shard_map/pallas_call | solution.py:264
  285.0 2.1 collective-permute-start.12
  287.1 2.2 collective-permute-start.13
  289.4 2.1 collective-permute-start.14
  291.5 2.2 collective-permute-start.15
  293.7 2.0 collective-permute-done.15.refs_3_
  295.7 1.7 copy-done.3
  297.4 4.3 %shard_map.97 = bf16[512,1024]{1,0:T(8,128)(2,1)S(1)} custom-call(s32[1]{0:T(128)} %bitcast.core_ref, bf16[512,1024]{1,0:T(8,128)(2,1)S(1)} %bitcast.22, bf16[8,144,1024]{2,1,0:T(8,128)(2,1)S(1)} %copy-done.3, bf16[2,144,1024]{2,1,0:T(8,128)(2,1)S(1)} %collective-permute-done.12.refs_0_, bf16[2,144,1024]{2,1,0:T(8,128)(2,1)S(1)} %collective-permute-done.13.refs_1_, ...), custom_call_target="tpu_custom_call" | custom-call | flops 2415919104 | bytes 7340032 | tf_op jit(solution)/shard_map/pallas_call | solution.py:311
  301.7 22.7 %all_to_all.20 = bf16[32,16,1024]{2,1,0:T(8,128)(2,1)S(1)} all-to-all(bf16[32,16,1024]{2,1,0:T(8,128)(2,1)S(1)} %bitcast.23), channel_id=1, replica_groups=mesh['zlo'=8,'core'=2,'zhi'=2,'xy'=16] {'core','xy'}, dimensions={0} | all-to-all | bytes 2097152 | tf_op jit(solution)/shard_map/all_to_all | solution.py:399
  324.4 1.2 shard_map.98
  (15 shorter events, 0.1 us)
Async XLA Ops:
  6.5 152.2 %all-gather.3.cloned.1.call-start = ((), (), s32[]{:S(2)}) async-start(), calls=%async_computation.4 | async-start | bytes 5013504 | tf_op jit(solution)/shard_map/all_gather | solution.py:363
  16.6 125.9 %copy-start = (bf16[1,128,1024]{2,1,0:T(8,128)(2,1)S(1)}, bf16[1,128,1024]{2,1,0:T(8,128)(2,1)}, u32[]{:S(2)}) copy-start(bf16[1,128,1024]{2,1,0:T(8,128)(2,1)} %refs_8_.1) | copy-start | bytes 786436
  16.6 125.9 %copy-start.1 = (bf16[1024,32]{0,1:T(8,128)(2,1)S(1)}, bf16[1024,32]{0,1:T(8,128)(2,1)}, u32[]{:S(2)}) copy-start(bf16[1024,32]{0,1:T(8,128)(2,1)} %param.14) | copy-start | bytes 196612
  16.7 125.9 %copy-start.2 = (s32[1,128,2]{1,2,0:T(2,128)S(1)}, s32[1,128,2]{1,2,0:T(2,128)}, u32[]{:S(2)}) copy-start(s32[1,128,2]{1,2,0:T(2,128)} %param.15) | copy-start | bytes 3076
  16.7 18.1 %collective-permute-start = (bf16[32,1024]{1,0:T(8,128)(2,1)}, bf16[32,1024]{1,0:T(8,128)(2,1)S(1)}, u32[]{:S(2)}, u32[]{:S(2)}) collective-permute-start(bf16[32,1024]{1,0:T(8,128)(2,1)} %param.13), channel_id=1, source_target_pairs={{0,16},{1,17},{2,18},{3,19},{4,20},{5,21},{6,22},{7,23},{8,24},{9,... | collective-permute-start | bytes 196616 | tf_op jit(solution)/shard_map/ppermute | solution.py:365
  34.7 0.6 copy-start.4
  60.5 46.2 %all-to-all-start = ((bf16[16,192,128]{2,1,0:T(8,128)(2,1)}), bf16[16,192,128]{2,1,0:T(8,128)(2,1)S(1)}, u32[]{:S(2)}, u32[]{:S(2)}) async-start(bf16[16,192,128]{2,1,0:T(8,128)(2,1)} %bitcast.27), calls=%async_computation | async-start | bytes 1572864 | tf_op jit(solution)/shard_map/all_to_all | solution.py:376
  69.5 8.7 %collective-permute-start.3 = (bf16[32,1024]{1,0:T(8,128)(2,1)S(1)}, bf16[32,1024]{1,0:T(8,128)(2,1)S(1)}, u32[]{:S(2)}, u32[]{:S(2)}) collective-permute-start(bf16[32,1024]{1,0:T(8,128)(2,1)S(1)} %broadcast_select_fusion), channel_id=1, source_target_pairs={{0,4},{1,5},{2,6},{3,7},{4,8},{5,9},{6,10},{7,11},{8,12},{9,13},{1... | collective-permute-start | bytes 196616 | tf_op jit(solution)/shard_map/ppermute | solution.py:367
  71.9 7.7 %collective-permute-start.2 = (bf16[32,1024]{1,0:T(8,128)(2,1)S(1)}, bf16[32,1024]{1,0:T(8,128)(2,1)S(1)}, u32[]{:S(2)}, u32[]{:S(2)}) collective-permute-start(bf16[32,1024]{1,0:T(8,128)(2,1)S(1)} %broadcast_select_fusion), channel_id=1, source_target_pairs={{0,8},{1,9},{2,10},{3,11},{4,12},{5,13},{6,14},{7,15},{8,0},{9,1},... | collective-permute-start | bytes 196616 | tf_op jit(solution)/shard_map/ppermute | solution.py:367
  76.2 7.4 %collective-permute-start.1 = (bf16[32,1024]{1,0:T(8,128)(2,1)S(1)}, bf16[32,1024]{1,0:T(8,128)(2,1)S(1)}, u32[]{:S(2)}, u32[]{:S(2)}) collective-permute-start(bf16[32,1024]{1,0:T(8,128)(2,1)S(1)} %broadcast_select_fusion), channel_id=1, source_target_pairs={{0,12},{1,13},{2,14},{3,15},{4,0},{5,1},{6,2},{7,3},{8,4},{9,5},{1... | collective-permute-start | bytes 196616 | tf_op jit(solution)/shard_map/ppermute | solution.py:367
  83.6 11.6 %collective-permute-start.6 = (bf16[4,32,1024]{2,1,0:T(8,128)(2,1)S(1)}, bf16[4,32,1024]{2,1,0:T(8,128)(2,1)S(1)}, u32[]{:S(2)}, u32[]{:S(2)}) collective-permute-start(bf16[4,32,1024]{2,1,0:T(8,128)(2,1)S(1)} %pad_maximum_fusion.refs_1_.refs_0_), channel_id=1, source_target_pairs={{0,1},{1,2},{2,3},{3,0},{4,5},{5,6},{6,7},{7,4},{8,9},{9,10},{10,1... | collective-permute-start | bytes 786440 | tf_op jit(solution)/shard_map/ppermute | solution.py:368
  87.1 10.0 %collective-permute-start.5 = (bf16[4,32,1024]{2,1,0:T(8,128)(2,1)S(1)}, bf16[4,32,1024]{2,1,0:T(8,128)(2,1)S(1)}, u32[]{:S(2)}, u32[]{:S(2)}) collective-permute-start(bf16[4,32,1024]{2,1,0:T(8,128)(2,1)S(1)} %pad_maximum_fusion.refs_1_.refs_0_), channel_id=1, source_target_pairs={{0,2},{1,3},{2,0},{3,1},{4,6},{5,7},{6,4},{7,5},{8,10},{9,11},{10,... | collective-permute-start | bytes 786440 | tf_op jit(solution)/shard_map/ppermute | solution.py:368
  91.9 8.3 %collective-permute-start.4 = (bf16[4,32,1024]{2,1,0:T(8,128)(2,1)S(1)}, bf16[4,32,1024]{2,1,0:T(8,128)(2,1)S(1)}, u32[]{:S(2)}, u32[]{:S(2)}) collective-permute-start(bf16[4,32,1024]{2,1,0:T(8,128)(2,1)S(1)} %pad_maximum_fusion.refs_1_.refs_0_), channel_id=1, source_target_pairs={{0,3},{1,0},{2,1},{3,2},{4,7},{5,4},{6,5},{7,6},{8,11},{9,8},{10,9... | collective-permute-start | bytes 786440 | tf_op jit(solution)/shard_map/ppermute | solution.py:368
  106.7 4.3 %collective-permute-start.7 = (bf16[16,128,128]{2,1,0:T(8,128)(2,1)S(1)}, bf16[16,128,128]{2,1,0:T(8,128)(2,1)S(1)}, u32[]{:S(2)}, u32[]{:S(2)}) collective-permute-start(bf16[16,128,128]{2,1,0:T(8,128)(2,1)S(1)} %shard_map.92), channel_id=1, source_target_pairs={{0,32},{1,33},{2,34},{3,35},{4,36},{5,37},{6,38},{7,39},{8,40},{9,... | collective-permute-start | bytes 1572872 | tf_op jit(solution)/shard_map/ppermute | solution.py:383
  114.2 28.3 %all-to-all-start.1 = ((bf16[16,64,128]{2,1,0:T(8,128)(2,1)}), bf16[16,64,128]{2,1,0:T(8,128)(2,1)S(1)}, u32[]{:S(2)}, u32[]{:S(2)}) async-start(bf16[16,64,128]{2,1,0:T(8,128)(2,1)} %shard_map.93), calls=%async_computation.1 | async-start | bytes 524288 | tf_op jit(solution)/shard_map/all_to_all | solution.py:386
  127.5 8.8 %collective-permute-start.8 = (bf16[4,32,1024]{2,1,0:T(8,128)(2,1)S(1)}, bf16[4,32,1024]{2,1,0:T(8,128)(2,1)S(1)}, u32[]{:S(2)}, u32[]{:S(2)}) collective-permute-start(bf16[4,32,1024]{2,1,0:T(8,128)(2,1)S(1)} %pad_maximum_fusion.refs_1_.refs_0_), channel_id=1, source_target_pairs={{0,32},{1,33},{2,34},{3,35},{4,36},{5,37},{6,38},{7,39},{8,40},{9,... | collective-permute-start | bytes 786440 | tf_op jit(solution)/shard_map/ppermute | solution.py:384
  129.8 6.5 %collective-permute-start.11 = (bf16[4,32,1024]{2,1,0:T(8,128)(2,1)S(1)}, bf16[4,32,1024]{2,1,0:T(8,128)(2,1)S(1)}, u32[]{:S(2)}, u32[]{:S(2)}) collective-permute-start(bf16[4,32,1024]{2,1,0:T(8,128)(2,1)S(1)} %collective-permute-done.6.refs_4_.refs_3_), channel_id=1, source_target_pairs={{0,32},{1,33},{2,34},{3,35},{4,36},{5,37},{6,38},{7,39},{8,40},{9,... | collective-permute-start | bytes 786440 | tf_op jit(solution)/shard_map/ppermute | solution.py:384
  131.8 4.4 %collective-permute-start.10 = (bf16[4,32,1024]{2,1,0:T(8,128)(2,1)S(1)}, bf16[4,32,1024]{2,1,0:T(8,128)(2,1)S(1)}, u32[]{:S(2)}, u32[]{:S(2)}) collective-permute-start(bf16[4,32,1024]{2,1,0:T(8,128)(2,1)S(1)} %collective-permute-done.5.refs_3_.refs_2_), channel_id=1, source_target_pairs={{0,32},{1,33},{2,34},{3,35},{4,36},{5,37},{6,38},{7,39},{8,40},{9,... | collective-permute-start | bytes 786440 | tf_op jit(solution)/shard_map/ppermute | solution.py:384
  134.1 3.4 %collective-permute-start.9 = (bf16[4,32,1024]{2,1,0:T(8,128)(2,1)S(1)}, bf16[4,32,1024]{2,1,0:T(8,128)(2,1)S(1)}, u32[]{:S(2)}, u32[]{:S(2)}) collective-permute-start(bf16[4,32,1024]{2,1,0:T(8,128)(2,1)S(1)} %collective-permute-done.4.refs_2_.refs_1_), channel_id=1, source_target_pairs={{0,32},{1,33},{2,34},{3,35},{4,36},{5,37},{6,38},{7,39},{8,40},{9,... | collective-permute-start | bytes 786440 | tf_op jit(solution)/shard_map/ppermute | solution.py:384
  149.2 144.5 %all-to-all-start.2 = ((bf16[32,16,1024]{2,1,0:T(8,128)(2,1)}), bf16[32,16,1024]{2,1,0:T(8,128)(2,1)S(1)}, u32[]{:S(2)}, u32[]{:S(2)}) async-start(bf16[32,16,1024]{2,1,0:T(8,128)(2,1)} %bitcast.13), calls=%async_computation.2 | async-start | bytes 2097152 | tf_op jit(solution)/shard_map/all_to_all | solution.py:393
  285.0 8.7 %collective-permute-start.12 = (bf16[2,144,1024]{2,1,0:T(8,128)(2,1)}, bf16[2,144,1024]{2,1,0:T(8,128)(2,1)S(1)}, u32[]{:S(2)}, u32[]{:S(2)}) collective-permute-start(bf16[2,144,1024]{2,1,0:T(8,128)(2,1)} %get-tuple-element.17), channel_id=1, source_target_pairs={{0,32},{1,33},{2,34},{3,35},{4,36},{5,37},{6,38},{7,39},{8,40},{9,... | collective-permute-start | bytes 1769480 | tf_op jit(solution)/shard_map/ppermute | solution.py:397
  287.1 6.6 %collective-permute-start.13 = (bf16[2,144,1024]{2,1,0:T(8,128)(2,1)}, bf16[2,144,1024]{2,1,0:T(8,128)(2,1)S(1)}, u32[]{:S(2)}, u32[]{:S(2)}) collective-permute-start(bf16[2,144,1024]{2,1,0:T(8,128)(2,1)} %get-tuple-element.18), channel_id=1, source_target_pairs={{0,32},{1,33},{2,34},{3,35},{4,36},{5,37},{6,38},{7,39},{8,40},{9,... | collective-permute-start | bytes 1769480 | tf_op jit(solution)/shard_map/ppermute | solution.py:397
  289.4 4.4 %collective-permute-start.14 = (bf16[2,144,1024]{2,1,0:T(8,128)(2,1)S(1)}, bf16[2,144,1024]{2,1,0:T(8,128)(2,1)}, u32[]{:S(2)}, u32[]{:S(2)}) collective-permute-start(bf16[2,144,1024]{2,1,0:T(8,128)(2,1)S(1)} %get-tuple-element.19), channel_id=1, source_target_pairs={{0,32},{1,33},{2,34},{3,35},{4,36},{5,37},{6,38},{7,39},{8,40},{9,... | collective-permute-start | bytes 1769480 | tf_op jit(solution)/shard_map/ppermute | solution.py:397
  291.5 4.2 %collective-permute-start.15 = (bf16[2,144,1024]{2,1,0:T(8,128)(2,1)}, bf16[2,144,1024]{2,1,0:T(8,128)(2,1)}, u32[]{:S(2)}, u32[]{:S(2)}) collective-permute-start(bf16[2,144,1024]{2,1,0:T(8,128)(2,1)} %get-tuple-element.20), channel_id=1, source_target_pairs={{0,32},{1,33},{2,34},{3,35},{4,36},{5,37},{6,38},{7,39},{8,40},{9,... | collective-permute-start | bytes 1769480 | tf_op jit(solution)/shard_map/ppermute | solution.py:397
  295.7 1.7 copy-start.3
Sparse Core Ops, SparseCore 0:
  16.8 116.3 all-gather.2

commit v3 on v2

--- a/solution.py
+++ b/solution.py
@@ -60,48 +60,75 @@
     return pltpu.CompilerParams(vmem_limit_bytes=mib << 20)
 
 
-def copy_kernel(plan, n_in, n_out, *refs):
-    ins, outs, sems = refs[:n_in], refs[n_in : n_in + n_out], refs[-1]
-    copies = [pltpu.make_async_copy(a, b, sems.at[n]) for n, (a, b) in enumerate(plan(ins, outs))]
+def pack_weights_kernel(up_ref, down_ref, out_ref, up, down, sems):
+    copies = [
+        pltpu.make_async_copy(up_ref.at[0], up, sems.at[0]),
+        pltpu.make_async_copy(down_ref.at[0], down, sems.at[1]),
+    ]
     for copy in copies:
         copy.start()
     for copy in copies:
         copy.wait()
-
-
-def copies_call(plan, count, outs, *operands, order=(), mib=56, bytes_accessed=2 << 20):
-    many = isinstance(outs, tuple)
-    return pl.pallas_call(
-        functools.partial(copy_kernel, plan, len(operands) + len(order), len(outs) if many else 1),
-        out_shape=outs,
-        in_specs=[HBM] * len(operands) + [ANY] * len(order),
-        out_specs=(HBM,) * len(outs) if many else HBM,
-        scratch_shapes=[pltpu.SemaphoreType.DMA((count,))],
-        compiler_params=params(mib),
-        cost_estimate=pl.CostEstimate(flops=0, bytes_accessed=bytes_accessed, transcendentals=0),
-    )(*operands, *order)
-
-
-def heads_plan(ins, outs):
-    return [
-        (ref.at[:, :, h * 128 : (h + 1) * 128], outs[0].at[h, :, j * 64 : (j + 1) * 64, :])
-        for h in range(HEADS)
-        for j, ref in enumerate(ins[:3])
+    out_ref[0:64, :] = up[:, 0:1024]
+    out_ref[64:96, 0:512] = up[0:32, 1024:1536]
+    out_ref[64:96, 512:1024] = up[32:64, 1024:1536]
+    out_ref[96:144, :] = down[...]
+
+
+def pack_weights(gate_up, down):
+    return pl.pallas_call(
+        pack_weights_kernel,
+        out_shape=jax.ShapeDtypeStruct((144, 1024), BF),
+        in_specs=[HBM, HBM],
+        out_specs=VMEM,
+        scratch_shapes=[
+            pltpu.VMEM(gate_up.shape[1:], BF),
+            pltpu.VMEM(down.shape[1:], BF),
+            pltpu.SemaphoreType.DMA((2,)),
+        ],
+        compiler_params=params(56),
+    )(gate_up, down)
+
+
+def pack_heads_kernel(q_ref, k_ref, v_ref, after_ref, out_ref, rows, sems):
+    copies = [
+        pltpu.make_async_copy(ref.at[0], rows.at[j], sems.at[j])
+        for j, ref in enumerate((q_ref, k_ref, v_ref))
     ]
-
-
-def weights_plan(ins, outs):
-    up, down = ins
-    return [
-        (up.at[:, 0:1024], outs[0].at[0:64, :]),
-        (up.at[0:32, 1024:1536], outs[0].at[64:96, 0:512]),
-        (up.at[32:64, 1024:1536], outs[0].at[64:96, 512:1024]),
-        (down, outs[0].at[96:144, :]),
-    ]
-
-
-def keys_plan(ins, outs):
-    return [(ins[0].at[:, 64:192, :], outs[0])]
+    for copy in copies:
+        copy.start()
+    for j, copy in enumerate(copies):
+        copy.wait()
+        for h in range(HEADS):
+            for c in range(2):
+                out_ref[h * 2 + c, j * 64 : (j + 1) * 64, :] = rows[
+                    j, c * 64 : (c + 1) * 64, h * 128 : (h + 1) * 128
+                ]
+
+
+def pack_heads(q, k, v, after):
+    return pl.pallas_call(
+        pack_heads_kernel,
+        out_shape=jax.ShapeDtypeStruct((16, 192, 128), BF),
+        in_specs=[HBM] * 3 + [ANY],
+        out_specs=VMEM,
+        scratch_shapes=[pltpu.VMEM((3,) + q.shape[1:], BF), pltpu.SemaphoreType.DMA((3,))],
+        compiler_params=params(56),
+    )(q, k, v, after)
+
+
+def keys_kernel(heads_ref, *refs):
+    refs[-1][...] = heads_ref[:, 64:192, :]
+
+
+def keys_of(heads, after):
+    return pl.pallas_call(
+        keys_kernel,
+        out_shape=jax.ShapeDtypeStruct((16, 128, 128), BF),
+        in_specs=[VMEM] + [ANY] * len(after),
+        out_specs=VMEM,
+        compiler_params=params(4),
+    )(heads, *after)
 
 
 def attention_kernel(core_ref, own_ref, oth_ref, out_ref):
@@ -159,28 +186,19 @@
 def middle_kernel(where_ref, ctx_ref, *refs):
     pieces, refs = refs[:8], refs[8:]
     res_ref, router_ref, ids_ref, hidden_ref, out_ref, gate_ref, target_ref = refs[:7]
-    halves, proj, res, sems = refs[7:]
+    halves, proj = refs[7:]
     own, place = where_ref[0], (where_ref[1], where_ref[2])
-    copies = [pltpu.make_async_copy(res_ref.at[0], res, sems.at[32])]
     for n in range(8):
         core = own if n < 4 else 1 - own
         for first in range(4):
             along = (place[0] + jnp.where(core == 0, first, n % 4)) % 4
             across = (place[1] + jnp.where(core == 0, n % 4, first)) % 4
-            copies.append(
-                pltpu.make_async_copy(
-                    pieces[n].at[first], proj.at[core, along * 4 + across], sems.at[n * 4 + first]
-                )
-            )
-    for copy in copies:
-        copy.start()
+            proj[core, along * 4 + across] = pieces[n][first]
     for h in range(HEADS):
         for c in range(2):
             halves[c * 64 : (c + 1) * 64, h * 128 : (h + 1) * 128] = ctx_ref[h * 2 + c]
-    for copy in copies:
-        copy.wait()
     attn = jnp.dot(halves[...], proj[...].reshape(1024, 1024), preferred_element_type=F32)
-    hidden = (res[...].astype(F32) + attn).astype(BF)
+    hidden = (res_ref[0].astype(F32) + attn).astype(BF)
     hidden_ref[...] = hidden
     wide = hidden.astype(F32)
     mean_square = jnp.mean(wide * wide, axis=1, keepdims=True)
@@ -225,13 +243,11 @@
             jax.ShapeDtypeStruct((TOP, tokens), F32),
             jax.ShapeDtypeStruct((TOP, tokens), jnp.int32),
         ),
-        in_specs=[SMEM, VMEM] + [ANY] * 9 + [VMEM, VMEM],
+        in_specs=[SMEM] + [VMEM] * 12,
         out_specs=(VMEM,) * 4,
         scratch_shapes=[
             pltpu.VMEM((128, 1024), BF),
             pltpu.VMEM((2, 16, 32, 1024), BF),
-            pltpu.VMEM((128, 1024), BF),
-            pltpu.SemaphoreType.DMA((33,)),
         ],
         compiler_params=params(16),
         cost_estimate=pl.CostEstimate(
@@ -266,7 +282,7 @@
         out_shape=(jax.ShapeDtypeStruct((PART,) + one, BF),) * parts
         + (jax.ShapeDtypeStruct((8,) + one, BF),),
         in_specs=[SMEM, HBM, ANY],
-        out_specs=(ANY,) * (parts + 1),
+        out_specs=(VMEM,) * (parts + 1),
         scratch_shapes=[pltpu.SemaphoreType.DMA((parts + 1,))],
         compiler_params=params(52),
         cost_estimate=pl.CostEstimate(flops=0, bytes_accessed=8 << 20, transcendentals=0),
@@ -274,33 +290,20 @@
 
 
 def expert_kernel(core_ref, x_ref, own_ref, *refs):
-    oth_refs, (out_ref, up, down, sems) = refs[: 8 // PART], refs[8 // PART :]
+    oth_refs, (out_ref, up, down) = refs[: 8 // PART], refs[8 // PART :]
     core = core_ref[0]
     pieces = [(own_ref, slice(0, 8), core)]
     pieces += [
         (ref, slice(n * PART, (n + 1) * PART), 1 - core) for n, ref in enumerate(oth_refs)
     ]
-    early, late = [], []
     for source, z, place in pieces:
-        early += [
-            (source.at[:, 0:64, :], up.at[z, place, :, 0:1024]),
-            (source.at[:, 64:96, 0:512], up.at[z, place, 0:32, 1024:1536]),
-            (source.at[:, 64:96, 512:1024], up.at[z, place, 32:64, 1024:1536]),
-        ]
-        late.append((source.at[:, 96:144, :], down.at[z, place]))
-    copies = [
-        pltpu.make_async_copy(src, dst, sems.at[n]) for n, (src, dst) in enumerate(early + late)
-    ]
-    for copy in copies:
-        copy.start()
-    for copy in copies[: len(early)]:
-        copy.wait()
+        up[z, place, :, 0:1024] = source[:, 0:64, :]
+        up[z, place, 0:32, 1024:1536] = source[:, 64:96, 0:512]
+        up[z, place, 32:64, 1024:1536] = source[:, 64:96, 512:1024]
+        down[z, place] = source[:, 96:144, :]
     ff = down.shape[0] * 2 * down.shape[2]
-    up_all = up[...].reshape(1024, 2 * ff)
-    inner = jnp.dot(x_ref[...], up_all, preferred_element_type=F32)
+    inner = jnp.dot(x_ref[...], up[...].reshape(1024, 2 * ff), preferred_element_type=F32)
     activation = (jax.nn.silu(inner[:, :ff]) * inner[:, ff:]).astype(BF)
-    for copy in copies[len(early) :]:
-        copy.wait()
     out_ref[...] = jnp.dot(
         activation, down[...].reshape(ff, 1024), preferred_element_type=F32
     ).astype(BF)
@@ -311,12 +314,11 @@
     return pl.pallas_call(
         expert_kernel,
         out_shape=jax.ShapeDtypeStruct((rows, 1024), BF),
-        in_specs=[SMEM, VMEM, ANY] + [ANY] * len(oth),
+        in_specs=[SMEM, VMEM, VMEM] + [VMEM] * len(oth),
         out_specs=VMEM,
         scratch_shapes=[
             pltpu.VMEM((8, 2, 64, 1536), BF),
             pltpu.VMEM((8, 2, 48, 1024), BF),
-            pltpu.SemaphoreType.DMA((4 * (1 + len(oth)),)),
         ],
         compiler_params=params(24),
         cost_estimate=pl.CostEstimate(
@@ -357,9 +359,7 @@
 ):
     core_index = lax.axis_index("core")
     core = core_index.astype(jnp.int32).reshape(1)
-    packed = copies_call(
-        weights_plan, 4, jax.ShapeDtypeStruct((144, 1024), BF), expert_gate_up[0], expert_down[0]
-    )
+    packed = pack_weights(expert_gate_up, expert_down)
     weights = lax.all_gather(packed, ("zhi", "zlo"), axis=0, tiled=False)
 
     moved = lax.ppermute(out_proj, ALL, HALF_MOVE)
@@ -367,19 +367,9 @@
     line = jnp.stack([shard] + [lax.ppermute(shard, ALL, plane_pairs(0, d)) for d in (1, 2, 3)])
     proj_own = [line] + [lax.ppermute(line, ALL, plane_pairs(1, d)) for d in (1, 2, 3)]
 
-    halves = (2, 64, 1024)
-    heads = copies_call(
-        heads_plan, 24, jax.ShapeDtypeStruct((8, 2, 192, 128), BF),
-        query_rows.reshape(halves), key_rows.reshape(halves), value_rows.reshape(halves),
-        order=(moved,),
-    )
-    heads = lax.all_to_all(
-        heads.reshape(16, 192, 128), ("zlo", "core"), split_axis=0, concat_axis=0, tiled=True
-    )
-    keys = copies_call(
-        keys_plan, 1, jax.ShapeDtypeStruct((16, 128, 128), BF), heads, order=tuple(proj_own),
-        mib=2,
-    )
+    heads = pack_heads(query_rows, key_rows, value_rows, moved)
+    heads = lax.all_to_all(heads, ("zlo", "core"), split_axis=0, concat_axis=0, tiled=True)
+    keys = keys_of(heads, proj_own)
     oth_keys = lax.ppermute(keys, ALL, CORE_SWAP)
     proj_oth = [lax.ppermute(p, ALL, CORE_SWAP) for p in proj_own]
     context = attention(core, heads, oth_keys)

time: 336 us -> 191 us (0.57)
  Pallas kernels: 177 us -> 19.7 us
  waiting for transfers between devices: 28.9 us -> 44.1 us
    pallas_call x1, Pallas kernels: 126 us -> 4.45 us  [pick(): pl.pallas_call(pick_kernel, out_shape=(jax.ShapeDtypeStruct((PART,) + one...]
    pallas_call x3, Pallas kernels: 35.3 us -> 3.87 us  [the longest x1 2.09 us: pack_heads(): pl.pallas_call(pack_heads_kernel, out_shape=jax.ShapeDtypeStruct((16, 192...]
    all_gather x1, waiting for transfers between devices: 0.02 us -> 10 us  [on_device(): weights = lax.all_gather(packed, ('zhi', 'zlo'), axis=0, tiled=False)]
    all_to_all x1, waiting for transfers between devices: 5 us -> 9.36 us  [on_device(): lax.all_to_all(context, ('zlo', 'core'), split_axis=0, concat_axis=0, til...]
    pallas_call x1, Pallas kernels: 6.6 us -> 2.87 us  [middle(): pl.pallas_call(middle_kernel, out_shape=(jax.ShapeDtypeStruct((tokens, wi...]
  transfers between devices with their start and end apart: 20 -> 20, of which waited for: 10 -> 11; matrix products, arithmetic and copies ran while one was open for 0% -> 1% of each run, Pallas kernels for 48% -> 7%
where the time goes in v3:
time: 191 us; the launch traced here: 188 us
  starting transfers between devices  83.9 us (44%)
  waiting for transfers between devices  44.1 us (23%)
  blocking collectives  23 us (12%)
  Pallas kernels  19.7 us (10%)
  between operations  13.7 us (7%)
  local copies, waits for them, and re-layouts  2.31 us (1%)
    all_to_all x1, blocking collectives, on_device(): lax.all_to_all(produced.reshape(32, SLOT, 1024), ('core', 'xy'), split_ax...  23 us
    ppermute x1, starting transfers between devices, on_device(): moved = lax.ppermute(out_proj, ALL, HALF_MOVE)  15.9 us
    all_to_all x1, starting transfers between devices, on_device(): lax.all_to_all(context, ('zlo', 'core'), split_axis=0, concat_axis=0, til...  12.6 us
    ppermute x3, starting transfers between devices, on_device(): lax.ppermute(line, ALL, plane_pairs(1, d))  11.5 us
    all_gather x1, waiting for transfers between devices, on_device(): weights = lax.all_gather(packed, ('zhi', 'zlo'), axis=0, tiled=False)  10 us
    all_to_all x1, waiting for transfers between devices, on_device(): lax.all_to_all(context, ('zlo', 'core'), split_axis=0, concat_axis=0, til...  9.36 us
    ppermute x4, starting transfers between devices, on_device(): oth_weights = [lax.ppermute(w, ALL, CORE_SWAP) for w in to_send]  8.65 us
    ppermute x4, starting transfers between devices, on_device(): proj_oth = [lax.ppermute(p, ALL, CORE_SWAP) for p in proj_own]  8.65 us
  transfers between devices with their start and end apart: 20, of which 11 were waited for; matrix products, arithmetic and copies ran while one was open for 1% of the time, Pallas kernels for 7%

profile of v3, /device:TPU:6, one launch (start us, length us, event | category | flops | bytes accessed | tf_op | source)
XLA Modules:
  0.0 187.7 jit_solution(13441468500093880810)
XLA Ops:
  6.5 1.8 shard_map.95
  8.3 0.0 all-gather.3.cloned.1.call-update
  8.3 0.0 copy-start
  8.3 0.0 copy-start.1
  8.3 0.0 copy-start.2
  8.4 15.9 %collective-permute-start = (bf16[32,1024]{1,0:T(8,128)(2,1)}, bf16[32,1024]{1,0:T(8,128)(2,1)S(1)}, u32[]{:S(2)}, u32[]{:S(2)}) collective-permute-start(bf16[32,1024]{1,0:T(8,128)(2,1)} %param.13), channel_id=1, source_target_pairs={{0,16},{1,17},{2,18},{3,19},{4,20},{5,21},{6,22},{7,23},{8,24},{9,... | collective-permute-start | bytes 196616 | tf_op jit(solution)/shard_map/ppermute | solution.py:365
  24.2 2.2 %collective-permute-done.after_ref = bf16[32,1024]{1,0:T(8,128)(2,1)S(1)} collective-permute-done((bf16[32,1024]{1,0:T(8,128)(2,1)}, bf16[32,1024]{1,0:T(8,128)(2,1)S(1)}, u32[]{:S(2)}, u32[]{:S(2)}) %collective-permute-start) | collective-permute-done | bytes 65568 | tf_op jit(solution)/shard_map/ppermute | solution.py:365
  26.4 0.6 copy-done.4
  27.1 2.1 %shard_map.91 = bf16[16,192,128]{2,1,0:T(8,128)(2,1)} custom-call(bf16[1,128,1024]{2,1,0:T(8,128)(2,1)} %q_ref.1, bf16[1,128,1024]{2,1,0:T(8,128)(2,1)} %k_ref.1, bf16[1,128,1024]{2,1,0:T(8,128)(2,1)} %v_ref.1, bf16[32,1024]{1,0:T(8,128)(2,1)} %copy-done.4), custom_call_target="tpu_custom_call" | custom-call | tf_op jit(solution)/shard_map/pallas_call | solution.py:110
  29.1 8.1 %all-to-all-start = ((bf16[16,192,128]{2,1,0:T(8,128)(2,1)}), bf16[16,192,128]{2,1,0:T(8,128)(2,1)S(1)}, u32[]{:S(2)}, u32[]{:S(2)}) async-start(bf16[16,192,128]{2,1,0:T(8,128)(2,1)} %shard_map.91), calls=%async_computation | async-start | bytes 1572864 | tf_op jit(solution)/shard_map/all_to_all | solution.py:371
  37.3 0.9 broadcast_select_fusion
  38.1 2.4 %collective-permute-start.3 = (bf16[32,1024]{1,0:T(8,128)(2,1)S(1)}, bf16[32,1024]{1,0:T(8,128)(2,1)S(1)}, u32[]{:S(2)}, u32[]{:S(2)}) collective-permute-start(bf16[32,1024]{1,0:T(8,128)(2,1)S(1)} %broadcast_select_fusion), channel_id=1, source_target_pairs={{0,4},{1,5},{2,6},{3,7},{4,8},{5,9},{6,10},{7,11},{8,12},{9,13},{1... | collective-permute-start | bytes 196616 | tf_op jit(solution)/shard_map/ppermute | solution.py:367
  40.5 4.3 %collective-permute-start.2 = (bf16[32,1024]{1,0:T(8,128)(2,1)S(1)}, bf16[32,1024]{1,0:T(8,128)(2,1)S(1)}, u32[]{:S(2)}, u32[]{:S(2)}) collective-permute-start(bf16[32,1024]{1,0:T(8,128)(2,1)S(1)} %broadcast_select_fusion), channel_id=1, source_target_pairs={{0,8},{1,9},{2,10},{3,11},{4,12},{5,13},{6,14},{7,15},{8,0},{9,1},... | collective-permute-start | bytes 196616 | tf_op jit(solution)/shard_map/ppermute | solution.py:367
  44.8 1.9 %collective-permute-start.1 = (bf16[32,1024]{1,0:T(8,128)(2,1)S(1)}, bf16[32,1024]{1,0:T(8,128)(2,1)S(1)}, u32[]{:S(2)}, u32[]{:S(2)}) collective-permute-start(bf16[32,1024]{1,0:T(8,128)(2,1)S(1)} %broadcast_select_fusion), channel_id=1, source_target_pairs={{0,12},{1,13},{2,14},{3,15},{4,0},{5,1},{6,2},{7,3},{8,4},{9,5},{1... | collective-permute-start | bytes 196616 | tf_op jit(solution)/shard_map/ppermute | solution.py:367
  46.8 0.0 collective-permute-done.3
  46.8 1.4 collective-permute-done.2
  48.2 4.0 %collective-permute-done.1 = bf16[32,1024]{1,0:T(8,128)(2,1)S(1)} collective-permute-done((bf16[32,1024]{1,0:T(8,128)(2,1)S(1)}, bf16[32,1024]{1,0:T(8,128)(2,1)S(1)}, u32[]{:S(2)}, u32[]{:S(2)}) %collective-permute-start.1) | collective-permute-done | bytes 65568 | tf_op jit(solution)/shard_map/ppermute | solution.py:367
  52.3 3.5 %collective-permute-start.6 = (bf16[4,32,1024]{2,1,0:T(8,128)(2,1)S(1)}, bf16[4,32,1024]{2,1,0:T(8,128)(2,1)S(1)}, u32[]{:S(2)}, u32[]{:S(2)}) collective-permute-start(bf16[4,32,1024]{2,1,0:T(8,128)(2,1)S(1)} %pad_maximum_fusion.refs_0_), channel_id=1, source_target_pairs={{0,1},{1,2},{2,3},{3,0},{4,5},{5,6},{6,7},{7,4},{8,9},{9,10},{10,1... | collective-permute-start | bytes 786440 | tf_op jit(solution)/shard_map/ppermute | solution.py:368
  55.7 4.8 %collective-permute-start.5 = (bf16[4,32,1024]{2,1,0:T(8,128)(2,1)S(1)}, bf16[4,32,1024]{2,1,0:T(8,128)(2,1)S(1)}, u32[]{:S(2)}, u32[]{:S(2)}) collective-permute-start(bf16[4,32,1024]{2,1,0:T(8,128)(2,1)S(1)} %pad_maximum_fusion.refs_0_), channel_id=1, source_target_pairs={{0,2},{1,3},{2,0},{3,1},{4,6},{5,7},{6,4},{7,5},{8,10},{9,11},{10,... | collective-permute-start | bytes 786440 | tf_op jit(solution)/shard_map/ppermute | solution.py:368
  60.6 3.3 %collective-permute-start.4 = (bf16[4,32,1024]{2,1,0:T(8,128)(2,1)S(1)}, bf16[4,32,1024]{2,1,0:T(8,128)(2,1)S(1)}, u32[]{:S(2)}, u32[]{:S(2)}) collective-permute-start(bf16[4,32,1024]{2,1,0:T(8,128)(2,1)S(1)} %pad_maximum_fusion.refs_0_), channel_id=1, source_target_pairs={{0,3},{1,0},{2,1},{3,2},{4,7},{5,4},{6,5},{7,6},{8,11},{9,8},{10,9... | collective-permute-start | bytes 786440 | tf_op jit(solution)/shard_map/ppermute | solution.py:368
  63.8 1.9 %collective-permute-done.5.refs_2_ = bf16[4,32,1024]{2,1,0:T(8,128)(2,1)S(1)} collective-permute-done((bf16[4,32,1024]{2,1,0:T(8,128)(2,1)S(1)}, bf16[4,32,1024]{2,1,0:T(8,128)(2,1)S(1)}, u32[]{:S(2)}, u32[]{:S(2)}) %collective-permute-start.5) | collective-permute-done | bytes 262176 | tf_op jit(solution)/shard_map/ppermute | solution.py:368
  65.8 3.0 %collective-permute-done.4.refs_1_ = bf16[4,32,1024]{2,1,0:T(8,128)(2,1)S(1)} collective-permute-done((bf16[4,32,1024]{2,1,0:T(8,128)(2,1)S(1)}, bf16[4,32,1024]{2,1,0:T(8,128)(2,1)S(1)}, u32[]{:S(2)}, u32[]{:S(2)}) %collective-permute-start.4) | collective-permute-done | bytes 262176 | tf_op jit(solution)/shard_map/ppermute | solution.py:368
  68.8 7.3 %all-to-all-done.heads_ref.own_ref = bf16[16,192,128]{2,1,0:T(8,128)(2,1)S(1)} async-done(((bf16[16,192,128]{2,1,0:T(8,128)(2,1)}), bf16[16,192,128]{2,1,0:T(8,128)(2,1)S(1)}, u32[]{:S(2)}, u32[]{:S(2)}) %all-to-all-start) | async-done | bytes 786464 | tf_op jit(solution)/shard_map/all_to_all | solution.py:371
  76.2 2.7 %collective-permute-start.7 = (bf16[16,128,128]{2,1,0:T(8,128)(2,1)S(1)}, bf16[16,128,128]{2,1,0:T(8,128)(2,1)S(1)}, u32[]{:S(2)}, u32[]{:S(2)}) collective-permute-start(bf16[16,128,128]{2,1,0:T(8,128)(2,1)S(1)} %shard_map.92), channel_id=1, source_target_pairs={{0,32},{1,33},{2,34},{3,35},{4,36},{5,37},{6,38},{7,39},{8,40},{9,... | collective-permute-start | bytes 1572872 | tf_op jit(solution)/shard_map/ppermute | solution.py:373
  78.9 1.5 collective-permute-done.7.oth_ref
  80.4 3.2 %shard_map.93 = bf16[16,64,128]{2,1,0:T(8,128)(2,1)} custom-call(s32[1]{0:T(128)} %bitcast.core_ref, bf16[16,192,128]{2,1,0:T(8,128)(2,1)S(1)} %all-to-all-done.heads_ref.own_ref, bf16[16,128,128]{2,1,0:T(8,128)(2,1)S(1)} %collective-permute-done.7.oth_ref), custom_call_target="tpu_custom_call" | custom-call | flops 671088640 | bytes 2097152 | tf_op jit(solution)/shard_map/pallas_call | solution.py:174
  83.6 12.6 %all-to-all-start.1 = ((bf16[16,64,128]{2,1,0:T(8,128)(2,1)}), bf16[16,64,128]{2,1,0:T(8,128)(2,1)S(1)}, u32[]{:S(2)}, u32[]{:S(2)}) async-start(bf16[16,64,128]{2,1,0:T(8,128)(2,1)} %shard_map.93), calls=%async_computation.1 | async-start | bytes 524288 | tf_op jit(solution)/shard_map/all_to_all | solution.py:376
  96.2 2.3 %collective-permute-start.8 = (bf16[4,32,1024]{2,1,0:T(8,128)(2,1)S(1)}, bf16[4,32,1024]{2,1,0:T(8,128)(2,1)S(1)}, u32[]{:S(2)}, u32[]{:S(2)}) collective-permute-start(bf16[4,32,1024]{2,1,0:T(8,128)(2,1)S(1)} %pad_maximum_fusion.refs_0_), channel_id=1, source_target_pairs={{0,32},{1,33},{2,34},{3,35},{4,36},{5,37},{6,38},{7,39},{8,40},{9,... | collective-permute-start | bytes 786440 | tf_op jit(solution)/shard_map/ppermute | solution.py:374
  98.5 2.0 %collective-permute-start.11 = (bf16[4,32,1024]{2,1,0:T(8,128)(2,1)S(1)}, bf16[4,32,1024]{2,1,0:T(8,128)(2,1)S(1)}, u32[]{:S(2)}, u32[]{:S(2)}) collective-permute-start(bf16[4,32,1024]{2,1,0:T(8,128)(2,1)S(1)} %collective-permute-done.6.refs_3_), channel_id=1, source_target_pairs={{0,32},{1,33},{2,34},{3,35},{4,36},{5,37},{6,38},{7,39},{8,40},{9,... | collective-permute-start | bytes 786440 | tf_op jit(solution)/shard_map/ppermute | solution.py:374
  100.6 2.3 %collective-permute-start.10 = (bf16[4,32,1024]{2,1,0:T(8,128)(2,1)S(1)}, bf16[4,32,1024]{2,1,0:T(8,128)(2,1)S(1)}, u32[]{:S(2)}, u32[]{:S(2)}) collective-permute-start(bf16[4,32,1024]{2,1,0:T(8,128)(2,1)S(1)} %collective-permute-done.5.refs_2_), channel_id=1, source_target_pairs={{0,32},{1,33},{2,34},{3,35},{4,36},{5,37},{6,38},{7,39},{8,40},{9,... | collective-permute-start | bytes 786440 | tf_op jit(solution)/shard_map/ppermute | solution.py:374
  102.9 2.0 %collective-permute-start.9 = (bf16[4,32,1024]{2,1,0:T(8,128)(2,1)S(1)}, bf16[4,32,1024]{2,1,0:T(8,128)(2,1)S(1)}, u32[]{:S(2)}, u32[]{:S(2)}) collective-permute-start(bf16[4,32,1024]{2,1,0:T(8,128)(2,1)S(1)} %collective-permute-done.4.refs_1_), channel_id=1, source_target_pairs={{0,32},{1,33},{2,34},{3,35},{4,36},{5,37},{6,38},{7,39},{8,40},{9,... | collective-permute-start | bytes 786440 | tf_op jit(solution)/shard_map/ppermute | solution.py:374
  104.9 0.1 pad_add_fusion.where_ref
  105.0 1.3 collective-permute-done.9.refs_5_
  106.3 9.4 %all-to-all-done.1.ctx_ref = bf16[16,64,128]{2,1,0:T(8,128)(2,1)S(1)} async-done(((bf16[16,64,128]{2,1,0:T(8,128)(2,1)}), bf16[16,64,128]{2,1,0:T(8,128)(2,1)S(1)}, u32[]{:S(2)}, u32[]{:S(2)}) %all-to-all-start.1) | async-done | bytes 262176 | tf_op jit(solution)/shard_map/all_to_all | solution.py:376
  115.7 2.9 %shard_map.94 = (bf16[128,1024]{1,0:T(8,128)(2,1)S(1)}, bf16[512,1024]{1,0:T(8,128)(2,1)}, f32[2,128]{1,0:T(2,128)S(1)}, s32[2,128]{1,0:T(2,128)S(1)}) custom-call(s32[3]{0:T(128)S(1)} %pad_add_fusion.where_ref, bf16[16,64,128]{2,1,0:T(8,128)(2,1)S(1)} %all-to-all-done.1.ctx_ref, bf16[4,32,1024]{2,1,0:T(8,128)(2,1)S(1)} %pad_maximum_fusion.refs_0_, ...), custom_call_target="tpu_custom_call" | custom-call | flops 419430400 | bytes 4194304 | tf_op jit(solution)/shard_map/pallas_call | solution.py:238
  118.5 7.2 %all-to-all-start.2 = ((bf16[32,16,1024]{2,1,0:T(8,128)(2,1)}), bf16[32,16,1024]{2,1,0:T(8,128)(2,1)S(1)}, u32[]{:S(2)}, u32[]{:S(2)}) async-start(bf16[32,16,1024]{2,1,0:T(8,128)(2,1)} %bitcast.9), calls=%async_computation.2 | async-start | bytes 2097152 | tf_op jit(solution)/shard_map/all_to_all | solution.py:383
  125.7 10.0 %all-gather.3.cloned.1.call-done = bf16[2304,1024]{1,0:T(8,128)(2,1)} async-done(((bf16[144,1024]{1,0:T(8,128)(2,1)}), bf16[2304,1024]{1,0:T(8,128)(2,1)}) %all-gather.3.cloned.1.call-update) | async-done | bytes 4718608 | tf_op jit(solution)/shard_map/all_gather | solution.py:363
  135.7 4.4 %shard_map.96 = (bf16[2,144,1024]{2,1,0:T(8,128)(2,1)}, bf16[2,144,1024]{2,1,0:T(8,128)(2,1)}, bf16[2,144,1024]{2,1,0:T(8,128)(2,1)S(1)}, bf16[2,144,1024]{2,1,0:T(8,128)(2,1)}, bf16[8,144,1024]{2,1,0:T(8,128)(2,1)}) custom-call(s32[1]{0:T(128)} %bitcast.core_ref, bf16[16,144,1024]{2,1,0:T(8,128)(2,1)} %bitcast.20, ...), custom_call_target="tpu_custom_call" | custom-call | bytes 8388608 | tf_op jit(solution)/shard_map/pallas_call | solution.py:280
  140.2 1.9 %collective-permute-start.12 = (bf16[2,144,1024]{2,1,0:T(8,128)(2,1)}, bf16[2,144,1024]{2,1,0:T(8,128)(2,1)S(1)}, u32[]{:S(2)}, u32[]{:S(2)}) collective-permute-start(bf16[2,144,1024]{2,1,0:T(8,128)(2,1)} %get-tuple-element.17), channel_id=1, source_target_pairs={{0,32},{1,33},{2,34},{3,35},{4,36},{5,37},{6,38},{7,39},{8,40},{9,... | collective-permute-start | bytes 1769480 | tf_op jit(solution)/shard_map/ppermute | solution.py:387
  142.1 2.4 %collective-permute-start.13 = (bf16[2,144,1024]{2,1,0:T(8,128)(2,1)}, bf16[2,144,1024]{2,1,0:T(8,128)(2,1)S(1)}, u32[]{:S(2)}, u32[]{:S(2)}) collective-permute-start(bf16[2,144,1024]{2,1,0:T(8,128)(2,1)} %get-tuple-element.18), channel_id=1, source_target_pairs={{0,32},{1,33},{2,34},{3,35},{4,36},{5,37},{6,38},{7,39},{8,40},{9,... | collective-permute-start | bytes 1769480 | tf_op jit(solution)/shard_map/ppermute | solution.py:387
  144.5 1.9 %collective-permute-start.14 = (bf16[2,144,1024]{2,1,0:T(8,128)(2,1)S(1)}, bf16[2,144,1024]{2,1,0:T(8,128)(2,1)}, u32[]{:S(2)}, u32[]{:S(2)}) collective-permute-start(bf16[2,144,1024]{2,1,0:T(8,128)(2,1)S(1)} %get-tuple-element.19), channel_id=1, source_target_pairs={{0,32},{1,33},{2,34},{3,35},{4,36},{5,37},{6,38},{7,39},{8,40},{9,... | collective-permute-start | bytes 1769480 | tf_op jit(solution)/shard_map/ppermute | solution.py:387
  146.5 2.4 %collective-permute-start.15 = (bf16[2,144,1024]{2,1,0:T(8,128)(2,1)}, bf16[2,144,1024]{2,1,0:T(8,128)(2,1)}, u32[]{:S(2)}, u32[]{:S(2)}) collective-permute-start(bf16[2,144,1024]{2,1,0:T(8,128)(2,1)} %get-tuple-element.20), channel_id=1, source_target_pairs={{0,32},{1,33},{2,34},{3,35},{4,36},{5,37},{6,38},{7,39},{8,40},{9,... | collective-permute-start | bytes 1769480 | tf_op jit(solution)/shard_map/ppermute | solution.py:387
  148.9 0.0 collective-permute-done.12.refs_0_
  148.9 1.9 %collective-permute-done.15.refs_3_ = bf16[2,144,1024]{2,1,0:T(8,128)(2,1)} collective-permute-done((bf16[2,144,1024]{2,1,0:T(8,128)(2,1)}, bf16[2,144,1024]{2,1,0:T(8,128)(2,1)}, u32[]{:S(2)}, u32[]{:S(2)}) %collective-permute-start.15) | collective-permute-done | bytes 589856 | tf_op jit(solution)/shard_map/ppermute | solution.py:387
  150.8 1.7 copy-done.3
  152.5 4.1 %shard_map.97 = bf16[512,1024]{1,0:T(8,128)(2,1)S(1)} custom-call(s32[1]{0:T(128)} %bitcast.core_ref, bf16[512,1024]{1,0:T(8,128)(2,1)S(1)} %bitcast.16, bf16[8,144,1024]{2,1,0:T(8,128)(2,1)S(1)} %copy-done.3, bf16[2,144,1024]{2,1,0:T(8,128)(2,1)S(1)} %collective-permute-done.12.refs_0_, bf16[2,144,1024]{2,1,0:T(8,128)(2,1)S(1)} %collective-permute-done.13.refs_1_, ...), custom_call_target="tpu_custom_call" | custom-call | flops 2415919104 | bytes 7340032 | tf_op jit(solution)/shard_map/pallas_call | solution.py:314
  156.6 23.0 %all_to_all.20 = bf16[32,16,1024]{2,1,0:T(8,128)(2,1)S(1)} all-to-all(bf16[32,16,1024]{2,1,0:T(8,128)(2,1)S(1)} %bitcast.17), channel_id=1, replica_groups=mesh['zlo'=8,'core'=2,'zhi'=2,'xy'=16] {'core','xy'}, dimensions={0} | all-to-all | bytes 2097152 | tf_op jit(solution)/shard_map/all_to_all | solution.py:389
  179.6 1.2 shard_map.98
  (15 shorter events, 0.1 us)
Async XLA Ops:
  6.5 129.2 %all-gather.3.cloned.1.call-start = ((), (), s32[]{:S(2)}) async-start(), calls=%async_computation.4 | async-start | bytes 5013504 | tf_op jit(solution)/shard_map/all_gather | solution.py:363
  8.3 107.3 %copy-start = (bf16[1,128,1024]{2,1,0:T(8,128)(2,1)S(1)}, bf16[1,128,1024]{2,1,0:T(8,128)(2,1)}, u32[]{:S(2)}) copy-start(bf16[1,128,1024]{2,1,0:T(8,128)(2,1)} %refs_8_.1) | copy-start | bytes 786436
  8.3 107.3 %copy-start.1 = (bf16[1024,32]{0,1:T(8,128)(2,1)S(1)}, bf16[1024,32]{0,1:T(8,128)(2,1)}, u32[]{:S(2)}) copy-start(bf16[1024,32]{0,1:T(8,128)(2,1)} %param.14) | copy-start | bytes 196612
  8.3 107.3 %copy-start.2 = (s32[1,128,2]{1,2,0:T(2,128)S(1)}, s32[1,128,2]{1,2,0:T(2,128)}, u32[]{:S(2)}) copy-start(s32[1,128,2]{1,2,0:T(2,128)} %param.15) | copy-start | bytes 3076
  8.4 18.1 %collective-permute-start = (bf16[32,1024]{1,0:T(8,128)(2,1)}, bf16[32,1024]{1,0:T(8,128)(2,1)S(1)}, u32[]{:S(2)}, u32[]{:S(2)}) collective-permute-start(bf16[32,1024]{1,0:T(8,128)(2,1)} %param.13), channel_id=1, source_target_pairs={{0,16},{1,17},{2,18},{3,19},{4,20},{5,21},{6,22},{7,23},{8,24},{9,... | collective-permute-start | bytes 196616 | tf_op jit(solution)/shard_map/ppermute | solution.py:365
  26.4 0.6 copy-start.4
  29.1 47.0 %all-to-all-start = ((bf16[16,192,128]{2,1,0:T(8,128)(2,1)}), bf16[16,192,128]{2,1,0:T(8,128)(2,1)S(1)}, u32[]{:S(2)}, u32[]{:S(2)}) async-start(bf16[16,192,128]{2,1,0:T(8,128)(2,1)} %shard_map.91), calls=%async_computation | async-start | bytes 1572864 | tf_op jit(solution)/shard_map/all_to_all | solution.py:371
  38.1 8.7 %collective-permute-start.3 = (bf16[32,1024]{1,0:T(8,128)(2,1)S(1)}, bf16[32,1024]{1,0:T(8,128)(2,1)S(1)}, u32[]{:S(2)}, u32[]{:S(2)}) collective-permute-start(bf16[32,1024]{1,0:T(8,128)(2,1)S(1)} %broadcast_select_fusion), channel_id=1, source_target_pairs={{0,4},{1,5},{2,6},{3,7},{4,8},{5,9},{6,10},{7,11},{8,12},{9,13},{1... | collective-permute-start | bytes 196616 | tf_op jit(solution)/shard_map/ppermute | solution.py:367
  40.5 7.7 %collective-permute-start.2 = (bf16[32,1024]{1,0:T(8,128)(2,1)S(1)}, bf16[32,1024]{1,0:T(8,128)(2,1)S(1)}, u32[]{:S(2)}, u32[]{:S(2)}) collective-permute-start(bf16[32,1024]{1,0:T(8,128)(2,1)S(1)} %broadcast_select_fusion), channel_id=1, source_target_pairs={{0,8},{1,9},{2,10},{3,11},{4,12},{5,13},{6,14},{7,15},{8,0},{9,1},... | collective-permute-start | bytes 196616 | tf_op jit(solution)/shard_map/ppermute | solution.py:367
  44.8 7.4 %collective-permute-start.1 = (bf16[32,1024]{1,0:T(8,128)(2,1)S(1)}, bf16[32,1024]{1,0:T(8,128)(2,1)S(1)}, u32[]{:S(2)}, u32[]{:S(2)}) collective-permute-start(bf16[32,1024]{1,0:T(8,128)(2,1)S(1)} %broadcast_select_fusion), channel_id=1, source_target_pairs={{0,12},{1,13},{2,14},{3,15},{4,0},{5,1},{6,2},{7,3},{8,4},{9,5},{1... | collective-permute-start | bytes 196616 | tf_op jit(solution)/shard_map/ppermute | solution.py:367
  52.3 11.6 %collective-permute-start.6 = (bf16[4,32,1024]{2,1,0:T(8,128)(2,1)S(1)}, bf16[4,32,1024]{2,1,0:T(8,128)(2,1)S(1)}, u32[]{:S(2)}, u32[]{:S(2)}) collective-permute-start(bf16[4,32,1024]{2,1,0:T(8,128)(2,1)S(1)} %pad_maximum_fusion.refs_0_), channel_id=1, source_target_pairs={{0,1},{1,2},{2,3},{3,0},{4,5},{5,6},{6,7},{7,4},{8,9},{9,10},{10,1... | collective-permute-start | bytes 786440 | tf_op jit(solution)/shard_map/ppermute | solution.py:368
  55.7 10.0 %collective-permute-start.5 = (bf16[4,32,1024]{2,1,0:T(8,128)(2,1)S(1)}, bf16[4,32,1024]{2,1,0:T(8,128)(2,1)S(1)}, u32[]{:S(2)}, u32[]{:S(2)}) collective-permute-start(bf16[4,32,1024]{2,1,0:T(8,128)(2,1)S(1)} %pad_maximum_fusion.refs_0_), channel_id=1, source_target_pairs={{0,2},{1,3},{2,0},{3,1},{4,6},{5,7},{6,4},{7,5},{8,10},{9,11},{10,... | collective-permute-start | bytes 786440 | tf_op jit(solution)/shard_map/ppermute | solution.py:368
  60.6 8.3 %collective-permute-start.4 = (bf16[4,32,1024]{2,1,0:T(8,128)(2,1)S(1)}, bf16[4,32,1024]{2,1,0:T(8,128)(2,1)S(1)}, u32[]{:S(2)}, u32[]{:S(2)}) collective-permute-start(bf16[4,32,1024]{2,1,0:T(8,128)(2,1)S(1)} %pad_maximum_fusion.refs_0_), channel_id=1, source_target_pairs={{0,3},{1,0},{2,1},{3,2},{4,7},{5,4},{6,5},{7,6},{8,11},{9,8},{10,9... | collective-permute-start | bytes 786440 | tf_op jit(solution)/shard_map/ppermute | solution.py:368
  76.2 4.2 %collective-permute-start.7 = (bf16[16,128,128]{2,1,0:T(8,128)(2,1)S(1)}, bf16[16,128,128]{2,1,0:T(8,128)(2,1)S(1)}, u32[]{:S(2)}, u32[]{:S(2)}) collective-permute-start(bf16[16,128,128]{2,1,0:T(8,128)(2,1)S(1)} %shard_map.92), channel_id=1, source_target_pairs={{0,32},{1,33},{2,34},{3,35},{4,36},{5,37},{6,38},{7,39},{8,40},{9,... | collective-permute-start | bytes 1572872 | tf_op jit(solution)/shard_map/ppermute | solution.py:373
  83.6 32.0 %all-to-all-start.1 = ((bf16[16,64,128]{2,1,0:T(8,128)(2,1)}), bf16[16,64,128]{2,1,0:T(8,128)(2,1)S(1)}, u32[]{:S(2)}, u32[]{:S(2)}) async-start(bf16[16,64,128]{2,1,0:T(8,128)(2,1)} %shard_map.93), calls=%async_computation.1 | async-start | bytes 524288 | tf_op jit(solution)/shard_map/all_to_all | solution.py:376
  96.2 8.8 %collective-permute-start.8 = (bf16[4,32,1024]{2,1,0:T(8,128)(2,1)S(1)}, bf16[4,32,1024]{2,1,0:T(8,128)(2,1)S(1)}, u32[]{:S(2)}, u32[]{:S(2)}) collective-permute-start(bf16[4,32,1024]{2,1,0:T(8,128)(2,1)S(1)} %pad_maximum_fusion.refs_0_), channel_id=1, source_target_pairs={{0,32},{1,33},{2,34},{3,35},{4,36},{5,37},{6,38},{7,39},{8,40},{9,... | collective-permute-start | bytes 786440 | tf_op jit(solution)/shard_map/ppermute | solution.py:374
  98.5 6.5 %collective-permute-start.11 = (bf16[4,32,1024]{2,1,0:T(8,128)(2,1)S(1)}, bf16[4,32,1024]{2,1,0:T(8,128)(2,1)S(1)}, u32[]{:S(2)}, u32[]{:S(2)}) collective-permute-start(bf16[4,32,1024]{2,1,0:T(8,128)(2,1)S(1)} %collective-permute-done.6.refs_3_), channel_id=1, source_target_pairs={{0,32},{1,33},{2,34},{3,35},{4,36},{5,37},{6,38},{7,39},{8,40},{9,... | collective-permute-start | bytes 786440 | tf_op jit(solution)/shard_map/ppermute | solution.py:374
  100.6 4.4 %collective-permute-start.10 = (bf16[4,32,1024]{2,1,0:T(8,128)(2,1)S(1)}, bf16[4,32,1024]{2,1,0:T(8,128)(2,1)S(1)}, u32[]{:S(2)}, u32[]{:S(2)}) collective-permute-start(bf16[4,32,1024]{2,1,0:T(8,128)(2,1)S(1)} %collective-permute-done.5.refs_2_), channel_id=1, source_target_pairs={{0,32},{1,33},{2,34},{3,35},{4,36},{5,37},{6,38},{7,39},{8,40},{9,... | collective-permute-start | bytes 786440 | tf_op jit(solution)/shard_map/ppermute | solution.py:374
  102.9 3.4 %collective-permute-start.9 = (bf16[4,32,1024]{2,1,0:T(8,128)(2,1)S(1)}, bf16[4,32,1024]{2,1,0:T(8,128)(2,1)S(1)}, u32[]{:S(2)}, u32[]{:S(2)}) collective-permute-start(bf16[4,32,1024]{2,1,0:T(8,128)(2,1)S(1)} %collective-permute-done.4.refs_1_), channel_id=1, source_target_pairs={{0,32},{1,33},{2,34},{3,35},{4,36},{5,37},{6,38},{7,39},{8,40},{9,... | collective-permute-start | bytes 786440 | tf_op jit(solution)/shard_map/ppermute | solution.py:374
  118.5 30.3 %all-to-all-start.2 = ((bf16[32,16,1024]{2,1,0:T(8,128)(2,1)}), bf16[32,16,1024]{2,1,0:T(8,128)(2,1)S(1)}, u32[]{:S(2)}, u32[]{:S(2)}) async-start(bf16[32,16,1024]{2,1,0:T(8,128)(2,1)} %bitcast.9), calls=%async_computation.2 | async-start | bytes 2097152 | tf_op jit(solution)/shard_map/all_to_all | solution.py:383
  140.2 8.7 %collective-permute-start.12 = (bf16[2,144,1024]{2,1,0:T(8,128)(2,1)}, bf16[2,144,1024]{2,1,0:T(8,128)(2,1)S(1)}, u32[]{:S(2)}, u32[]{:S(2)}) collective-permute-start(bf16[2,144,1024]{2,1,0:T(8,128)(2,1)} %get-tuple-element.17), channel_id=1, source_target_pairs={{0,32},{1,33},{2,34},{3,35},{4,36},{5,37},{6,38},{7,39},{8,40},{9,... | collective-permute-start | bytes 1769480 | tf_op jit(solution)/shard_map/ppermute | solution.py:387
  142.1 6.8 %collective-permute-start.13 = (bf16[2,144,1024]{2,1,0:T(8,128)(2,1)}, bf16[2,144,1024]{2,1,0:T(8,128)(2,1)S(1)}, u32[]{:S(2)}, u32[]{:S(2)}) collective-permute-start(bf16[2,144,1024]{2,1,0:T(8,128)(2,1)} %get-tuple-element.18), channel_id=1, source_target_pairs={{0,32},{1,33},{2,34},{3,35},{4,36},{5,37},{6,38},{7,39},{8,40},{9,... | collective-permute-start | bytes 1769480 | tf_op jit(solution)/shard_map/ppermute | solution.py:387
  144.5 4.4 %collective-permute-start.14 = (bf16[2,144,1024]{2,1,0:T(8,128)(2,1)S(1)}, bf16[2,144,1024]{2,1,0:T(8,128)(2,1)}, u32[]{:S(2)}, u32[]{:S(2)}) collective-permute-start(bf16[2,144,1024]{2,1,0:T(8,128)(2,1)S(1)} %get-tuple-element.19), channel_id=1, source_target_pairs={{0,32},{1,33},{2,34},{3,35},{4,36},{5,37},{6,38},{7,39},{8,40},{9,... | collective-permute-start | bytes 1769480 | tf_op jit(solution)/shard_map/ppermute | solution.py:387
  146.5 4.4 %collective-permute-start.15 = (bf16[2,144,1024]{2,1,0:T(8,128)(2,1)}, bf16[2,144,1024]{2,1,0:T(8,128)(2,1)}, u32[]{:S(2)}, u32[]{:S(2)}) collective-permute-start(bf16[2,144,1024]{2,1,0:T(8,128)(2,1)} %get-tuple-element.20), channel_id=1, source_target_pairs={{0,32},{1,33},{2,34},{3,35},{4,36},{5,37},{6,38},{7,39},{8,40},{9,... | collective-permute-start | bytes 1769480 | tf_op jit(solution)/shard_map/ppermute | solution.py:387
  150.8 1.7 copy-start.3
Sparse Core Ops, SparseCore 0:
  9.4 126.2 all-gather.2

commit v4 on v3

--- a/solution.py
+++ b/solution.py
@@ -90,7 +90,7 @@
     )(gate_up, down)
 
 
-def pack_heads_kernel(q_ref, k_ref, v_ref, after_ref, out_ref, rows, sems):
+def pack_heads_kernel(q_ref, k_ref, v_ref, out_ref, rows, sems):
     copies = [
         pltpu.make_async_copy(ref.at[0], rows.at[j], sems.at[j])
         for j, ref in enumerate((q_ref, k_ref, v_ref))
@@ -106,15 +106,16 @@
                 ]
 
 
-def pack_heads(q, k, v, after):
+def pack_heads(q, k, v):
     return pl.pallas_call(
         pack_heads_kernel,
         out_shape=jax.ShapeDtypeStruct((16, 192, 128), BF),
-        in_specs=[HBM] * 3 + [ANY],
+        in_specs=[HBM] * 3,
         out_specs=VMEM,
         scratch_shapes=[pltpu.VMEM((3,) + q.shape[1:], BF), pltpu.SemaphoreType.DMA((3,))],
         compiler_params=params(56),
-    )(q, k, v, after)
+        cost_estimate=pl.CostEstimate(flops=0, bytes_accessed=20 << 20, transcendentals=0),
+    )(q, k, v)
 
 
 def keys_kernel(heads_ref, *refs):
@@ -129,6 +130,21 @@
         out_specs=VMEM,
         compiler_params=params(4),
     )(heads, *after)
+
+
+def line_kernel(*refs):
+    for n, ref in enumerate(refs[:4]):
+        refs[-1][n] = ref[...]
+
+
+def line_of(pieces, after):
+    return pl.pallas_call(
+        line_kernel,
+        out_shape=jax.ShapeDtypeStruct((4,) + pieces[0].shape, BF),
+        in_specs=[VMEM] * 4 + [ANY],
+        out_specs=VMEM,
+        compiler_params=params(4),
+    )(*pieces, after)
 
 
 def attention_kernel(core_ref, own_ref, oth_ref, out_ref):
@@ -256,35 +272,30 @@
     )(where, ctx, *own, *oth, residual, router.T, ids[0].T)
 
 
-def pick_kernel(core_ref, weights_ref, after_ref, *refs):
+def pick_kernel(flip, core_ref, weights_ref, after_ref, *refs):
     sems = refs[-1]
     core = core_ref[0]
-    copies = [
-        pltpu.make_async_copy(
-            weights_ref.at[pl.ds((1 - core) * 8 + n * PART, PART)], ref, sems.at[n]
+    first = ((1 - core) if flip else core) * 8
+    copies = []
+    for n, ref in enumerate(refs[:-1]):
+        size = ref.shape[0]
+        copies.append(
+            pltpu.make_async_copy(weights_ref.at[pl.ds(first + n * size, size)], ref, sems.at[n])
         )
-        for n, ref in enumerate(refs[:-2])
-    ]
-    copies.append(
-        pltpu.make_async_copy(weights_ref.at[pl.ds(core * 8, 8)], refs[-2], sems.at[8 // PART])
-    )
     for copy in copies:
         copy.start()
     for copy in copies:
         copy.wait()
 
 
-def pick(core, weights, after):
-    parts = 8 // PART
-    one = weights.shape[1:]
-    return pl.pallas_call(
-        pick_kernel,
-        out_shape=(jax.ShapeDtypeStruct((PART,) + one, BF),) * parts
-        + (jax.ShapeDtypeStruct((8,) + one, BF),),
+def pick(core, weights, after, flip, parts):
+    return pl.pallas_call(
+        functools.partial(pick_kernel, flip),
+        out_shape=(jax.ShapeDtypeStruct((8 // parts,) + weights.shape[1:], BF),) * parts,
         in_specs=[SMEM, HBM, ANY],
-        out_specs=(VMEM,) * (parts + 1),
-        scratch_shapes=[pltpu.SemaphoreType.DMA((parts + 1,))],
-        compiler_params=params(52),
+        out_specs=(VMEM,) * parts,
+        scratch_shapes=[pltpu.SemaphoreType.DMA((parts,))],
+        compiler_params=params(52 if flip else 40),
         cost_estimate=pl.CostEstimate(flops=0, bytes_accessed=8 << 20, transcendentals=0),
     )(core, weights, after)
 
@@ -364,15 +375,16 @@
 
     moved = lax.ppermute(out_proj, ALL, HALF_MOVE)
     shard = jnp.where(lax.axis_index("zhi") == core_index, out_proj, moved)
-    line = jnp.stack([shard] + [lax.ppermute(shard, ALL, plane_pairs(0, d)) for d in (1, 2, 3)])
+    pieces = [shard] + [lax.ppermute(shard, ALL, plane_pairs(0, d)) for d in (1, 2, 3)]
+
+    heads = pack_heads(query_rows, key_rows, value_rows)
+    heads = lax.all_to_all(heads, ("zlo", "core"), split_axis=0, concat_axis=0, tiled=True)
+    oth_keys = lax.ppermute(keys_of(heads, pieces), ALL, CORE_SWAP)
+    context = attention(core, heads, oth_keys)
+
+    line = line_of(pieces, context)
     proj_own = [line] + [lax.ppermute(line, ALL, plane_pairs(1, d)) for d in (1, 2, 3)]
-
-    heads = pack_heads(query_rows, key_rows, value_rows, moved)
-    heads = lax.all_to_all(heads, ("zlo", "core"), split_axis=0, concat_axis=0, tiled=True)
-    keys = keys_of(heads, proj_own)
-    oth_keys = lax.ppermute(keys, ALL, CORE_SWAP)
     proj_oth = [lax.ppermute(p, ALL, CORE_SWAP) for p in proj_own]
-    context = attention(core, heads, oth_keys)
     context = lax.all_to_all(context, ("zlo", "core"), split_axis=0, concat_axis=0, tiled=True)
 
     xy = lax.axis_index("xy").astype(jnp.int32).reshape(1)
@@ -383,8 +395,9 @@
     arrived = lax.all_to_all(
         outgoing.reshape(32, SLOT, 1024), ("core", "xy"), split_axis=0, concat_axis=0, tiled=True
     )
-    *to_send, own_weights = pick(core, weights, target)
+    to_send = pick(core, weights, target, True, 8 // PART)
     oth_weights = [lax.ppermute(w, ALL, CORE_SWAP) for w in to_send]
+    (own_weights,) = pick(core, weights, target, False, 1)
     produced = experts(core, arrived.reshape(32 * SLOT, 1024), own_weights, oth_weights)
     back = lax.all_to_all(
         produced.reshape(32, SLOT, 1024), ("core", "xy"), split_axis=0, concat_axis=0, tiled=True

time: 191 us -> 185 us (0.969)
  waiting for transfers between devices: 44.1 us -> 29.4 us
  starting transfers between devices: 83.9 us -> 97.1 us
    all_to_all x1, starting transfers between devices: 12.6 us -> 31.1 us  [on_device(): lax.all_to_all(context, ('zlo', 'core'), split_axis=0, concat_axis=0, til...]
    ppermute x1, waiting for transfers between devices: 2.2 us -> 18 us  [on_device(): moved = lax.ppermute(out_proj, ALL, HALF_MOVE)]
    all_gather x1, waiting for transfers between devices: 10 us -> 0.02 us  [on_device(): weights = lax.all_gather(packed, ('zhi', 'zlo'), axis=0, tiled=False)]
    all_to_all x1, waiting for transfers between devices: 9.36 us -> 0.01 us  [on_device(): lax.all_to_all(context, ('zlo', 'core'), split_axis=0, concat_axis=0, til...]
    ppermute x1, starting transfers between devices: 15.9 us -> 8.22 us  [on_device(): moved = lax.ppermute(out_proj, ALL, HALF_MOVE)]
    all_to_all x1, waiting for transfers between devices: 7.34 us -> 0.01 us  [on_device(): lax.all_to_all(heads, ('zlo', 'core'), split_axis=0, concat_axis=0, tiled...]
    ppermute x3, waiting for transfers between devices: 4.99 us -> 0.01 us  [on_device(): lax.ppermute(line, ALL, plane_pairs(1, d))]
    all_to_all x1, starting transfers between devices: 8.09 us -> 12.6 us  [on_device(): lax.all_to_all(heads, ('zlo', 'core'), split_axis=0, concat_axis=0, tiled...]
  transfers between devices with their start and end apart: 20 -> 20, of which waited for: 11 -> 6; matrix products, arithmetic and copies ran while one was open for 1% -> 1% of each run, Pallas kernels for 7% -> 6%
where the time goes in v4:
time: 185 us; the launch traced here: 182 us
  starting transfers between devices  97.1 us (52%)
  waiting for transfers between devices  29.4 us (16%)
  blocking collectives  21.1 us (11%)
  Pallas kernels  19.1 us (10%)
  between operations  13.7 us (7%)
    all_to_all x1, starting transfers between devices, on_device(): lax.all_to_all(context, ('zlo', 'core'), split_axis=0, concat_axis=0, til...  31.1 us
    all_to_all x1, blocking collectives, on_device(): lax.all_to_all(produced.reshape(32, SLOT, 1024), ('core', 'xy'), split_ax...  21.1 us
    ppermute x1, waiting for transfers between devices, on_device(): moved = lax.ppermute(out_proj, ALL, HALF_MOVE)  18 us
    all_to_all x1, starting transfers between devices, on_device(): lax.all_to_all(heads, ('zlo', 'core'), split_axis=0, concat_axis=0, tiled...  12.6 us
    ppermute x3, starting transfers between devices, on_device(): lax.ppermute(line, ALL, plane_pairs(1, d))  9.41 us
    ppermute x4, starting transfers between devices, on_device(): oth_weights = [lax.ppermute(w, ALL, CORE_SWAP) for w in to_send]  8.66 us
    ppermute x4, starting transfers between devices, on_device(): proj_oth = [lax.ppermute(p, ALL, CORE_SWAP) for p in proj_own]  8.65 us
    ppermute x3, starting transfers between devices, on_device(): lax.ppermute(shard, ALL, plane_pairs(0, d))  8.62 us
  transfers between devices with their start and end apart: 20, of which 6 were waited for; matrix products, arithmetic and copies ran while one was open for 1% of the time, Pallas kernels for 6%

profile of v4, /device:TPU:6, one launch (start us, length us, event | category | flops | bytes accessed | tf_op | source)
XLA Modules:
  0.0 182.2 jit_solution(16229404701746153918)
XLA Ops:
  6.5 1.8 shard_map.96
  8.3 0.0 all-gather.3.cloned.1.call-update
  8.4 2.1 %shard_map.91 = bf16[16,192,128]{2,1,0:T(8,128)(2,1)} custom-call(bf16[1,128,1024]{2,1,0:T(8,128)(2,1)} %q_ref.1, bf16[1,128,1024]{2,1,0:T(8,128)(2,1)} %k_ref.1, bf16[1,128,1024]{2,1,0:T(8,128)(2,1)} %v_ref.1), custom_call_target="tpu_custom_call" | custom-call | bytes 20971520 | tf_op jit(solution)/shard_map/pallas_call | solution.py:110
  10.5 12.6 %all-to-all-start = ((bf16[16,192,128]{2,1,0:T(8,128)(2,1)}), bf16[16,192,128]{2,1,0:T(8,128)(2,1)S(1)}, u32[]{:S(2)}, u32[]{:S(2)}) async-start(bf16[16,192,128]{2,1,0:T(8,128)(2,1)} %shard_map.91), calls=%async_computation | async-start | bytes 1572864 | tf_op jit(solution)/shard_map/all_to_all | solution.py:381
  23.1 8.2 %collective-permute-start = (bf16[32,1024]{1,0:T(8,128)(2,1)}, bf16[32,1024]{1,0:T(8,128)(2,1)S(1)}, u32[]{:S(2)}, u32[]{:S(2)}) collective-permute-start(bf16[32,1024]{1,0:T(8,128)(2,1)} %param.13), channel_id=1, source_target_pairs={{0,16},{1,17},{2,18},{3,19},{4,20},{5,21},{6,22},{7,23},{8,24},{9,... | collective-permute-start | bytes 196616 | tf_op jit(solution)/shard_map/ppermute | solution.py:376
  31.4 18.0 %collective-permute-done = bf16[32,1024]{1,0:T(8,128)(2,1)S(1)} collective-permute-done((bf16[32,1024]{1,0:T(8,128)(2,1)}, bf16[32,1024]{1,0:T(8,128)(2,1)S(1)}, u32[]{:S(2)}, u32[]{:S(2)}) %collective-permute-start) | collective-permute-done | bytes 65568 | tf_op jit(solution)/shard_map/ppermute | solution.py:376
  49.4 0.8 broadcast_select_fusion.refs_0_
  50.2 2.4 %collective-permute-start.3 = (bf16[32,1024]{1,0:T(8,128)(2,1)S(1)}, bf16[32,1024]{1,0:T(8,128)(2,1)S(1)}, u32[]{:S(2)}, u32[]{:S(2)}) collective-permute-start(bf16[32,1024]{1,0:T(8,128)(2,1)S(1)} %broadcast_select_fusion.refs_0_), channel_id=1, source_target_pairs={{0,4},{1,5},{2,6},{3,7},{4,8},{5,9},{6,10},{7,11},{8,12},{9,13},{1... | collective-permute-start | bytes 196616 | tf_op jit(solution)/shard_map/ppermute | solution.py:378
  52.6 4.3 %collective-permute-start.2 = (bf16[32,1024]{1,0:T(8,128)(2,1)S(1)}, bf16[32,1024]{1,0:T(8,128)(2,1)S(1)}, u32[]{:S(2)}, u32[]{:S(2)}) collective-permute-start(bf16[32,1024]{1,0:T(8,128)(2,1)S(1)} %broadcast_select_fusion.refs_0_), channel_id=1, source_target_pairs={{0,8},{1,9},{2,10},{3,11},{4,12},{5,13},{6,14},{7,15},{8,0},{9,1},... | collective-permute-start | bytes 196616 | tf_op jit(solution)/shard_map/ppermute | solution.py:378
  57.0 1.9 %collective-permute-start.1 = (bf16[32,1024]{1,0:T(8,128)(2,1)S(1)}, bf16[32,1024]{1,0:T(8,128)(2,1)S(1)}, u32[]{:S(2)}, u32[]{:S(2)}) collective-permute-start(bf16[32,1024]{1,0:T(8,128)(2,1)S(1)} %broadcast_select_fusion.refs_0_), channel_id=1, source_target_pairs={{0,12},{1,13},{2,14},{3,15},{4,0},{5,1},{6,2},{7,3},{8,4},{9,5},{1... | collective-permute-start | bytes 196616 | tf_op jit(solution)/shard_map/ppermute | solution.py:378
  58.9 0.0 collective-permute-done.3.refs_3_
  58.9 1.4 collective-permute-done.2.refs_2_
  60.3 4.0 %collective-permute-done.1.refs_1_ = bf16[32,1024]{1,0:T(8,128)(2,1)S(1)} collective-permute-done((bf16[32,1024]{1,0:T(8,128)(2,1)S(1)}, bf16[32,1024]{1,0:T(8,128)(2,1)S(1)}, u32[]{:S(2)}, u32[]{:S(2)}) %collective-permute-start.1) | collective-permute-done | bytes 65568 | tf_op jit(solution)/shard_map/ppermute | solution.py:378
  64.4 3.0 %collective-permute-start.4 = (bf16[16,128,128]{2,1,0:T(8,128)(2,1)S(1)}, bf16[16,128,128]{2,1,0:T(8,128)(2,1)S(1)}, u32[]{:S(2)}, u32[]{:S(2)}) collective-permute-start(bf16[16,128,128]{2,1,0:T(8,128)(2,1)S(1)} %shard_map.92), channel_id=1, source_target_pairs={{0,32},{1,33},{2,34},{3,35},{4,36},{5,37},{6,38},{7,39},{8,40},{9,... | collective-permute-start | bytes 1572872 | tf_op jit(solution)/shard_map/ppermute | solution.py:382
  67.3 1.5 collective-permute-done.4.oth_ref
  68.9 3.2 %shard_map.93.refs_4_ = bf16[16,64,128]{2,1,0:T(8,128)(2,1)} custom-call(s32[1]{0:T(128)} %bitcast.core_ref, bf16[16,192,128]{2,1,0:T(8,128)(2,1)S(1)} %all-to-all-done.heads_ref.own_ref, bf16[16,128,128]{2,1,0:T(8,128)(2,1)S(1)} %collective-permute-done.4.oth_ref), custom_call_target="tpu_custom_call" | custom-call | flops 671088640 | bytes 2097152 | tf_op jit(solution)/shard_map/pallas_call | solution.py:190
  72.0 31.1 %all-to-all-start.1 = ((bf16[16,64,128]{2,1,0:T(8,128)(2,1)}), bf16[16,64,128]{2,1,0:T(8,128)(2,1)S(1)}, u32[]{:S(2)}, u32[]{:S(2)}) async-start(bf16[16,64,128]{2,1,0:T(8,128)(2,1)} %shard_map.93.refs_4_), calls=%async_computation.1 | async-start | bytes 524288 | tf_op jit(solution)/shard_map/all_to_all | solution.py:388
  103.2 1.9 %collective-permute-start.7 = (bf16[4,32,1024]{2,1,0:T(8,128)(2,1)S(1)}, bf16[4,32,1024]{2,1,0:T(8,128)(2,1)S(1)}, u32[]{:S(2)}, u32[]{:S(2)}) collective-permute-start(bf16[4,32,1024]{2,1,0:T(8,128)(2,1)S(1)} %shard_map.94.refs_0_), channel_id=1, source_target_pairs={{0,1},{1,2},{2,3},{3,0},{4,5},{5,6},{6,7},{7,4},{8,9},{9,10},{10,1... | collective-permute-start | bytes 786440 | tf_op jit(solution)/shard_map/ppermute | solution.py:386
  105.1 5.5 %collective-permute-start.6 = (bf16[4,32,1024]{2,1,0:T(8,128)(2,1)S(1)}, bf16[4,32,1024]{2,1,0:T(8,128)(2,1)S(1)}, u32[]{:S(2)}, u32[]{:S(2)}) collective-permute-start(bf16[4,32,1024]{2,1,0:T(8,128)(2,1)S(1)} %shard_map.94.refs_0_), channel_id=1, source_target_pairs={{0,2},{1,3},{2,0},{3,1},{4,6},{5,7},{6,4},{7,5},{8,10},{9,11},{10,... | collective-permute-start | bytes 786440 | tf_op jit(solution)/shard_map/ppermute | solution.py:386
  110.6 2.0 %collective-permute-start.5 = (bf16[4,32,1024]{2,1,0:T(8,128)(2,1)S(1)}, bf16[4,32,1024]{2,1,0:T(8,128)(2,1)S(1)}, u32[]{:S(2)}, u32[]{:S(2)}) collective-permute-start(bf16[4,32,1024]{2,1,0:T(8,128)(2,1)S(1)} %shard_map.94.refs_0_), channel_id=1, source_target_pairs={{0,3},{1,0},{2,1},{3,2},{4,7},{5,4},{6,5},{7,6},{8,11},{9,8},{10,9... | collective-permute-start | bytes 786440 | tf_op jit(solution)/shard_map/ppermute | solution.py:386
  112.6 1.9 %collective-permute-start.8 = (bf16[4,32,1024]{2,1,0:T(8,128)(2,1)S(1)}, bf16[4,32,1024]{2,1,0:T(8,128)(2,1)S(1)}, u32[]{:S(2)}, u32[]{:S(2)}) collective-permute-start(bf16[4,32,1024]{2,1,0:T(8,128)(2,1)S(1)} %shard_map.94.refs_0_), channel_id=1, source_target_pairs={{0,32},{1,33},{2,34},{3,35},{4,36},{5,37},{6,38},{7,39},{8,40},{9,... | collective-permute-start | bytes 786440 | tf_op jit(solution)/shard_map/ppermute | solution.py:387
  114.5 0.0 collective-permute-done.7.refs_3_
  114.5 2.4 %collective-permute-start.11 = (bf16[4,32,1024]{2,1,0:T(8,128)(2,1)S(1)}, bf16[4,32,1024]{2,1,0:T(8,128)(2,1)S(1)}, u32[]{:S(2)}, u32[]{:S(2)}) collective-permute-start(bf16[4,32,1024]{2,1,0:T(8,128)(2,1)S(1)} %collective-permute-done.7.refs_3_), channel_id=1, source_target_pairs={{0,32},{1,33},{2,34},{3,35},{4,36},{5,37},{6,38},{7,39},{8,40},{9,... | collective-permute-start | bytes 786440 | tf_op jit(solution)/shard_map/ppermute | solution.py:387
  117.0 0.0 collective-permute-done.6.refs_2_
  117.0 1.9 %collective-permute-start.10 = (bf16[4,32,1024]{2,1,0:T(8,128)(2,1)S(1)}, bf16[4,32,1024]{2,1,0:T(8,128)(2,1)S(1)}, u32[]{:S(2)}, u32[]{:S(2)}) collective-permute-start(bf16[4,32,1024]{2,1,0:T(8,128)(2,1)S(1)} %collective-permute-done.6.refs_2_), channel_id=1, source_target_pairs={{0,32},{1,33},{2,34},{3,35},{4,36},{5,37},{6,38},{7,39},{8,40},{9,... | collective-permute-start | bytes 786440 | tf_op jit(solution)/shard_map/ppermute | solution.py:387
  118.9 0.0 collective-permute-done.5.refs_1_
  118.9 2.4 %collective-permute-start.9 = (bf16[4,32,1024]{2,1,0:T(8,128)(2,1)S(1)}, bf16[4,32,1024]{2,1,0:T(8,128)(2,1)S(1)}, u32[]{:S(2)}, u32[]{:S(2)}) collective-permute-start(bf16[4,32,1024]{2,1,0:T(8,128)(2,1)S(1)} %collective-permute-done.5.refs_1_), channel_id=1, source_target_pairs={{0,32},{1,33},{2,34},{3,35},{4,36},{5,37},{6,38},{7,39},{8,40},{9,... | collective-permute-start | bytes 786440 | tf_op jit(solution)/shard_map/ppermute | solution.py:387
  121.3 0.1 pad_add_fusion.where_ref
  121.4 0.0 collective-permute-done.8.refs_4_
  121.4 0.0 collective-permute-done.11.refs_7_
  121.4 0.0 collective-permute-done.10.refs_6_
  121.4 1.0 collective-permute-done.9.refs_5_
  122.5 2.9 %shard_map.95 = (bf16[128,1024]{1,0:T(8,128)(2,1)S(1)}, bf16[512,1024]{1,0:T(8,128)(2,1)}, f32[2,128]{1,0:T(2,128)S(1)}, s32[2,128]{1,0:T(2,128)S(1)}) custom-call(s32[3]{0:T(128)S(1)} %pad_add_fusion.where_ref, bf16[16,64,128]{2,1,0:T(8,128)(2,1)S(1)} %all-to-all-done.1.ctx_ref, bf16[4,32,1024]{2,1,0:T(8,128)(2,1)S(1)} %shard_map.94.refs_0_, ...), custom_call_target="tpu_custom_call" | custom-call | flops 419430400 | bytes 4194304 | tf_op jit(solution)/shard_map/pallas_call | solution.py:254
  125.4 0.7 copy-done.1
  126.1 6.8 %all-to-all-start.2 = ((bf16[32,16,1024]{2,1,0:T(8,128)(2,1)}), bf16[32,16,1024]{2,1,0:T(8,128)(2,1)S(1)}, u32[]{:S(2)}, u32[]{:S(2)}) async-start(bf16[32,16,1024]{2,1,0:T(8,128)(2,1)} %bitcast.5), calls=%async_computation.2 | async-start | bytes 2097152 | tf_op jit(solution)/shard_map/all_to_all | solution.py:395
  132.9 0.0 all-gather.3.cloned.1.call-done
  132.9 3.3 %shard_map.98 = (bf16[2,144,1024]{2,1,0:T(8,128)(2,1)}, bf16[2,144,1024]{2,1,0:T(8,128)(2,1)}, bf16[2,144,1024]{2,1,0:T(8,128)(2,1)}, bf16[2,144,1024]{2,1,0:T(8,128)(2,1)}) custom-call(s32[1]{0:T(128)} %bitcast.core_ref, bf16[16,144,1024]{2,1,0:T(8,128)(2,1)} %bitcast.11, s32[2,128]{1,0:T(2,128)S(1)} %get-tuple-element.14.after_ref.target_ref), custom_call_target="tpu_custom_call" | custom-call | bytes 8388608 | tf_op jit(solution)/shard_map/pallas_call | solution.py:292
  136.2 2.1 %collective-permute-start.12 = (bf16[2,144,1024]{2,1,0:T(8,128)(2,1)}, bf16[2,144,1024]{2,1,0:T(8,128)(2,1)}, u32[]{:S(2)}, u32[]{:S(2)}) collective-permute-start(bf16[2,144,1024]{2,1,0:T(8,128)(2,1)} %get-tuple-element.15), channel_id=1, source_target_pairs={{0,32},{1,33},{2,34},{3,35},{4,36},{5,37},{6,38},{7,39},{8,40},{9,... | collective-permute-start | bytes 1769480 | tf_op jit(solution)/shard_map/ppermute | solution.py:399
  138.3 2.2 %collective-permute-start.13 = (bf16[2,144,1024]{2,1,0:T(8,128)(2,1)}, bf16[2,144,1024]{2,1,0:T(8,128)(2,1)}, u32[]{:S(2)}, u32[]{:S(2)}) collective-permute-start(bf16[2,144,1024]{2,1,0:T(8,128)(2,1)} %get-tuple-element.16), channel_id=1, source_target_pairs={{0,32},{1,33},{2,34},{3,35},{4,36},{5,37},{6,38},{7,39},{8,40},{9,... | collective-permute-start | bytes 1769480 | tf_op jit(solution)/shard_map/ppermute | solution.py:399
  140.6 2.1 %collective-permute-start.14 = (bf16[2,144,1024]{2,1,0:T(8,128)(2,1)}, bf16[2,144,1024]{2,1,0:T(8,128)(2,1)}, u32[]{:S(2)}, u32[]{:S(2)}) collective-permute-start(bf16[2,144,1024]{2,1,0:T(8,128)(2,1)} %get-tuple-element.17), channel_id=1, source_target_pairs={{0,32},{1,33},{2,34},{3,35},{4,36},{5,37},{6,38},{7,39},{8,40},{9,... | collective-permute-start | bytes 1769480 | tf_op jit(solution)/shard_map/ppermute | solution.py:399
  142.7 2.2 %collective-permute-start.15 = (bf16[2,144,1024]{2,1,0:T(8,128)(2,1)}, bf16[2,144,1024]{2,1,0:T(8,128)(2,1)}, u32[]{:S(2)}, u32[]{:S(2)}) collective-permute-start(bf16[2,144,1024]{2,1,0:T(8,128)(2,1)} %get-tuple-element.18), channel_id=1, source_target_pairs={{0,32},{1,33},{2,34},{3,35},{4,36},{5,37},{6,38},{7,39},{8,40},{9,... | collective-permute-start | bytes 1769480 | tf_op jit(solution)/shard_map/ppermute | solution.py:399
  144.9 0.2 shard_map.97.own_ref
  145.1 3.4 %all-to-all-done.2 = bf16[32,16,1024]{2,1,0:T(8,128)(2,1)S(1)} async-done(((bf16[32,16,1024]{2,1,0:T(8,128)(2,1)}), bf16[32,16,1024]{2,1,0:T(8,128)(2,1)S(1)}, u32[]{:S(2)}, u32[]{:S(2)}) %all-to-all-start.2) | async-done | bytes 1048608 | tf_op jit(solution)/shard_map/all_to_all | solution.py:395
  148.5 0.0 collective-permute-done.13.refs_1_
  148.5 0.0 copy-start.2
  148.5 4.5 %shard_map.99 = bf16[512,1024]{1,0:T(8,128)(2,1)S(1)} custom-call(s32[1]{0:T(128)} %bitcast.core_ref, bf16[512,1024]{1,0:T(8,128)(2,1)S(1)} %bitcast.14, bf16[8,144,1024]{2,1,0:T(8,128)(2,1)S(1)} %shard_map.97.own_ref, bf16[2,144,1024]{2,1,0:T(8,128)(2,1)} %collective-permute-done.12.refs_0_, bf16[2,144,1024]{2,1,0:T(8,128)(2,1)} %collective-permute-done.13.refs_1_, ...), custom_call_target="tpu_custom_call" | custom-call | flops 2415919104 | bytes 7340032 | tf_op jit(solution)/shard_map/pallas_call | solution.py:325
  153.0 21.1 %all_to_all.20 = bf16[32,16,1024]{2,1,0:T(8,128)(2,1)S(1)} all-to-all(bf16[32,16,1024]{2,1,0:T(8,128)(2,1)S(1)} %bitcast.15), channel_id=1, replica_groups=mesh['zlo'=8,'core'=2,'zhi'=2,'xy'=16] {'core','xy'}, dimensions={0} | all-to-all | bytes 2097152 | tf_op jit(solution)/shard_map/all_to_all | solution.py:402
  174.1 1.2 shard_map.100
  (18 shorter events, 0.1 us)
Async XLA Ops:
  6.5 115.9 %copy-start.5 = (s32[1,128,2]{1,2,0:T(2,128)S(1)}, s32[1,128,2]{1,2,0:T(2,128)}, u32[]{:S(2)}) copy-start(s32[1,128,2]{1,2,0:T(2,128)} %param.15) | copy-start | bytes 3076
  6.5 115.9 %copy-start.4 = (bf16[1024,32]{0,1:T(8,128)(2,1)S(1)}, bf16[1024,32]{0,1:T(8,128)(2,1)}, u32[]{:S(2)}) copy-start(bf16[1024,32]{0,1:T(8,128)(2,1)} %param.14) | copy-start | bytes 196612
  6.5 115.9 %copy-start.3 = (bf16[1,128,1024]{2,1,0:T(8,128)(2,1)S(1)}, bf16[1,128,1024]{2,1,0:T(8,128)(2,1)}, u32[]{:S(2)}) copy-start(bf16[1,128,1024]{2,1,0:T(8,128)(2,1)} %refs_8_.1) | copy-start | bytes 786436
  6.5 126.4 %all-gather.3.cloned.1.call-start = ((), (), s32[]{:S(2)}) async-start(), calls=%async_computation.4 | async-start | bytes 5013504 | tf_op jit(solution)/shard_map/all_gather | solution.py:374
  10.5 53.9 %all-to-all-start = ((bf16[16,192,128]{2,1,0:T(8,128)(2,1)}), bf16[16,192,128]{2,1,0:T(8,128)(2,1)S(1)}, u32[]{:S(2)}, u32[]{:S(2)}) async-start(bf16[16,192,128]{2,1,0:T(8,128)(2,1)} %shard_map.91), calls=%async_computation | async-start | bytes 1572864 | tf_op jit(solution)/shard_map/all_to_all | solution.py:381
  23.1 26.3 %collective-permute-start = (bf16[32,1024]{1,0:T(8,128)(2,1)}, bf16[32,1024]{1,0:T(8,128)(2,1)S(1)}, u32[]{:S(2)}, u32[]{:S(2)}) collective-permute-start(bf16[32,1024]{1,0:T(8,128)(2,1)} %param.13), channel_id=1, source_target_pairs={{0,16},{1,17},{2,18},{3,19},{4,20},{5,21},{6,22},{7,23},{8,24},{9,... | collective-permute-start | bytes 196616 | tf_op jit(solution)/shard_map/ppermute | solution.py:376
  50.2 8.7 %collective-permute-start.3 = (bf16[32,1024]{1,0:T(8,128)(2,1)S(1)}, bf16[32,1024]{1,0:T(8,128)(2,1)S(1)}, u32[]{:S(2)}, u32[]{:S(2)}) collective-permute-start(bf16[32,1024]{1,0:T(8,128)(2,1)S(1)} %broadcast_select_fusion.refs_0_), channel_id=1, source_target_pairs={{0,4},{1,5},{2,6},{3,7},{4,8},{5,9},{6,10},{7,11},{8,12},{9,13},{1... | collective-permute-start | bytes 196616 | tf_op jit(solution)/shard_map/ppermute | solution.py:378
  52.6 7.7 %collective-permute-start.2 = (bf16[32,1024]{1,0:T(8,128)(2,1)S(1)}, bf16[32,1024]{1,0:T(8,128)(2,1)S(1)}, u32[]{:S(2)}, u32[]{:S(2)}) collective-permute-start(bf16[32,1024]{1,0:T(8,128)(2,1)S(1)} %broadcast_select_fusion.refs_0_), channel_id=1, source_target_pairs={{0,8},{1,9},{2,10},{3,11},{4,12},{5,13},{6,14},{7,15},{8,0},{9,1},... | collective-permute-start | bytes 196616 | tf_op jit(solution)/shard_map/ppermute | solution.py:378
  57.0 7.4 %collective-permute-start.1 = (bf16[32,1024]{1,0:T(8,128)(2,1)S(1)}, bf16[32,1024]{1,0:T(8,128)(2,1)S(1)}, u32[]{:S(2)}, u32[]{:S(2)}) collective-permute-start(bf16[32,1024]{1,0:T(8,128)(2,1)S(1)} %broadcast_select_fusion.refs_0_), channel_id=1, source_target_pairs={{0,12},{1,13},{2,14},{3,15},{4,0},{5,1},{6,2},{7,3},{8,4},{9,5},{1... | collective-permute-start | bytes 196616 | tf_op jit(solution)/shard_map/ppermute | solution.py:378
  64.4 4.5 %collective-permute-start.4 = (bf16[16,128,128]{2,1,0:T(8,128)(2,1)S(1)}, bf16[16,128,128]{2,1,0:T(8,128)(2,1)S(1)}, u32[]{:S(2)}, u32[]{:S(2)}) collective-permute-start(bf16[16,128,128]{2,1,0:T(8,128)(2,1)S(1)} %shard_map.92), channel_id=1, source_target_pairs={{0,32},{1,33},{2,34},{3,35},{4,36},{5,37},{6,38},{7,39},{8,40},{9,... | collective-permute-start | bytes 1572872 | tf_op jit(solution)/shard_map/ppermute | solution.py:382
  72.0 50.4 %all-to-all-start.1 = ((bf16[16,64,128]{2,1,0:T(8,128)(2,1)}), bf16[16,64,128]{2,1,0:T(8,128)(2,1)S(1)}, u32[]{:S(2)}, u32[]{:S(2)}) async-start(bf16[16,64,128]{2,1,0:T(8,128)(2,1)} %shard_map.93.refs_4_), calls=%async_computation.1 | async-start | bytes 524288 | tf_op jit(solution)/shard_map/all_to_all | solution.py:388
  103.2 11.4 %collective-permute-start.7 = (bf16[4,32,1024]{2,1,0:T(8,128)(2,1)S(1)}, bf16[4,32,1024]{2,1,0:T(8,128)(2,1)S(1)}, u32[]{:S(2)}, u32[]{:S(2)}) collective-permute-start(bf16[4,32,1024]{2,1,0:T(8,128)(2,1)S(1)} %shard_map.94.refs_0_), channel_id=1, source_target_pairs={{0,1},{1,2},{2,3},{3,0},{4,5},{5,6},{6,7},{7,4},{8,9},{9,10},{10,1... | collective-permute-start | bytes 786440 | tf_op jit(solution)/shard_map/ppermute | solution.py:386
  105.1 11.9 %collective-permute-start.6 = (bf16[4,32,1024]{2,1,0:T(8,128)(2,1)S(1)}, bf16[4,32,1024]{2,1,0:T(8,128)(2,1)S(1)}, u32[]{:S(2)}, u32[]{:S(2)}) collective-permute-start(bf16[4,32,1024]{2,1,0:T(8,128)(2,1)S(1)} %shard_map.94.refs_0_), channel_id=1, source_target_pairs={{0,2},{1,3},{2,0},{3,1},{4,6},{5,7},{6,4},{7,5},{8,10},{9,11},{10,... | collective-permute-start | bytes 786440 | tf_op jit(solution)/shard_map/ppermute | solution.py:386
  110.6 8.3 %collective-permute-start.5 = (bf16[4,32,1024]{2,1,0:T(8,128)(2,1)S(1)}, bf16[4,32,1024]{2,1,0:T(8,128)(2,1)S(1)}, u32[]{:S(2)}, u32[]{:S(2)}) collective-permute-start(bf16[4,32,1024]{2,1,0:T(8,128)(2,1)S(1)} %shard_map.94.refs_0_), channel_id=1, source_target_pairs={{0,3},{1,0},{2,1},{3,2},{4,7},{5,4},{6,5},{7,6},{8,11},{9,8},{10,9... | collective-permute-start | bytes 786440 | tf_op jit(solution)/shard_map/ppermute | solution.py:386
  112.6 8.8 %collective-permute-start.8 = (bf16[4,32,1024]{2,1,0:T(8,128)(2,1)S(1)}, bf16[4,32,1024]{2,1,0:T(8,128)(2,1)S(1)}, u32[]{:S(2)}, u32[]{:S(2)}) collective-permute-start(bf16[4,32,1024]{2,1,0:T(8,128)(2,1)S(1)} %shard_map.94.refs_0_), channel_id=1, source_target_pairs={{0,32},{1,33},{2,34},{3,35},{4,36},{5,37},{6,38},{7,39},{8,40},{9,... | collective-permute-start | bytes 786440 | tf_op jit(solution)/shard_map/ppermute | solution.py:387
  114.5 6.9 %collective-permute-start.11 = (bf16[4,32,1024]{2,1,0:T(8,128)(2,1)S(1)}, bf16[4,32,1024]{2,1,0:T(8,128)(2,1)S(1)}, u32[]{:S(2)}, u32[]{:S(2)}) collective-permute-start(bf16[4,32,1024]{2,1,0:T(8,128)(2,1)S(1)} %collective-permute-done.7.refs_3_), channel_id=1, source_target_pairs={{0,32},{1,33},{2,34},{3,35},{4,36},{5,37},{6,38},{7,39},{8,40},{9,... | collective-permute-start | bytes 786440 | tf_op jit(solution)/shard_map/ppermute | solution.py:387
  117.0 4.5 %collective-permute-start.10 = (bf16[4,32,1024]{2,1,0:T(8,128)(2,1)S(1)}, bf16[4,32,1024]{2,1,0:T(8,128)(2,1)S(1)}, u32[]{:S(2)}, u32[]{:S(2)}) collective-permute-start(bf16[4,32,1024]{2,1,0:T(8,128)(2,1)S(1)} %collective-permute-done.6.refs_2_), channel_id=1, source_target_pairs={{0,32},{1,33},{2,34},{3,35},{4,36},{5,37},{6,38},{7,39},{8,40},{9,... | collective-permute-start | bytes 786440 | tf_op jit(solution)/shard_map/ppermute | solution.py:387
  118.9 3.6 %collective-permute-start.9 = (bf16[4,32,1024]{2,1,0:T(8,128)(2,1)S(1)}, bf16[4,32,1024]{2,1,0:T(8,128)(2,1)S(1)}, u32[]{:S(2)}, u32[]{:S(2)}) collective-permute-start(bf16[4,32,1024]{2,1,0:T(8,128)(2,1)S(1)} %collective-permute-done.5.refs_1_), channel_id=1, source_target_pairs={{0,32},{1,33},{2,34},{3,35},{4,36},{5,37},{6,38},{7,39},{8,40},{9,... | collective-permute-start | bytes 786440 | tf_op jit(solution)/shard_map/ppermute | solution.py:387
  125.3 0.7 copy-start.1
  126.1 22.4 %all-to-all-start.2 = ((bf16[32,16,1024]{2,1,0:T(8,128)(2,1)}), bf16[32,16,1024]{2,1,0:T(8,128)(2,1)S(1)}, u32[]{:S(2)}, u32[]{:S(2)}) async-start(bf16[32,16,1024]{2,1,0:T(8,128)(2,1)} %bitcast.5), calls=%async_computation.2 | async-start | bytes 2097152 | tf_op jit(solution)/shard_map/all_to_all | solution.py:395
  132.9 12.0 %copy-start = (bf16[2304,1024]{1,0:T(8,128)(2,1)S(1)}, bf16[2304,1024]{1,0:T(8,128)(2,1)}, u32[]{:S(2)}) copy-start(bf16[2304,1024]{1,0:T(8,128)(2,1)} %all-gather.3.cloned.1.call-done) | copy-start | bytes 14155780
  136.2 12.3 %collective-permute-start.12 = (bf16[2,144,1024]{2,1,0:T(8,128)(2,1)}, bf16[2,144,1024]{2,1,0:T(8,128)(2,1)}, u32[]{:S(2)}, u32[]{:S(2)}) collective-permute-start(bf16[2,144,1024]{2,1,0:T(8,128)(2,1)} %get-tuple-element.15), channel_id=1, source_target_pairs={{0,32},{1,33},{2,34},{3,35},{4,36},{5,37},{6,38},{7,39},{8,40},{9,... | collective-permute-start | bytes 1769480 | tf_op jit(solution)/shard_map/ppermute | solution.py:399
  138.3 10.2 %collective-permute-start.13 = (bf16[2,144,1024]{2,1,0:T(8,128)(2,1)}, bf16[2,144,1024]{2,1,0:T(8,128)(2,1)}, u32[]{:S(2)}, u32[]{:S(2)}) collective-permute-start(bf16[2,144,1024]{2,1,0:T(8,128)(2,1)} %get-tuple-element.16), channel_id=1, source_target_pairs={{0,32},{1,33},{2,34},{3,35},{4,36},{5,37},{6,38},{7,39},{8,40},{9,... | collective-permute-start | bytes 1769480 | tf_op jit(solution)/shard_map/ppermute | solution.py:399
  140.6 7.9 %collective-permute-start.14 = (bf16[2,144,1024]{2,1,0:T(8,128)(2,1)}, bf16[2,144,1024]{2,1,0:T(8,128)(2,1)}, u32[]{:S(2)}, u32[]{:S(2)}) collective-permute-start(bf16[2,144,1024]{2,1,0:T(8,128)(2,1)} %get-tuple-element.17), channel_id=1, source_target_pairs={{0,32},{1,33},{2,34},{3,35},{4,36},{5,37},{6,38},{7,39},{8,40},{9,... | collective-permute-start | bytes 1769480 | tf_op jit(solution)/shard_map/ppermute | solution.py:399
  142.7 5.8 %collective-permute-start.15 = (bf16[2,144,1024]{2,1,0:T(8,128)(2,1)}, bf16[2,144,1024]{2,1,0:T(8,128)(2,1)}, u32[]{:S(2)}, u32[]{:S(2)}) collective-permute-start(bf16[2,144,1024]{2,1,0:T(8,128)(2,1)} %get-tuple-element.18), channel_id=1, source_target_pairs={{0,32},{1,33},{2,34},{3,35},{4,36},{5,37},{6,38},{7,39},{8,40},{9,... | collective-permute-start | bytes 1769480 | tf_op jit(solution)/shard_map/ppermute | solution.py:399
  148.5 25.6 %copy-start.2 = (bf16[128,1024]{1,0:T(8,128)(2,1)S(1)}, bf16[128,1024]{1,0:T(8,128)(2,1)}, u32[]{:S(2)}) copy-start(bf16[128,1024]{1,0:T(8,128)(2,1)} %copy-done.1) | copy-start | bytes 786436
Sparse Core Ops, SparseCore 0:
  9.4 120.3 all-gather.2

commit v5 on v3

--- a/solution.py
+++ b/solution.py
@@ -11,7 +11,7 @@
 HEAD_DIM = 128
 TOP = 2
 SLOT = 16
-PART = 2
+PARTS = (3, 3, 2)
 NEG_FILL = -1e30
 LOG2E = 1.4426950408889634
 BF = jnp.bfloat16
@@ -114,6 +114,7 @@
         out_specs=VMEM,
         scratch_shapes=[pltpu.VMEM((3,) + q.shape[1:], BF), pltpu.SemaphoreType.DMA((3,))],
         compiler_params=params(56),
+        cost_estimate=pl.CostEstimate(flops=0, bytes_accessed=20 << 20, transcendentals=0),
     )(q, k, v, after)
 
 
@@ -256,46 +257,42 @@
     )(where, ctx, *own, *oth, residual, router.T, ids[0].T)
 
 
-def pick_kernel(core_ref, weights_ref, after_ref, *refs):
+def pick_kernel(flip, core_ref, weights_ref, after_ref, *refs):
     sems = refs[-1]
     core = core_ref[0]
-    copies = [
-        pltpu.make_async_copy(
-            weights_ref.at[pl.ds((1 - core) * 8 + n * PART, PART)], ref, sems.at[n]
+    first = ((1 - core) if flip else core) * 8
+    copies = []
+    for n, ref in enumerate(refs[:-1]):
+        copies.append(
+            pltpu.make_async_copy(weights_ref.at[pl.ds(first, ref.shape[0])], ref, sems.at[n])
         )
-        for n, ref in enumerate(refs[:-2])
-    ]
-    copies.append(
-        pltpu.make_async_copy(weights_ref.at[pl.ds(core * 8, 8)], refs[-2], sems.at[8 // PART])
-    )
+        first = first + ref.shape[0]
     for copy in copies:
         copy.start()
     for copy in copies:
         copy.wait()
 
 
-def pick(core, weights, after):
-    parts = 8 // PART
-    one = weights.shape[1:]
-    return pl.pallas_call(
-        pick_kernel,
-        out_shape=(jax.ShapeDtypeStruct((PART,) + one, BF),) * parts
-        + (jax.ShapeDtypeStruct((8,) + one, BF),),
+def pick(core, weights, after, flip, parts):
+    return pl.pallas_call(
+        functools.partial(pick_kernel, flip),
+        out_shape=tuple(jax.ShapeDtypeStruct((n,) + weights.shape[1:], BF) for n in parts),
         in_specs=[SMEM, HBM, ANY],
-        out_specs=(VMEM,) * (parts + 1),
-        scratch_shapes=[pltpu.SemaphoreType.DMA((parts + 1,))],
-        compiler_params=params(52),
+        out_specs=(VMEM,) * len(parts),
+        scratch_shapes=[pltpu.SemaphoreType.DMA((len(parts),))],
+        compiler_params=params(52 if flip else 40),
         cost_estimate=pl.CostEstimate(flops=0, bytes_accessed=8 << 20, transcendentals=0),
     )(core, weights, after)
 
 
 def expert_kernel(core_ref, x_ref, own_ref, *refs):
-    oth_refs, (out_ref, up, down) = refs[: 8 // PART], refs[8 // PART :]
+    oth_refs, (out_ref, up, down) = refs[: len(PARTS)], refs[len(PARTS) :]
     core = core_ref[0]
     pieces = [(own_ref, slice(0, 8), core)]
-    pieces += [
-        (ref, slice(n * PART, (n + 1) * PART), 1 - core) for n, ref in enumerate(oth_refs)
-    ]
+    first = 0
+    for ref in oth_refs:
+        pieces.append((ref, slice(first, first + ref.shape[0]), 1 - core))
+        first += ref.shape[0]
     for source, z, place in pieces:
         up[z, place, :, 0:1024] = source[:, 0:64, :]
         up[z, place, 0:32, 1024:1536] = source[:, 64:96, 0:512]
@@ -369,8 +366,7 @@
 
     heads = pack_heads(query_rows, key_rows, value_rows, moved)
     heads = lax.all_to_all(heads, ("zlo", "core"), split_axis=0, concat_axis=0, tiled=True)
-    keys = keys_of(heads, proj_own)
-    oth_keys = lax.ppermute(keys, ALL, CORE_SWAP)
+    oth_keys = lax.ppermute(keys_of(heads, proj_own), ALL, CORE_SWAP)
     proj_oth = [lax.ppermute(p, ALL, CORE_SWAP) for p in proj_own]
     context = attention(core, heads, oth_keys)
     context = lax.all_to_all(context, ("zlo", "core"), split_axis=0, concat_axis=0, tiled=True)
@@ -383,8 +379,9 @@
     arrived = lax.all_to_all(
         outgoing.reshape(32, SLOT, 1024), ("core", "xy"), split_axis=0, concat_axis=0, tiled=True
     )
-    *to_send, own_weights = pick(core, weights, target)
+    to_send = pick(core, weights, target, True, PARTS)
     oth_weights = [lax.ppermute(w, ALL, CORE_SWAP) for w in to_send]
+    (own_weights,) = pick(core, weights, target, False, (8,))
     produced = experts(core, arrived.reshape(32 * SLOT, 1024), own_weights, oth_weights)
     back = lax.all_to_all(
         produced.reshape(32, SLOT, 1024), ("core", "xy"), split_axis=0, concat_axis=0, tiled=True

time: 191 us -> 186 us (0.974)
  starting transfers between devices: 83.9 us -> 81.6 us
    ppermute x4 -> x3, starting transfers between devices: 8.65 us -> 6.25 us  [on_device(): oth_weights = [lax.ppermute(w, ALL, CORE_SWAP) for w in to_send]]
    pallas_call x1 -> x2, Pallas kernels: 4.45 us -> 3.44 us  [pick(): pl.pallas_call(functools.partial(pick_kernel, flip), out_shape=tuple((jax...]
  transfers between devices with their start and end apart: 20 -> 19, of which waited for: 11 -> 11; matrix products, arithmetic and copies ran while one was open for 1% -> 1% of each run, Pallas kernels for 7% -> 6%
where the time goes in v5:
time: 186 us; the launch traced here: 183 us
  starting transfers between devices  81.6 us (44%)
  waiting for transfers between devices  43.5 us (23%)
  blocking collectives  23.1 us (12%)
  Pallas kernels  19.1 us (10%)
  between operations  13.7 us (7%)
    all_to_all x1, blocking collectives, on_device(): lax.all_to_all(produced.reshape(32, SLOT, 1024), ('core', 'xy'), split_ax...  23.1 us
    ppermute x1, starting transfers between devices, on_device(): moved = lax.ppermute(out_proj, ALL, HALF_MOVE)  15.9 us
    all_to_all x1, starting transfers between devices, on_device(): lax.all_to_all(context, ('zlo', 'core'), split_axis=0, concat_axis=0, til...  12.6 us
    ppermute x3, starting transfers between devices, on_device(): lax.ppermute(line, ALL, plane_pairs(1, d))  11.5 us
    all_to_all x1, waiting for transfers between devices, on_device(): lax.all_to_all(context, ('zlo', 'core'), split_axis=0, concat_axis=0, til...  9.35 us
    all_gather x1, waiting for transfers between devices, on_device(): weights = lax.all_gather(packed, ('zhi', 'zlo'), axis=0, tiled=False)  9.28 us
    ppermute x4, starting transfers between devices, on_device(): proj_oth = [lax.ppermute(p, ALL, CORE_SWAP) for p in proj_own]  8.65 us
    ppermute x3, starting transfers between devices, on_device(): lax.ppermute(shard, ALL, plane_pairs(0, d))  8.63 us
  transfers between devices with their start and end apart: 19, of which 11 were waited for; matrix products, arithmetic and copies ran while one was open for 1% of the time, Pallas kernels for 6%

profile of v5, /device:TPU:6, one launch (start us, length us, event | category | flops | bytes accessed | tf_op | source)
XLA Modules:
  0.0 183.3 jit_solution(245499944231390328)
XLA Ops:
  6.5 1.7 shard_map.95
  8.3 0.0 all-gather.3.cloned.1.call-update
  8.3 0.0 copy-start.3
  8.3 0.0 copy-start.4
  8.3 0.0 copy-start.5
  8.4 15.9 %collective-permute-start = (bf16[32,1024]{1,0:T(8,128)(2,1)}, bf16[32,1024]{1,0:T(8,128)(2,1)S(1)}, u32[]{:S(2)}, u32[]{:S(2)}) collective-permute-start(bf16[32,1024]{1,0:T(8,128)(2,1)} %param.13), channel_id=1, source_target_pairs={{0,16},{1,17},{2,18},{3,19},{4,20},{5,21},{6,22},{7,23},{8,24},{9,... | collective-permute-start | bytes 196616 | tf_op jit(solution)/shard_map/ppermute | solution.py:362
  24.2 2.2 %collective-permute-done.after_ref = bf16[32,1024]{1,0:T(8,128)(2,1)S(1)} collective-permute-done((bf16[32,1024]{1,0:T(8,128)(2,1)}, bf16[32,1024]{1,0:T(8,128)(2,1)S(1)}, u32[]{:S(2)}, u32[]{:S(2)}) %collective-permute-start) | collective-permute-done | bytes 65568 | tf_op jit(solution)/shard_map/ppermute | solution.py:362
  26.4 0.6 copy-done.6
  27.0 2.1 %shard_map.91 = bf16[16,192,128]{2,1,0:T(8,128)(2,1)} custom-call(bf16[1,128,1024]{2,1,0:T(8,128)(2,1)} %q_ref.1, bf16[1,128,1024]{2,1,0:T(8,128)(2,1)} %k_ref.1, bf16[1,128,1024]{2,1,0:T(8,128)(2,1)} %v_ref.1, bf16[32,1024]{1,0:T(8,128)(2,1)} %copy-done.6), custom_call_target="tpu_custom_call" | custom-call | bytes 20971520 | tf_op jit(solution)/shard_map/pallas_call | solution.py:110
  29.1 8.1 %all-to-all-start = ((bf16[16,192,128]{2,1,0:T(8,128)(2,1)}), bf16[16,192,128]{2,1,0:T(8,128)(2,1)S(1)}, u32[]{:S(2)}, u32[]{:S(2)}) async-start(bf16[16,192,128]{2,1,0:T(8,128)(2,1)} %shard_map.91), calls=%async_computation | async-start | bytes 1572864 | tf_op jit(solution)/shard_map/all_to_all | solution.py:368
  37.2 0.9 broadcast_select_fusion
  38.1 2.4 %collective-permute-start.3 = (bf16[32,1024]{1,0:T(8,128)(2,1)S(1)}, bf16[32,1024]{1,0:T(8,128)(2,1)S(1)}, u32[]{:S(2)}, u32[]{:S(2)}) collective-permute-start(bf16[32,1024]{1,0:T(8,128)(2,1)S(1)} %broadcast_select_fusion), channel_id=1, source_target_pairs={{0,4},{1,5},{2,6},{3,7},{4,8},{5,9},{6,10},{7,11},{8,12},{9,13},{1... | collective-permute-start | bytes 196616 | tf_op jit(solution)/shard_map/ppermute | solution.py:364
  40.5 4.3 %collective-permute-start.2 = (bf16[32,1024]{1,0:T(8,128)(2,1)S(1)}, bf16[32,1024]{1,0:T(8,128)(2,1)S(1)}, u32[]{:S(2)}, u32[]{:S(2)}) collective-permute-start(bf16[32,1024]{1,0:T(8,128)(2,1)S(1)} %broadcast_select_fusion), channel_id=1, source_target_pairs={{0,8},{1,9},{2,10},{3,11},{4,12},{5,13},{6,14},{7,15},{8,0},{9,1},... | collective-permute-start | bytes 196616 | tf_op jit(solution)/shard_map/ppermute | solution.py:364
  44.8 1.9 %collective-permute-start.1 = (bf16[32,1024]{1,0:T(8,128)(2,1)S(1)}, bf16[32,1024]{1,0:T(8,128)(2,1)S(1)}, u32[]{:S(2)}, u32[]{:S(2)}) collective-permute-start(bf16[32,1024]{1,0:T(8,128)(2,1)S(1)} %broadcast_select_fusion), channel_id=1, source_target_pairs={{0,12},{1,13},{2,14},{3,15},{4,0},{5,1},{6,2},{7,3},{8,4},{9,5},{1... | collective-permute-start | bytes 196616 | tf_op jit(solution)/shard_map/ppermute | solution.py:364
  46.8 1.4 collective-permute-done.2
  48.2 4.0 %collective-permute-done.1 = bf16[32,1024]{1,0:T(8,128)(2,1)S(1)} collective-permute-done((bf16[32,1024]{1,0:T(8,128)(2,1)S(1)}, bf16[32,1024]{1,0:T(8,128)(2,1)S(1)}, u32[]{:S(2)}, u32[]{:S(2)}) %collective-permute-start.1) | collective-permute-done | bytes 65568 | tf_op jit(solution)/shard_map/ppermute | solution.py:364
  52.2 3.5 %collective-permute-start.6 = (bf16[4,32,1024]{2,1,0:T(8,128)(2,1)S(1)}, bf16[4,32,1024]{2,1,0:T(8,128)(2,1)S(1)}, u32[]{:S(2)}, u32[]{:S(2)}) collective-permute-start(bf16[4,32,1024]{2,1,0:T(8,128)(2,1)S(1)} %pad_maximum_fusion.refs_0_), channel_id=1, source_target_pairs={{0,1},{1,2},{2,3},{3,0},{4,5},{5,6},{6,7},{7,4},{8,9},{9,10},{10,1... | collective-permute-start | bytes 786440 | tf_op jit(solution)/shard_map/ppermute | solution.py:365
  55.7 4.8 %collective-permute-start.5 = (bf16[4,32,1024]{2,1,0:T(8,128)(2,1)S(1)}, bf16[4,32,1024]{2,1,0:T(8,128)(2,1)S(1)}, u32[]{:S(2)}, u32[]{:S(2)}) collective-permute-start(bf16[4,32,1024]{2,1,0:T(8,128)(2,1)S(1)} %pad_maximum_fusion.refs_0_), channel_id=1, source_target_pairs={{0,2},{1,3},{2,0},{3,1},{4,6},{5,7},{6,4},{7,5},{8,10},{9,11},{10,... | collective-permute-start | bytes 786440 | tf_op jit(solution)/shard_map/ppermute | solution.py:365
  60.6 3.3 %collective-permute-start.4 = (bf16[4,32,1024]{2,1,0:T(8,128)(2,1)S(1)}, bf16[4,32,1024]{2,1,0:T(8,128)(2,1)S(1)}, u32[]{:S(2)}, u32[]{:S(2)}) collective-permute-start(bf16[4,32,1024]{2,1,0:T(8,128)(2,1)S(1)} %pad_maximum_fusion.refs_0_), channel_id=1, source_target_pairs={{0,3},{1,0},{2,1},{3,2},{4,7},{5,4},{6,5},{7,6},{8,11},{9,8},{10,9... | collective-permute-start | bytes 786440 | tf_op jit(solution)/shard_map/ppermute | solution.py:365
  63.8 0.0 collective-permute-done.6.refs_3_
  63.8 1.9 %collective-permute-done.5.refs_2_ = bf16[4,32,1024]{2,1,0:T(8,128)(2,1)S(1)} collective-permute-done((bf16[4,32,1024]{2,1,0:T(8,128)(2,1)S(1)}, bf16[4,32,1024]{2,1,0:T(8,128)(2,1)S(1)}, u32[]{:S(2)}, u32[]{:S(2)}) %collective-permute-start.5) | collective-permute-done | bytes 262176 | tf_op jit(solution)/shard_map/ppermute | solution.py:365
  65.8 3.0 %collective-permute-done.4.refs_1_ = bf16[4,32,1024]{2,1,0:T(8,128)(2,1)S(1)} collective-permute-done((bf16[4,32,1024]{2,1,0:T(8,128)(2,1)S(1)}, bf16[4,32,1024]{2,1,0:T(8,128)(2,1)S(1)}, u32[]{:S(2)}, u32[]{:S(2)}) %collective-permute-start.4) | collective-permute-done | bytes 262176 | tf_op jit(solution)/shard_map/ppermute | solution.py:365
  68.8 7.3 %all-to-all-done.heads_ref.own_ref = bf16[16,192,128]{2,1,0:T(8,128)(2,1)S(1)} async-done(((bf16[16,192,128]{2,1,0:T(8,128)(2,1)}), bf16[16,192,128]{2,1,0:T(8,128)(2,1)S(1)}, u32[]{:S(2)}, u32[]{:S(2)}) %all-to-all-start) | async-done | bytes 786464 | tf_op jit(solution)/shard_map/all_to_all | solution.py:368
  76.2 2.7 %collective-permute-start.7 = (bf16[16,128,128]{2,1,0:T(8,128)(2,1)S(1)}, bf16[16,128,128]{2,1,0:T(8,128)(2,1)S(1)}, u32[]{:S(2)}, u32[]{:S(2)}) collective-permute-start(bf16[16,128,128]{2,1,0:T(8,128)(2,1)S(1)} %shard_map.92), channel_id=1, source_target_pairs={{0,32},{1,33},{2,34},{3,35},{4,36},{5,37},{6,38},{7,39},{8,40},{9,... | collective-permute-start | bytes 1572872 | tf_op jit(solution)/shard_map/ppermute | solution.py:369
  78.9 1.5 collective-permute-done.7.oth_ref
  80.4 3.2 %shard_map.93 = bf16[16,64,128]{2,1,0:T(8,128)(2,1)} custom-call(s32[1]{0:T(128)} %bitcast.core_ref, bf16[16,192,128]{2,1,0:T(8,128)(2,1)S(1)} %all-to-all-done.heads_ref.own_ref, bf16[16,128,128]{2,1,0:T(8,128)(2,1)S(1)} %collective-permute-done.7.oth_ref), custom_call_target="tpu_custom_call" | custom-call | flops 671088640 | bytes 2097152 | tf_op jit(solution)/shard_map/pallas_call | solution.py:175
  83.6 12.6 %all-to-all-start.1 = ((bf16[16,64,128]{2,1,0:T(8,128)(2,1)}), bf16[16,64,128]{2,1,0:T(8,128)(2,1)S(1)}, u32[]{:S(2)}, u32[]{:S(2)}) async-start(bf16[16,64,128]{2,1,0:T(8,128)(2,1)} %shard_map.93), calls=%async_computation.1 | async-start | bytes 524288 | tf_op jit(solution)/shard_map/all_to_all | solution.py:372
  96.2 2.3 %collective-permute-start.8 = (bf16[4,32,1024]{2,1,0:T(8,128)(2,1)S(1)}, bf16[4,32,1024]{2,1,0:T(8,128)(2,1)S(1)}, u32[]{:S(2)}, u32[]{:S(2)}) collective-permute-start(bf16[4,32,1024]{2,1,0:T(8,128)(2,1)S(1)} %pad_maximum_fusion.refs_0_), channel_id=1, source_target_pairs={{0,32},{1,33},{2,34},{3,35},{4,36},{5,37},{6,38},{7,39},{8,40},{9,... | collective-permute-start | bytes 786440 | tf_op jit(solution)/shard_map/ppermute | solution.py:370
  98.5 2.0 %collective-permute-start.11 = (bf16[4,32,1024]{2,1,0:T(8,128)(2,1)S(1)}, bf16[4,32,1024]{2,1,0:T(8,128)(2,1)S(1)}, u32[]{:S(2)}, u32[]{:S(2)}) collective-permute-start(bf16[4,32,1024]{2,1,0:T(8,128)(2,1)S(1)} %collective-permute-done.6.refs_3_), channel_id=1, source_target_pairs={{0,32},{1,33},{2,34},{3,35},{4,36},{5,37},{6,38},{7,39},{8,40},{9,... | collective-permute-start | bytes 786440 | tf_op jit(solution)/shard_map/ppermute | solution.py:370
  100.5 2.3 %collective-permute-start.10 = (bf16[4,32,1024]{2,1,0:T(8,128)(2,1)S(1)}, bf16[4,32,1024]{2,1,0:T(8,128)(2,1)S(1)}, u32[]{:S(2)}, u32[]{:S(2)}) collective-permute-start(bf16[4,32,1024]{2,1,0:T(8,128)(2,1)S(1)} %collective-permute-done.5.refs_2_), channel_id=1, source_target_pairs={{0,32},{1,33},{2,34},{3,35},{4,36},{5,37},{6,38},{7,39},{8,40},{9,... | collective-permute-start | bytes 786440 | tf_op jit(solution)/shard_map/ppermute | solution.py:370
  102.9 2.0 %collective-permute-start.9 = (bf16[4,32,1024]{2,1,0:T(8,128)(2,1)S(1)}, bf16[4,32,1024]{2,1,0:T(8,128)(2,1)S(1)}, u32[]{:S(2)}, u32[]{:S(2)}) collective-permute-start(bf16[4,32,1024]{2,1,0:T(8,128)(2,1)S(1)} %collective-permute-done.4.refs_1_), channel_id=1, source_target_pairs={{0,32},{1,33},{2,34},{3,35},{4,36},{5,37},{6,38},{7,39},{8,40},{9,... | collective-permute-start | bytes 786440 | tf_op jit(solution)/shard_map/ppermute | solution.py:370
  104.9 0.1 pad_add_fusion.where_ref
  105.0 0.0 collective-permute-done.8.refs_4_
  105.0 1.3 collective-permute-done.9.refs_5_
  106.3 9.3 %all-to-all-done.1.ctx_ref = bf16[16,64,128]{2,1,0:T(8,128)(2,1)S(1)} async-done(((bf16[16,64,128]{2,1,0:T(8,128)(2,1)}), bf16[16,64,128]{2,1,0:T(8,128)(2,1)S(1)}, u32[]{:S(2)}, u32[]{:S(2)}) %all-to-all-start.1) | async-done | bytes 262176 | tf_op jit(solution)/shard_map/all_to_all | solution.py:372
  115.6 2.9 %shard_map.94 = (bf16[128,1024]{1,0:T(8,128)(2,1)S(1)}, bf16[512,1024]{1,0:T(8,128)(2,1)}, f32[2,128]{1,0:T(2,128)S(1)}, s32[2,128]{1,0:T(2,128)S(1)}) custom-call(s32[3]{0:T(128)S(1)} %pad_add_fusion.where_ref, bf16[16,64,128]{2,1,0:T(8,128)(2,1)S(1)} %all-to-all-done.1.ctx_ref, bf16[4,32,1024]{2,1,0:T(8,128)(2,1)S(1)} %pad_maximum_fusion.refs_0_, ...), custom_call_target="tpu_custom_call" | custom-call | flops 419430400 | bytes 4194304 | tf_op jit(solution)/shard_map/pallas_call | solution.py:239
  118.5 0.7 copy-done.1
  119.2 7.3 %all-to-all-start.2 = ((bf16[32,16,1024]{2,1,0:T(8,128)(2,1)}), bf16[32,16,1024]{2,1,0:T(8,128)(2,1)S(1)}, u32[]{:S(2)}, u32[]{:S(2)}) async-start(bf16[32,16,1024]{2,1,0:T(8,128)(2,1)} %bitcast.9), calls=%async_computation.2 | async-start | bytes 2097152 | tf_op jit(solution)/shard_map/all_to_all | solution.py:379
  126.5 9.3 %all-gather.3.cloned.1.call-done = bf16[2304,1024]{1,0:T(8,128)(2,1)} async-done(((bf16[144,1024]{1,0:T(8,128)(2,1)}), bf16[2304,1024]{1,0:T(8,128)(2,1)}) %all-gather.3.cloned.1.call-update) | async-done | bytes 4718608 | tf_op jit(solution)/shard_map/all_gather | solution.py:360
  135.8 3.3 %shard_map.97 = (bf16[3,144,1024]{2,1,0:T(8,128)(2,1)}, bf16[3,144,1024]{2,1,0:T(8,128)(2,1)}, bf16[2,144,1024]{2,1,0:T(8,128)(2,1)}) custom-call(s32[1]{0:T(128)} %bitcast.core_ref, bf16[16,144,1024]{2,1,0:T(8,128)(2,1)} %bitcast.15, s32[2,128]{1,0:T(2,128)S(1)} %get-tuple-element.13.after_ref.target_ref), custom_call_target="tpu_custom_call" | custom-call | bytes 8388608 | tf_op jit(solution)/shard_map/pallas_call | solution.py:277
  139.0 1.9 %collective-permute-start.12 = (bf16[3,144,1024]{2,1,0:T(8,128)(2,1)}, bf16[3,144,1024]{2,1,0:T(8,128)(2,1)}, u32[]{:S(2)}, u32[]{:S(2)}) collective-permute-start(bf16[3,144,1024]{2,1,0:T(8,128)(2,1)} %get-tuple-element.14), channel_id=1, source_target_pairs={{0,32},{1,33},{2,34},{3,35},{4,36},{5,37},{6,38},{7,39},{8,40},{9,... | collective-permute-start | bytes 2654216 | tf_op jit(solution)/shard_map/ppermute | solution.py:383
  141.0 2.4 %collective-permute-start.13 = (bf16[3,144,1024]{2,1,0:T(8,128)(2,1)}, bf16[3,144,1024]{2,1,0:T(8,128)(2,1)}, u32[]{:S(2)}, u32[]{:S(2)}) collective-permute-start(bf16[3,144,1024]{2,1,0:T(8,128)(2,1)} %get-tuple-element.15), channel_id=1, source_target_pairs={{0,32},{1,33},{2,34},{3,35},{4,36},{5,37},{6,38},{7,39},{8,40},{9,... | collective-permute-start | bytes 2654216 | tf_op jit(solution)/shard_map/ppermute | solution.py:383
  143.4 1.9 %collective-permute-start.14 = (bf16[2,144,1024]{2,1,0:T(8,128)(2,1)}, bf16[2,144,1024]{2,1,0:T(8,128)(2,1)}, u32[]{:S(2)}, u32[]{:S(2)}) collective-permute-start(bf16[2,144,1024]{2,1,0:T(8,128)(2,1)} %get-tuple-element.16), channel_id=1, source_target_pairs={{0,32},{1,33},{2,34},{3,35},{4,36},{5,37},{6,38},{7,39},{8,40},{9,... | collective-permute-start | bytes 1769480 | tf_op jit(solution)/shard_map/ppermute | solution.py:383
  145.3 0.2 shard_map.96.own_ref
  145.5 2.1 %collective-permute-done.14.refs_2_ = bf16[2,144,1024]{2,1,0:T(8,128)(2,1)} collective-permute-done((bf16[2,144,1024]{2,1,0:T(8,128)(2,1)}, bf16[2,144,1024]{2,1,0:T(8,128)(2,1)}, u32[]{:S(2)}, u32[]{:S(2)}) %collective-permute-start.14) | collective-permute-done | bytes 589856 | tf_op jit(solution)/shard_map/ppermute | solution.py:383
  147.6 4.5 %shard_map.98 = bf16[512,1024]{1,0:T(8,128)(2,1)S(1)} custom-call(s32[1]{0:T(128)} %bitcast.core_ref, bf16[512,1024]{1,0:T(8,128)(2,1)S(1)} %bitcast.18, bf16[8,144,1024]{2,1,0:T(8,128)(2,1)S(1)} %shard_map.96.own_ref, bf16[3,144,1024]{2,1,0:T(8,128)(2,1)} %collective-permute-done.12.refs_0_, bf16[3,144,1024]{2,1,0:T(8,128)(2,1)} %collective-permute-done.13.refs_1_, ...), custom_call_target="tpu_custom_call" | custom-call | flops 2415919104 | bytes 7340032 | tf_op jit(solution)/shard_map/pallas_call | solution.py:311
  152.1 23.1 %all_to_all.20 = bf16[32,16,1024]{2,1,0:T(8,128)(2,1)S(1)} all-to-all(bf16[32,16,1024]{2,1,0:T(8,128)(2,1)S(1)} %bitcast.19), channel_id=1, replica_groups=mesh['zlo'=8,'core'=2,'zhi'=2,'xy'=16] {'core','xy'}, dimensions={0} | all-to-all | bytes 2097152 | tf_op jit(solution)/shard_map/all_to_all | solution.py:386
  175.2 1.2 shard_map.99
  (18 shorter events, 0.1 us)
Async XLA Ops:
  6.5 129.2 %all-gather.3.cloned.1.call-start = ((), (), s32[]{:S(2)}) async-start(), calls=%async_computation.4 | async-start | bytes 5013504 | tf_op jit(solution)/shard_map/all_gather | solution.py:360
  8.3 107.3 %copy-start.3 = (bf16[1,128,1024]{2,1,0:T(8,128)(2,1)S(1)}, bf16[1,128,1024]{2,1,0:T(8,128)(2,1)}, u32[]{:S(2)}) copy-start(bf16[1,128,1024]{2,1,0:T(8,128)(2,1)} %refs_8_.1) | copy-start | bytes 786436
  8.3 107.3 %copy-start.4 = (bf16[1024,32]{0,1:T(8,128)(2,1)S(1)}, bf16[1024,32]{0,1:T(8,128)(2,1)}, u32[]{:S(2)}) copy-start(bf16[1024,32]{0,1:T(8,128)(2,1)} %param.14) | copy-start | bytes 196612
  8.3 107.3 %copy-start.5 = (s32[1,128,2]{1,2,0:T(2,128)S(1)}, s32[1,128,2]{1,2,0:T(2,128)}, u32[]{:S(2)}) copy-start(s32[1,128,2]{1,2,0:T(2,128)} %param.15) | copy-start | bytes 3076
  8.4 18.1 %collective-permute-start = (bf16[32,1024]{1,0:T(8,128)(2,1)}, bf16[32,1024]{1,0:T(8,128)(2,1)S(1)}, u32[]{:S(2)}, u32[]{:S(2)}) collective-permute-start(bf16[32,1024]{1,0:T(8,128)(2,1)} %param.13), channel_id=1, source_target_pairs={{0,16},{1,17},{2,18},{3,19},{4,20},{5,21},{6,22},{7,23},{8,24},{9,... | collective-permute-start | bytes 196616 | tf_op jit(solution)/shard_map/ppermute | solution.py:362
  26.4 0.6 copy-start.6
  29.1 47.0 %all-to-all-start = ((bf16[16,192,128]{2,1,0:T(8,128)(2,1)}), bf16[16,192,128]{2,1,0:T(8,128)(2,1)S(1)}, u32[]{:S(2)}, u32[]{:S(2)}) async-start(bf16[16,192,128]{2,1,0:T(8,128)(2,1)} %shard_map.91), calls=%async_computation | async-start | bytes 1572864 | tf_op jit(solution)/shard_map/all_to_all | solution.py:368
  38.1 8.7 %collective-permute-start.3 = (bf16[32,1024]{1,0:T(8,128)(2,1)S(1)}, bf16[32,1024]{1,0:T(8,128)(2,1)S(1)}, u32[]{:S(2)}, u32[]{:S(2)}) collective-permute-start(bf16[32,1024]{1,0:T(8,128)(2,1)S(1)} %broadcast_select_fusion), channel_id=1, source_target_pairs={{0,4},{1,5},{2,6},{3,7},{4,8},{5,9},{6,10},{7,11},{8,12},{9,13},{1... | collective-permute-start | bytes 196616 | tf_op jit(solution)/shard_map/ppermute | solution.py:364
  40.5 7.7 %collective-permute-start.2 = (bf16[32,1024]{1,0:T(8,128)(2,1)S(1)}, bf16[32,1024]{1,0:T(8,128)(2,1)S(1)}, u32[]{:S(2)}, u32[]{:S(2)}) collective-permute-start(bf16[32,1024]{1,0:T(8,128)(2,1)S(1)} %broadcast_select_fusion), channel_id=1, source_target_pairs={{0,8},{1,9},{2,10},{3,11},{4,12},{5,13},{6,14},{7,15},{8,0},{9,1},... | collective-permute-start | bytes 196616 | tf_op jit(solution)/shard_map/ppermute | solution.py:364
  44.8 7.4 %collective-permute-start.1 = (bf16[32,1024]{1,0:T(8,128)(2,1)S(1)}, bf16[32,1024]{1,0:T(8,128)(2,1)S(1)}, u32[]{:S(2)}, u32[]{:S(2)}) collective-permute-start(bf16[32,1024]{1,0:T(8,128)(2,1)S(1)} %broadcast_select_fusion), channel_id=1, source_target_pairs={{0,12},{1,13},{2,14},{3,15},{4,0},{5,1},{6,2},{7,3},{8,4},{9,5},{1... | collective-permute-start | bytes 196616 | tf_op jit(solution)/shard_map/ppermute | solution.py:364
  52.2 11.6 %collective-permute-start.6 = (bf16[4,32,1024]{2,1,0:T(8,128)(2,1)S(1)}, bf16[4,32,1024]{2,1,0:T(8,128)(2,1)S(1)}, u32[]{:S(2)}, u32[]{:S(2)}) collective-permute-start(bf16[4,32,1024]{2,1,0:T(8,128)(2,1)S(1)} %pad_maximum_fusion.refs_0_), channel_id=1, source_target_pairs={{0,1},{1,2},{2,3},{3,0},{4,5},{5,6},{6,7},{7,4},{8,9},{9,10},{10,1... | collective-permute-start | bytes 786440 | tf_op jit(solution)/shard_map/ppermute | solution.py:365
  55.7 10.0 %collective-permute-start.5 = (bf16[4,32,1024]{2,1,0:T(8,128)(2,1)S(1)}, bf16[4,32,1024]{2,1,0:T(8,128)(2,1)S(1)}, u32[]{:S(2)}, u32[]{:S(2)}) collective-permute-start(bf16[4,32,1024]{2,1,0:T(8,128)(2,1)S(1)} %pad_maximum_fusion.refs_0_), channel_id=1, source_target_pairs={{0,2},{1,3},{2,0},{3,1},{4,6},{5,7},{6,4},{7,5},{8,10},{9,11},{10,... | collective-permute-start | bytes 786440 | tf_op jit(solution)/shard_map/ppermute | solution.py:365
  60.6 8.3 %collective-permute-start.4 = (bf16[4,32,1024]{2,1,0:T(8,128)(2,1)S(1)}, bf16[4,32,1024]{2,1,0:T(8,128)(2,1)S(1)}, u32[]{:S(2)}, u32[]{:S(2)}) collective-permute-start(bf16[4,32,1024]{2,1,0:T(8,128)(2,1)S(1)} %pad_maximum_fusion.refs_0_), channel_id=1, source_target_pairs={{0,3},{1,0},{2,1},{3,2},{4,7},{5,4},{6,5},{7,6},{8,11},{9,8},{10,9... | collective-permute-start | bytes 786440 | tf_op jit(solution)/shard_map/ppermute | solution.py:365
  76.2 4.2 %collective-permute-start.7 = (bf16[16,128,128]{2,1,0:T(8,128)(2,1)S(1)}, bf16[16,128,128]{2,1,0:T(8,128)(2,1)S(1)}, u32[]{:S(2)}, u32[]{:S(2)}) collective-permute-start(bf16[16,128,128]{2,1,0:T(8,128)(2,1)S(1)} %shard_map.92), channel_id=1, source_target_pairs={{0,32},{1,33},{2,34},{3,35},{4,36},{5,37},{6,38},{7,39},{8,40},{9,... | collective-permute-start | bytes 1572872 | tf_op jit(solution)/shard_map/ppermute | solution.py:369
  83.6 32.0 %all-to-all-start.1 = ((bf16[16,64,128]{2,1,0:T(8,128)(2,1)}), bf16[16,64,128]{2,1,0:T(8,128)(2,1)S(1)}, u32[]{:S(2)}, u32[]{:S(2)}) async-start(bf16[16,64,128]{2,1,0:T(8,128)(2,1)} %shard_map.93), calls=%async_computation.1 | async-start | bytes 524288 | tf_op jit(solution)/shard_map/all_to_all | solution.py:372
  96.2 8.8 %collective-permute-start.8 = (bf16[4,32,1024]{2,1,0:T(8,128)(2,1)S(1)}, bf16[4,32,1024]{2,1,0:T(8,128)(2,1)S(1)}, u32[]{:S(2)}, u32[]{:S(2)}) collective-permute-start(bf16[4,32,1024]{2,1,0:T(8,128)(2,1)S(1)} %pad_maximum_fusion.refs_0_), channel_id=1, source_target_pairs={{0,32},{1,33},{2,34},{3,35},{4,36},{5,37},{6,38},{7,39},{8,40},{9,... | collective-permute-start | bytes 786440 | tf_op jit(solution)/shard_map/ppermute | solution.py:370
  98.5 6.5 %collective-permute-start.11 = (bf16[4,32,1024]{2,1,0:T(8,128)(2,1)S(1)}, bf16[4,32,1024]{2,1,0:T(8,128)(2,1)S(1)}, u32[]{:S(2)}, u32[]{:S(2)}) collective-permute-start(bf16[4,32,1024]{2,1,0:T(8,128)(2,1)S(1)} %collective-permute-done.6.refs_3_), channel_id=1, source_target_pairs={{0,32},{1,33},{2,34},{3,35},{4,36},{5,37},{6,38},{7,39},{8,40},{9,... | collective-permute-start | bytes 786440 | tf_op jit(solution)/shard_map/ppermute | solution.py:370
  100.5 4.4 %collective-permute-start.10 = (bf16[4,32,1024]{2,1,0:T(8,128)(2,1)S(1)}, bf16[4,32,1024]{2,1,0:T(8,128)(2,1)S(1)}, u32[]{:S(2)}, u32[]{:S(2)}) collective-permute-start(bf16[4,32,1024]{2,1,0:T(8,128)(2,1)S(1)} %collective-permute-done.5.refs_2_), channel_id=1, source_target_pairs={{0,32},{1,33},{2,34},{3,35},{4,36},{5,37},{6,38},{7,39},{8,40},{9,... | collective-permute-start | bytes 786440 | tf_op jit(solution)/shard_map/ppermute | solution.py:370
  102.9 3.4 %collective-permute-start.9 = (bf16[4,32,1024]{2,1,0:T(8,128)(2,1)S(1)}, bf16[4,32,1024]{2,1,0:T(8,128)(2,1)S(1)}, u32[]{:S(2)}, u32[]{:S(2)}) collective-permute-start(bf16[4,32,1024]{2,1,0:T(8,128)(2,1)S(1)} %collective-permute-done.4.refs_1_), channel_id=1, source_target_pairs={{0,32},{1,33},{2,34},{3,35},{4,36},{5,37},{6,38},{7,39},{8,40},{9,... | collective-permute-start | bytes 786440 | tf_op jit(solution)/shard_map/ppermute | solution.py:370
  118.5 0.7 copy-start.1
  119.2 26.3 %all-to-all-start.2 = ((bf16[32,16,1024]{2,1,0:T(8,128)(2,1)}), bf16[32,16,1024]{2,1,0:T(8,128)(2,1)S(1)}, u32[]{:S(2)}, u32[]{:S(2)}) async-start(bf16[32,16,1024]{2,1,0:T(8,128)(2,1)} %bitcast.9), calls=%async_computation.2 | async-start | bytes 2097152 | tf_op jit(solution)/shard_map/all_to_all | solution.py:379
  135.8 9.5 %copy-start = (bf16[2304,1024]{1,0:T(8,128)(2,1)S(1)}, bf16[2304,1024]{1,0:T(8,128)(2,1)}, u32[]{:S(2)}) copy-start(bf16[2304,1024]{1,0:T(8,128)(2,1)} %all-gather.3.cloned.1.call-done) | copy-start | bytes 14155780
  139.0 8.6 %collective-permute-start.12 = (bf16[3,144,1024]{2,1,0:T(8,128)(2,1)}, bf16[3,144,1024]{2,1,0:T(8,128)(2,1)}, u32[]{:S(2)}, u32[]{:S(2)}) collective-permute-start(bf16[3,144,1024]{2,1,0:T(8,128)(2,1)} %get-tuple-element.14), channel_id=1, source_target_pairs={{0,32},{1,33},{2,34},{3,35},{4,36},{5,37},{6,38},{7,39},{8,40},{9,... | collective-permute-start | bytes 2654216 | tf_op jit(solution)/shard_map/ppermute | solution.py:383
  141.0 6.7 %collective-permute-start.13 = (bf16[3,144,1024]{2,1,0:T(8,128)(2,1)}, bf16[3,144,1024]{2,1,0:T(8,128)(2,1)}, u32[]{:S(2)}, u32[]{:S(2)}) collective-permute-start(bf16[3,144,1024]{2,1,0:T(8,128)(2,1)} %get-tuple-element.15), channel_id=1, source_target_pairs={{0,32},{1,33},{2,34},{3,35},{4,36},{5,37},{6,38},{7,39},{8,40},{9,... | collective-permute-start | bytes 2654216 | tf_op jit(solution)/shard_map/ppermute | solution.py:383
  143.4 4.2 %collective-permute-start.14 = (bf16[2,144,1024]{2,1,0:T(8,128)(2,1)}, bf16[2,144,1024]{2,1,0:T(8,128)(2,1)}, u32[]{:S(2)}, u32[]{:S(2)}) collective-permute-start(bf16[2,144,1024]{2,1,0:T(8,128)(2,1)} %get-tuple-element.16), channel_id=1, source_target_pairs={{0,32},{1,33},{2,34},{3,35},{4,36},{5,37},{6,38},{7,39},{8,40},{9,... | collective-permute-start | bytes 1769480 | tf_op jit(solution)/shard_map/ppermute | solution.py:383
  147.6 27.6 %copy-start.2 = (bf16[128,1024]{1,0:T(8,128)(2,1)S(1)}, bf16[128,1024]{1,0:T(8,128)(2,1)}, u32[]{:S(2)}) copy-start(bf16[128,1024]{1,0:T(8,128)(2,1)} %copy-done.1) | copy-start | bytes 786436
Sparse Core Ops, SparseCore 0:
  9.4 126.2 all-gather.2

commit v6 on v4

--- a/solution.py
+++ b/solution.py
@@ -11,7 +11,7 @@
 HEAD_DIM = 128
 TOP = 2
 SLOT = 16
-PART = 2
+PARTS = (3, 3, 2)
 NEG_FILL = -1e30
 LOG2E = 1.4426950408889634
 BF = jnp.bfloat16
@@ -41,7 +41,9 @@
 
 
 CORE_SWAP = all_pairs(lambda zlo, core, zhi, xy: (zlo, 1 - core, zhi, xy))
-HALF_MOVE = all_pairs(lambda zlo, core, zhi, xy: (zlo, core, 1 - zhi, xy) if zhi == core else None)
+HALF_MOVE = all_pairs(
+    lambda zlo, core, zhi, xy: (7 - zlo, core, 1 - zhi, xy) if zhi == core else None
+)
 
 
 def plane_pairs(phase, step):
@@ -278,10 +280,10 @@
     first = ((1 - core) if flip else core) * 8
     copies = []
     for n, ref in enumerate(refs[:-1]):
-        size = ref.shape[0]
         copies.append(
-            pltpu.make_async_copy(weights_ref.at[pl.ds(first + n * size, size)], ref, sems.at[n])
+            pltpu.make_async_copy(weights_ref.at[pl.ds(first, ref.shape[0])], ref, sems.at[n])
         )
+        first = first + ref.shape[0]
     for copy in copies:
         copy.start()
     for copy in copies:
@@ -291,22 +293,23 @@
 def pick(core, weights, after, flip, parts):
     return pl.pallas_call(
         functools.partial(pick_kernel, flip),
-        out_shape=(jax.ShapeDtypeStruct((8 // parts,) + weights.shape[1:], BF),) * parts,
+        out_shape=tuple(jax.ShapeDtypeStruct((n,) + weights.shape[1:], BF) for n in parts),
         in_specs=[SMEM, HBM, ANY],
-        out_specs=(VMEM,) * parts,
-        scratch_shapes=[pltpu.SemaphoreType.DMA((parts,))],
+        out_specs=(VMEM,) * len(parts),
+        scratch_shapes=[pltpu.SemaphoreType.DMA((len(parts),))],
         compiler_params=params(52 if flip else 40),
         cost_estimate=pl.CostEstimate(flops=0, bytes_accessed=8 << 20, transcendentals=0),
     )(core, weights, after)
 
 
 def expert_kernel(core_ref, x_ref, own_ref, *refs):
-    oth_refs, (out_ref, up, down) = refs[: 8 // PART], refs[8 // PART :]
+    oth_refs, (out_ref, up, down) = refs[: len(PARTS)], refs[len(PARTS) :]
     core = core_ref[0]
     pieces = [(own_ref, slice(0, 8), core)]
-    pieces += [
-        (ref, slice(n * PART, (n + 1) * PART), 1 - core) for n, ref in enumerate(oth_refs)
-    ]
+    first = 0
+    for ref in oth_refs:
+        pieces.append((ref, slice(first, first + ref.shape[0]), 1 - core))
+        first += ref.shape[0]
     for source, z, place in pieces:
         up[z, place, :, 0:1024] = source[:, 0:64, :]
         up[z, place, 0:32, 1024:1536] = source[:, 64:96, 0:512]
@@ -395,9 +398,9 @@
     arrived = lax.all_to_all(
         outgoing.reshape(32, SLOT, 1024), ("core", "xy"), split_axis=0, concat_axis=0, tiled=True
     )
-    to_send = pick(core, weights, target, True, 8 // PART)
+    to_send = pick(core, weights, target, True, PARTS)
     oth_weights = [lax.ppermute(w, ALL, CORE_SWAP) for w in to_send]
-    (own_weights,) = pick(core, weights, target, False, 1)
+    (own_weights,) = pick(core, weights, target, False, (8,))
     produced = experts(core, arrived.reshape(32 * SLOT, 1024), own_weights, oth_weights)
     back = lax.all_to_all(
         produced.reshape(32, SLOT, 1024), ("core", "xy"), split_axis=0, concat_axis=0, tiled=True

time: 185 us -> 178 us (0.962)
  starting transfers between devices: 97.1 us -> 89.5 us
    ppermute x1, waiting for transfers between devices: 18 us -> 2.26 us  [on_device(): moved = lax.ppermute(out_proj, ALL, HALF_MOVE)]
    all_to_all x1, waiting for transfers between devices: 0.01 us -> 9.56 us  [on_device(): lax.all_to_all(heads, ('zlo', 'core'), split_axis=0, concat_axis=0, tiled...]
    all_to_all x1, starting transfers between devices: 31.1 us -> 22.6 us  [on_device(): lax.all_to_all(context, ('zlo', 'core'), split_axis=0, concat_axis=0, til...]
    all_gather x1, waiting for transfers between devices: 0.02 us -> 6.72 us  [on_device(): weights = lax.all_gather(packed, ('zhi', 'zlo'), axis=0, tiled=False)]
    all_to_all x1, waiting for transfers between devices: 3.37 us -> 0.01 us  [on_device(): lax.all_to_all(outgoing.reshape(32, SLOT, 1024), ('core', 'xy'), split_ax...]
    ppermute x4 -> x3, starting transfers between devices: 8.66 us -> 6.25 us  [on_device(): oth_weights = [lax.ppermute(w, ALL, CORE_SWAP) for w in to_send]]
    ppermute x1, starting transfers between devices: 2.97 us -> 5.3 us  [on_device(): oth_keys = lax.ppermute(keys_of(heads, pieces), ALL, CORE_SWAP)]
    ppermute x4 -> x3, waiting for transfers between devices: 0.01 us -> 2.11 us  [on_device(): oth_weights = [lax.ppermute(w, ALL, CORE_SWAP) for w in to_send]]
  transfers between devices with their start and end apart: 20 -> 19, of which waited for: 6 -> 8; matrix products, arithmetic and copies ran while one was open for 1% -> 1% of each run, Pallas kernels for 6% -> 7%
where the time goes in v6:
time: 178 us; the launch traced here: 175 us
  starting transfers between devices  89.5 us (50%)
  waiting for transfers between devices  28.7 us (16%)
  blocking collectives  22.8 us (13%)
  Pallas kernels  19.1 us (11%)
  between operations  13.7 us (8%)
    all_to_all x1, blocking collectives, on_device(): lax.all_to_all(produced.reshape(32, SLOT, 1024), ('core', 'xy'), split_ax...  22.8 us
    all_to_all x1, starting transfers between devices, on_device(): lax.all_to_all(context, ('zlo', 'core'), split_axis=0, concat_axis=0, til...  22.6 us
    all_to_all x1, starting transfers between devices, on_device(): lax.all_to_all(heads, ('zlo', 'core'), split_axis=0, concat_axis=0, tiled...  12.6 us
    ppermute x3, starting transfers between devices, on_device(): lax.ppermute(line, ALL, plane_pairs(1, d))  9.75 us
    all_to_all x1, waiting for transfers between devices, on_device(): lax.all_to_all(heads, ('zlo', 'core'), split_axis=0, concat_axis=0, tiled...  9.56 us
    ppermute x3, starting transfers between devices, on_device(): lax.ppermute(shard, ALL, plane_pairs(0, d))  8.85 us
    ppermute x1, starting transfers between devices, on_device(): moved = lax.ppermute(out_proj, ALL, HALF_MOVE)  8.68 us
    ppermute x4, starting transfers between devices, on_device(): proj_oth = [lax.ppermute(p, ALL, CORE_SWAP) for p in proj_own]  8.62 us
  transfers between devices with their start and end apart: 19, of which 8 were waited for; matrix products, arithmetic and copies ran while one was open for 1% of the time, Pallas kernels for 7%

profile of v6, /device:TPU:6, one launch (start us, length us, event | category | flops | bytes accessed | tf_op | source)
XLA Modules:
  0.0 175.4 jit_solution(8859839730379677073)
XLA Ops:
  6.5 1.8 %shard_map.96 = bf16[144,1024]{1,0:T(8,128)(2,1)} custom-call(bf16[1,64,1536]{2,1,0:T(8,128)(2,1)} %up_ref.1, bf16[1,48,1024]{2,1,0:T(8,128)(2,1)} %down_ref.1), custom_call_target="tpu_custom_call" | custom-call | tf_op jit(solution)/shard_map/pallas_call | solution.py:81
  8.3 0.0 all-gather.3.cloned.1.call-update
  8.4 2.1 %shard_map.91 = bf16[16,192,128]{2,1,0:T(8,128)(2,1)} custom-call(bf16[1,128,1024]{2,1,0:T(8,128)(2,1)} %q_ref.1, bf16[1,128,1024]{2,1,0:T(8,128)(2,1)} %k_ref.1, bf16[1,128,1024]{2,1,0:T(8,128)(2,1)} %v_ref.1), custom_call_target="tpu_custom_call" | custom-call | bytes 20971520 | tf_op jit(solution)/shard_map/pallas_call | solution.py:112
  10.5 12.6 %all-to-all-start = ((bf16[16,192,128]{2,1,0:T(8,128)(2,1)}), bf16[16,192,128]{2,1,0:T(8,128)(2,1)S(1)}, u32[]{:S(2)}, u32[]{:S(2)}) async-start(bf16[16,192,128]{2,1,0:T(8,128)(2,1)} %shard_map.91), calls=%async_computation | async-start | bytes 1572864 | tf_op jit(solution)/shard_map/all_to_all | solution.py:384
  23.1 8.7 %collective-permute-start = (bf16[32,1024]{1,0:T(8,128)(2,1)}, bf16[32,1024]{1,0:T(8,128)(2,1)S(1)}, u32[]{:S(2)}, u32[]{:S(2)}) collective-permute-start(bf16[32,1024]{1,0:T(8,128)(2,1)} %param.13), channel_id=1, source_target_pairs={{0,464},{1,465},{2,466},{3,467},{4,468},{5,469},{6,470},{7,471},{8... | collective-permute-start | bytes 196616 | tf_op jit(solution)/shard_map/ppermute | solution.py:379
  31.8 2.3 %collective-permute-done = bf16[32,1024]{1,0:T(8,128)(2,1)S(1)} collective-permute-done((bf16[32,1024]{1,0:T(8,128)(2,1)}, bf16[32,1024]{1,0:T(8,128)(2,1)S(1)}, u32[]{:S(2)}, u32[]{:S(2)}) %collective-permute-start) | collective-permute-done | bytes 65568 | tf_op jit(solution)/shard_map/ppermute | solution.py:379
  34.1 0.8 broadcast_select_fusion.refs_0_
  34.9 2.3 %collective-permute-start.3 = (bf16[32,1024]{1,0:T(8,128)(2,1)S(1)}, bf16[32,1024]{1,0:T(8,128)(2,1)S(1)}, u32[]{:S(2)}, u32[]{:S(2)}) collective-permute-start(bf16[32,1024]{1,0:T(8,128)(2,1)S(1)} %broadcast_select_fusion.refs_0_), channel_id=1, source_target_pairs={{0,4},{1,5},{2,6},{3,7},{4,8},{5,9},{6,10},{7,11},{8,12},{9,13},{1... | collective-permute-start | bytes 196616 | tf_op jit(solution)/shard_map/ppermute | solution.py:381
  37.2 4.6 %collective-permute-start.2 = (bf16[32,1024]{1,0:T(8,128)(2,1)S(1)}, bf16[32,1024]{1,0:T(8,128)(2,1)S(1)}, u32[]{:S(2)}, u32[]{:S(2)}) collective-permute-start(bf16[32,1024]{1,0:T(8,128)(2,1)S(1)} %broadcast_select_fusion.refs_0_), channel_id=1, source_target_pairs={{0,8},{1,9},{2,10},{3,11},{4,12},{5,13},{6,14},{7,15},{8,0},{9,1},... | collective-permute-start | bytes 196616 | tf_op jit(solution)/shard_map/ppermute | solution.py:381
  41.9 1.9 %collective-permute-start.1 = (bf16[32,1024]{1,0:T(8,128)(2,1)S(1)}, bf16[32,1024]{1,0:T(8,128)(2,1)S(1)}, u32[]{:S(2)}, u32[]{:S(2)}) collective-permute-start(bf16[32,1024]{1,0:T(8,128)(2,1)S(1)} %broadcast_select_fusion.refs_0_), channel_id=1, source_target_pairs={{0,12},{1,13},{2,14},{3,15},{4,0},{5,1},{6,2},{7,3},{8,4},{9,5},{1... | collective-permute-start | bytes 196616 | tf_op jit(solution)/shard_map/ppermute | solution.py:381
  43.8 0.0 collective-permute-done.3.refs_3_
  43.8 1.1 collective-permute-done.2.refs_2_
  44.9 4.3 %collective-permute-done.1.refs_1_ = bf16[32,1024]{1,0:T(8,128)(2,1)S(1)} collective-permute-done((bf16[32,1024]{1,0:T(8,128)(2,1)S(1)}, bf16[32,1024]{1,0:T(8,128)(2,1)S(1)}, u32[]{:S(2)}, u32[]{:S(2)}) %collective-permute-start.1) | collective-permute-done | bytes 65568 | tf_op jit(solution)/shard_map/ppermute | solution.py:381
  49.2 9.6 %all-to-all-done.heads_ref.own_ref = bf16[16,192,128]{2,1,0:T(8,128)(2,1)S(1)} async-done(((bf16[16,192,128]{2,1,0:T(8,128)(2,1)}), bf16[16,192,128]{2,1,0:T(8,128)(2,1)S(1)}, u32[]{:S(2)}, u32[]{:S(2)}) %all-to-all-start) | async-done | bytes 786464 | tf_op jit(solution)/shard_map/all_to_all | solution.py:384
  58.8 5.3 %collective-permute-start.4 = (bf16[16,128,128]{2,1,0:T(8,128)(2,1)S(1)}, bf16[16,128,128]{2,1,0:T(8,128)(2,1)S(1)}, u32[]{:S(2)}, u32[]{:S(2)}) collective-permute-start(bf16[16,128,128]{2,1,0:T(8,128)(2,1)S(1)} %shard_map.92), channel_id=1, source_target_pairs={{0,32},{1,33},{2,34},{3,35},{4,36},{5,37},{6,38},{7,39},{8,40},{9,... | collective-permute-start | bytes 1572872 | tf_op jit(solution)/shard_map/ppermute | solution.py:385
  64.2 1.5 collective-permute-done.4.oth_ref
  65.7 3.2 %shard_map.93.refs_4_ = bf16[16,64,128]{2,1,0:T(8,128)(2,1)} custom-call(s32[1]{0:T(128)} %bitcast.core_ref, bf16[16,192,128]{2,1,0:T(8,128)(2,1)S(1)} %all-to-all-done.heads_ref.own_ref, bf16[16,128,128]{2,1,0:T(8,128)(2,1)S(1)} %collective-permute-done.4.oth_ref), custom_call_target="tpu_custom_call" | custom-call | flops 671088640 | bytes 2097152 | tf_op jit(solution)/shard_map/pallas_call | solution.py:192
  68.8 22.6 %all-to-all-start.1 = ((bf16[16,64,128]{2,1,0:T(8,128)(2,1)}), bf16[16,64,128]{2,1,0:T(8,128)(2,1)S(1)}, u32[]{:S(2)}, u32[]{:S(2)}) async-start(bf16[16,64,128]{2,1,0:T(8,128)(2,1)} %shard_map.93.refs_4_), calls=%async_computation.1 | async-start | bytes 524288 | tf_op jit(solution)/shard_map/all_to_all | solution.py:391
  91.5 1.9 %collective-permute-start.7 = (bf16[4,32,1024]{2,1,0:T(8,128)(2,1)S(1)}, bf16[4,32,1024]{2,1,0:T(8,128)(2,1)S(1)}, u32[]{:S(2)}, u32[]{:S(2)}) collective-permute-start(bf16[4,32,1024]{2,1,0:T(8,128)(2,1)S(1)} %shard_map.94.refs_0_), channel_id=1, source_target_pairs={{0,1},{1,2},{2,3},{3,0},{4,5},{5,6},{6,7},{7,4},{8,9},{9,10},{10,1... | collective-permute-start | bytes 786440 | tf_op jit(solution)/shard_map/ppermute | solution.py:389
  93.4 5.9 %collective-permute-start.6 = (bf16[4,32,1024]{2,1,0:T(8,128)(2,1)S(1)}, bf16[4,32,1024]{2,1,0:T(8,128)(2,1)S(1)}, u32[]{:S(2)}, u32[]{:S(2)}) collective-permute-start(bf16[4,32,1024]{2,1,0:T(8,128)(2,1)S(1)} %shard_map.94.refs_0_), channel_id=1, source_target_pairs={{0,2},{1,3},{2,0},{3,1},{4,6},{5,7},{6,4},{7,5},{8,10},{9,11},{10,... | collective-permute-start | bytes 786440 | tf_op jit(solution)/shard_map/ppermute | solution.py:389
  99.4 1.9 %collective-permute-start.5 = (bf16[4,32,1024]{2,1,0:T(8,128)(2,1)S(1)}, bf16[4,32,1024]{2,1,0:T(8,128)(2,1)S(1)}, u32[]{:S(2)}, u32[]{:S(2)}) collective-permute-start(bf16[4,32,1024]{2,1,0:T(8,128)(2,1)S(1)} %shard_map.94.refs_0_), channel_id=1, source_target_pairs={{0,3},{1,0},{2,1},{3,2},{4,7},{5,4},{6,5},{7,6},{8,11},{9,8},{10,9... | collective-permute-start | bytes 786440 | tf_op jit(solution)/shard_map/ppermute | solution.py:389
  101.3 1.9 %collective-permute-start.8 = (bf16[4,32,1024]{2,1,0:T(8,128)(2,1)S(1)}, bf16[4,32,1024]{2,1,0:T(8,128)(2,1)S(1)}, u32[]{:S(2)}, u32[]{:S(2)}) collective-permute-start(bf16[4,32,1024]{2,1,0:T(8,128)(2,1)S(1)} %shard_map.94.refs_0_), channel_id=1, source_target_pairs={{0,32},{1,33},{2,34},{3,35},{4,36},{5,37},{6,38},{7,39},{8,40},{9,... | collective-permute-start | bytes 786440 | tf_op jit(solution)/shard_map/ppermute | solution.py:390
  103.2 0.0 collective-permute-done.7.refs_3_
  103.2 2.4 %collective-permute-start.11 = (bf16[4,32,1024]{2,1,0:T(8,128)(2,1)S(1)}, bf16[4,32,1024]{2,1,0:T(8,128)(2,1)S(1)}, u32[]{:S(2)}, u32[]{:S(2)}) collective-permute-start(bf16[4,32,1024]{2,1,0:T(8,128)(2,1)S(1)} %collective-permute-done.7.refs_3_), channel_id=1, source_target_pairs={{0,32},{1,33},{2,34},{3,35},{4,36},{5,37},{6,38},{7,39},{8,40},{9,... | collective-permute-start | bytes 786440 | tf_op jit(solution)/shard_map/ppermute | solution.py:390
  105.6 0.0 collective-permute-done.6.refs_2_
  105.7 1.9 %collective-permute-start.10 = (bf16[4,32,1024]{2,1,0:T(8,128)(2,1)S(1)}, bf16[4,32,1024]{2,1,0:T(8,128)(2,1)S(1)}, u32[]{:S(2)}, u32[]{:S(2)}) collective-permute-start(bf16[4,32,1024]{2,1,0:T(8,128)(2,1)S(1)} %collective-permute-done.6.refs_2_), channel_id=1, source_target_pairs={{0,32},{1,33},{2,34},{3,35},{4,36},{5,37},{6,38},{7,39},{8,40},{9,... | collective-permute-start | bytes 786440 | tf_op jit(solution)/shard_map/ppermute | solution.py:390
  107.6 0.0 collective-permute-done.5.refs_1_
  107.6 2.4 %collective-permute-start.9 = (bf16[4,32,1024]{2,1,0:T(8,128)(2,1)S(1)}, bf16[4,32,1024]{2,1,0:T(8,128)(2,1)S(1)}, u32[]{:S(2)}, u32[]{:S(2)}) collective-permute-start(bf16[4,32,1024]{2,1,0:T(8,128)(2,1)S(1)} %collective-permute-done.5.refs_1_), channel_id=1, source_target_pairs={{0,32},{1,33},{2,34},{3,35},{4,36},{5,37},{6,38},{7,39},{8,40},{9,... | collective-permute-start | bytes 786440 | tf_op jit(solution)/shard_map/ppermute | solution.py:390
  110.0 0.1 pad_add_fusion.where_ref
  110.1 0.0 collective-permute-done.8.refs_4_
  110.1 0.0 collective-permute-done.11.refs_7_
  110.1 0.0 collective-permute-done.10.refs_6_
  110.1 1.0 collective-permute-done.9.refs_5_
  111.2 0.0 all-to-all-done.1.ctx_ref
  111.2 2.9 %shard_map.95 = (bf16[128,1024]{1,0:T(8,128)(2,1)S(1)}, bf16[512,1024]{1,0:T(8,128)(2,1)}, f32[2,128]{1,0:T(2,128)S(1)}, s32[2,128]{1,0:T(2,128)S(1)}) custom-call(s32[3]{0:T(128)S(1)} %pad_add_fusion.where_ref, bf16[16,64,128]{2,1,0:T(8,128)(2,1)S(1)} %all-to-all-done.1.ctx_ref, bf16[4,32,1024]{2,1,0:T(8,128)(2,1)S(1)} %shard_map.94.refs_0_, ...), custom_call_target="tpu_custom_call" | custom-call | flops 419430400 | bytes 4194304 | tf_op jit(solution)/shard_map/pallas_call | solution.py:256
  114.0 0.7 copy-done.1
  114.7 6.7 %all-to-all-start.2 = ((bf16[32,16,1024]{2,1,0:T(8,128)(2,1)}), bf16[32,16,1024]{2,1,0:T(8,128)(2,1)S(1)}, u32[]{:S(2)}, u32[]{:S(2)}) async-start(bf16[32,16,1024]{2,1,0:T(8,128)(2,1)} %bitcast.5), calls=%async_computation.2 | async-start | bytes 2097152 | tf_op jit(solution)/shard_map/all_to_all | solution.py:398
  121.5 6.7 %all-gather.3.cloned.1.call-done = bf16[2304,1024]{1,0:T(8,128)(2,1)} async-done(((bf16[144,1024]{1,0:T(8,128)(2,1)}), bf16[2304,1024]{1,0:T(8,128)(2,1)}) %all-gather.3.cloned.1.call-update) | async-done | bytes 4718608 | tf_op jit(solution)/shard_map/all_gather | solution.py:377
  128.2 3.3 %shard_map.98 = (bf16[3,144,1024]{2,1,0:T(8,128)(2,1)}, bf16[3,144,1024]{2,1,0:T(8,128)(2,1)}, bf16[2,144,1024]{2,1,0:T(8,128)(2,1)}) custom-call(s32[1]{0:T(128)} %bitcast.core_ref, bf16[16,144,1024]{2,1,0:T(8,128)(2,1)} %bitcast.11, s32[2,128]{1,0:T(2,128)S(1)} %get-tuple-element.13.after_ref.target_ref), custom_call_target="tpu_custom_call" | custom-call | bytes 8388608 | tf_op jit(solution)/shard_map/pallas_call | solution.py:294
  131.5 1.9 %collective-permute-start.12 = (bf16[3,144,1024]{2,1,0:T(8,128)(2,1)}, bf16[3,144,1024]{2,1,0:T(8,128)(2,1)}, u32[]{:S(2)}, u32[]{:S(2)}) collective-permute-start(bf16[3,144,1024]{2,1,0:T(8,128)(2,1)} %get-tuple-element.14), channel_id=1, source_target_pairs={{0,32},{1,33},{2,34},{3,35},{4,36},{5,37},{6,38},{7,39},{8,40},{9,... | collective-permute-start | bytes 2654216 | tf_op jit(solution)/shard_map/ppermute | solution.py:402
  133.4 2.4 %collective-permute-start.13 = (bf16[3,144,1024]{2,1,0:T(8,128)(2,1)}, bf16[3,144,1024]{2,1,0:T(8,128)(2,1)}, u32[]{:S(2)}, u32[]{:S(2)}) collective-permute-start(bf16[3,144,1024]{2,1,0:T(8,128)(2,1)} %get-tuple-element.15), channel_id=1, source_target_pairs={{0,32},{1,33},{2,34},{3,35},{4,36},{5,37},{6,38},{7,39},{8,40},{9,... | collective-permute-start | bytes 2654216 | tf_op jit(solution)/shard_map/ppermute | solution.py:402
  135.8 1.9 %collective-permute-start.14 = (bf16[2,144,1024]{2,1,0:T(8,128)(2,1)}, bf16[2,144,1024]{2,1,0:T(8,128)(2,1)}, u32[]{:S(2)}, u32[]{:S(2)}) collective-permute-start(bf16[2,144,1024]{2,1,0:T(8,128)(2,1)} %get-tuple-element.16), channel_id=1, source_target_pairs={{0,32},{1,33},{2,34},{3,35},{4,36},{5,37},{6,38},{7,39},{8,40},{9,... | collective-permute-start | bytes 1769480 | tf_op jit(solution)/shard_map/ppermute | solution.py:402
  137.8 0.2 shard_map.97.own_ref
  137.9 0.0 all-to-all-done.2
  137.9 2.1 %collective-permute-done.14.refs_2_ = bf16[2,144,1024]{2,1,0:T(8,128)(2,1)} collective-permute-done((bf16[2,144,1024]{2,1,0:T(8,128)(2,1)}, bf16[2,144,1024]{2,1,0:T(8,128)(2,1)}, u32[]{:S(2)}, u32[]{:S(2)}) %collective-permute-start.14) | collective-permute-done | bytes 589856 | tf_op jit(solution)/shard_map/ppermute | solution.py:402
  140.1 4.5 %shard_map.99 = bf16[512,1024]{1,0:T(8,128)(2,1)S(1)} custom-call(s32[1]{0:T(128)} %bitcast.core_ref, bf16[512,1024]{1,0:T(8,128)(2,1)S(1)} %bitcast.14, bf16[8,144,1024]{2,1,0:T(8,128)(2,1)S(1)} %shard_map.97.own_ref, bf16[3,144,1024]{2,1,0:T(8,128)(2,1)} %collective-permute-done.12.refs_0_, bf16[3,144,1024]{2,1,0:T(8,128)(2,1)} %collective-permute-done.13.refs_1_, ...), custom_call_target="tpu_custom_call" | custom-call | flops 2415919104 | bytes 7340032 | tf_op jit(solution)/shard_map/pallas_call | solution.py:328
  144.5 22.8 %all_to_all.20 = bf16[32,16,1024]{2,1,0:T(8,128)(2,1)S(1)} all-to-all(bf16[32,16,1024]{2,1,0:T(8,128)(2,1)S(1)} %bitcast.15), channel_id=1, replica_groups=mesh['zlo'=8,'core'=2,'zhi'=2,'xy'=16] {'core','xy'}, dimensions={0} | all-to-all | bytes 2097152 | tf_op jit(solution)/shard_map/all_to_all | solution.py:405
  167.3 1.2 shard_map.100
  (16 shorter events, 0.1 us)
Async XLA Ops:
  6.5 104.6 %copy-start.5 = (s32[1,128,2]{1,2,0:T(2,128)S(1)}, s32[1,128,2]{1,2,0:T(2,128)}, u32[]{:S(2)}) copy-start(s32[1,128,2]{1,2,0:T(2,128)} %param.15) | copy-start | bytes 3076
  6.5 104.6 %copy-start.4 = (bf16[1024,32]{0,1:T(8,128)(2,1)S(1)}, bf16[1024,32]{0,1:T(8,128)(2,1)}, u32[]{:S(2)}) copy-start(bf16[1024,32]{0,1:T(8,128)(2,1)} %param.14) | copy-start | bytes 196612
  6.5 104.6 %copy-start.3 = (bf16[1,128,1024]{2,1,0:T(8,128)(2,1)S(1)}, bf16[1,128,1024]{2,1,0:T(8,128)(2,1)}, u32[]{:S(2)}) copy-start(bf16[1,128,1024]{2,1,0:T(8,128)(2,1)} %refs_8_.1) | copy-start | bytes 786436
  6.5 121.7 %all-gather.3.cloned.1.call-start = ((), (), s32[]{:S(2)}) async-start(), calls=%async_computation.4 | async-start | bytes 5013504 | tf_op jit(solution)/shard_map/all_gather | solution.py:377
  10.5 48.3 %all-to-all-start = ((bf16[16,192,128]{2,1,0:T(8,128)(2,1)}), bf16[16,192,128]{2,1,0:T(8,128)(2,1)S(1)}, u32[]{:S(2)}, u32[]{:S(2)}) async-start(bf16[16,192,128]{2,1,0:T(8,128)(2,1)} %shard_map.91), calls=%async_computation | async-start | bytes 1572864 | tf_op jit(solution)/shard_map/all_to_all | solution.py:384
  23.1 11.0 %collective-permute-start = (bf16[32,1024]{1,0:T(8,128)(2,1)}, bf16[32,1024]{1,0:T(8,128)(2,1)S(1)}, u32[]{:S(2)}, u32[]{:S(2)}) collective-permute-start(bf16[32,1024]{1,0:T(8,128)(2,1)} %param.13), channel_id=1, source_target_pairs={{0,464},{1,465},{2,466},{3,467},{4,468},{5,469},{6,470},{7,471},{8... | collective-permute-start | bytes 196616 | tf_op jit(solution)/shard_map/ppermute | solution.py:379
  34.9 8.9 %collective-permute-start.3 = (bf16[32,1024]{1,0:T(8,128)(2,1)S(1)}, bf16[32,1024]{1,0:T(8,128)(2,1)S(1)}, u32[]{:S(2)}, u32[]{:S(2)}) collective-permute-start(bf16[32,1024]{1,0:T(8,128)(2,1)S(1)} %broadcast_select_fusion.refs_0_), channel_id=1, source_target_pairs={{0,4},{1,5},{2,6},{3,7},{4,8},{5,9},{6,10},{7,11},{8,12},{9,13},{1... | collective-permute-start | bytes 196616 | tf_op jit(solution)/shard_map/ppermute | solution.py:381
  37.2 7.7 %collective-permute-start.2 = (bf16[32,1024]{1,0:T(8,128)(2,1)S(1)}, bf16[32,1024]{1,0:T(8,128)(2,1)S(1)}, u32[]{:S(2)}, u32[]{:S(2)}) collective-permute-start(bf16[32,1024]{1,0:T(8,128)(2,1)S(1)} %broadcast_select_fusion.refs_0_), channel_id=1, source_target_pairs={{0,8},{1,9},{2,10},{3,11},{4,12},{5,13},{6,14},{7,15},{8,0},{9,1},... | collective-permute-start | bytes 196616 | tf_op jit(solution)/shard_map/ppermute | solution.py:381
  41.9 7.4 %collective-permute-start.1 = (bf16[32,1024]{1,0:T(8,128)(2,1)S(1)}, bf16[32,1024]{1,0:T(8,128)(2,1)S(1)}, u32[]{:S(2)}, u32[]{:S(2)}) collective-permute-start(bf16[32,1024]{1,0:T(8,128)(2,1)S(1)} %broadcast_select_fusion.refs_0_), channel_id=1, source_target_pairs={{0,12},{1,13},{2,14},{3,15},{4,0},{5,1},{6,2},{7,3},{8,4},{9,5},{1... | collective-permute-start | bytes 196616 | tf_op jit(solution)/shard_map/ppermute | solution.py:381
  58.8 6.8 %collective-permute-start.4 = (bf16[16,128,128]{2,1,0:T(8,128)(2,1)S(1)}, bf16[16,128,128]{2,1,0:T(8,128)(2,1)S(1)}, u32[]{:S(2)}, u32[]{:S(2)}) collective-permute-start(bf16[16,128,128]{2,1,0:T(8,128)(2,1)S(1)} %shard_map.92), channel_id=1, source_target_pairs={{0,32},{1,33},{2,34},{3,35},{4,36},{5,37},{6,38},{7,39},{8,40},{9,... | collective-permute-start | bytes 1572872 | tf_op jit(solution)/shard_map/ppermute | solution.py:385
  68.8 42.3 %all-to-all-start.1 = ((bf16[16,64,128]{2,1,0:T(8,128)(2,1)}), bf16[16,64,128]{2,1,0:T(8,128)(2,1)S(1)}, u32[]{:S(2)}, u32[]{:S(2)}) async-start(bf16[16,64,128]{2,1,0:T(8,128)(2,1)} %shard_map.93.refs_4_), calls=%async_computation.1 | async-start | bytes 524288 | tf_op jit(solution)/shard_map/all_to_all | solution.py:391
  91.5 11.7 %collective-permute-start.7 = (bf16[4,32,1024]{2,1,0:T(8,128)(2,1)S(1)}, bf16[4,32,1024]{2,1,0:T(8,128)(2,1)S(1)}, u32[]{:S(2)}, u32[]{:S(2)}) collective-permute-start(bf16[4,32,1024]{2,1,0:T(8,128)(2,1)S(1)} %shard_map.94.refs_0_), channel_id=1, source_target_pairs={{0,1},{1,2},{2,3},{3,0},{4,5},{5,6},{6,7},{7,4},{8,9},{9,10},{10,1... | collective-permute-start | bytes 786440 | tf_op jit(solution)/shard_map/ppermute | solution.py:389
  93.4 12.2 %collective-permute-start.6 = (bf16[4,32,1024]{2,1,0:T(8,128)(2,1)S(1)}, bf16[4,32,1024]{2,1,0:T(8,128)(2,1)S(1)}, u32[]{:S(2)}, u32[]{:S(2)}) collective-permute-start(bf16[4,32,1024]{2,1,0:T(8,128)(2,1)S(1)} %shard_map.94.refs_0_), channel_id=1, source_target_pairs={{0,2},{1,3},{2,0},{3,1},{4,6},{5,7},{6,4},{7,5},{8,10},{9,11},{10,... | collective-permute-start | bytes 786440 | tf_op jit(solution)/shard_map/ppermute | solution.py:389
  99.4 8.3 %collective-permute-start.5 = (bf16[4,32,1024]{2,1,0:T(8,128)(2,1)S(1)}, bf16[4,32,1024]{2,1,0:T(8,128)(2,1)S(1)}, u32[]{:S(2)}, u32[]{:S(2)}) collective-permute-start(bf16[4,32,1024]{2,1,0:T(8,128)(2,1)S(1)} %shard_map.94.refs_0_), channel_id=1, source_target_pairs={{0,3},{1,0},{2,1},{3,2},{4,7},{5,4},{6,5},{7,6},{8,11},{9,8},{10,9... | collective-permute-start | bytes 786440 | tf_op jit(solution)/shard_map/ppermute | solution.py:389
  101.3 8.8 %collective-permute-start.8 = (bf16[4,32,1024]{2,1,0:T(8,128)(2,1)S(1)}, bf16[4,32,1024]{2,1,0:T(8,128)(2,1)S(1)}, u32[]{:S(2)}, u32[]{:S(2)}) collective-permute-start(bf16[4,32,1024]{2,1,0:T(8,128)(2,1)S(1)} %shard_map.94.refs_0_), channel_id=1, source_target_pairs={{0,32},{1,33},{2,34},{3,35},{4,36},{5,37},{6,38},{7,39},{8,40},{9,... | collective-permute-start | bytes 786440 | tf_op jit(solution)/shard_map/ppermute | solution.py:390
  103.2 6.9 %collective-permute-start.11 = (bf16[4,32,1024]{2,1,0:T(8,128)(2,1)S(1)}, bf16[4,32,1024]{2,1,0:T(8,128)(2,1)S(1)}, u32[]{:S(2)}, u32[]{:S(2)}) collective-permute-start(bf16[4,32,1024]{2,1,0:T(8,128)(2,1)S(1)} %collective-permute-done.7.refs_3_), channel_id=1, source_target_pairs={{0,32},{1,33},{2,34},{3,35},{4,36},{5,37},{6,38},{7,39},{8,40},{9,... | collective-permute-start | bytes 786440 | tf_op jit(solution)/shard_map/ppermute | solution.py:390
  105.7 4.5 %collective-permute-start.10 = (bf16[4,32,1024]{2,1,0:T(8,128)(2,1)S(1)}, bf16[4,32,1024]{2,1,0:T(8,128)(2,1)S(1)}, u32[]{:S(2)}, u32[]{:S(2)}) collective-permute-start(bf16[4,32,1024]{2,1,0:T(8,128)(2,1)S(1)} %collective-permute-done.6.refs_2_), channel_id=1, source_target_pairs={{0,32},{1,33},{2,34},{3,35},{4,36},{5,37},{6,38},{7,39},{8,40},{9,... | collective-permute-start | bytes 786440 | tf_op jit(solution)/shard_map/ppermute | solution.py:390
  107.6 3.5 %collective-permute-start.9 = (bf16[4,32,1024]{2,1,0:T(8,128)(2,1)S(1)}, bf16[4,32,1024]{2,1,0:T(8,128)(2,1)S(1)}, u32[]{:S(2)}, u32[]{:S(2)}) collective-permute-start(bf16[4,32,1024]{2,1,0:T(8,128)(2,1)S(1)} %collective-permute-done.5.refs_1_), channel_id=1, source_target_pairs={{0,32},{1,33},{2,34},{3,35},{4,36},{5,37},{6,38},{7,39},{8,40},{9,... | collective-permute-start | bytes 786440 | tf_op jit(solution)/shard_map/ppermute | solution.py:390
  114.0 0.7 copy-start.1
  114.7 23.2 %all-to-all-start.2 = ((bf16[32,16,1024]{2,1,0:T(8,128)(2,1)}), bf16[32,16,1024]{2,1,0:T(8,128)(2,1)S(1)}, u32[]{:S(2)}, u32[]{:S(2)}) async-start(bf16[32,16,1024]{2,1,0:T(8,128)(2,1)} %bitcast.5), calls=%async_computation.2 | async-start | bytes 2097152 | tf_op jit(solution)/shard_map/all_to_all | solution.py:398
  128.2 9.5 %copy-start = (bf16[2304,1024]{1,0:T(8,128)(2,1)S(1)}, bf16[2304,1024]{1,0:T(8,128)(2,1)}, u32[]{:S(2)}) copy-start(bf16[2304,1024]{1,0:T(8,128)(2,1)} %all-gather.3.cloned.1.call-done) | copy-start | bytes 14155780
  131.5 8.6 %collective-permute-start.12 = (bf16[3,144,1024]{2,1,0:T(8,128)(2,1)}, bf16[3,144,1024]{2,1,0:T(8,128)(2,1)}, u32[]{:S(2)}, u32[]{:S(2)}) collective-permute-start(bf16[3,144,1024]{2,1,0:T(8,128)(2,1)} %get-tuple-element.14), channel_id=1, source_target_pairs={{0,32},{1,33},{2,34},{3,35},{4,36},{5,37},{6,38},{7,39},{8,40},{9,... | collective-permute-start | bytes 2654216 | tf_op jit(solution)/shard_map/ppermute | solution.py:402
  133.4 6.7 %collective-permute-start.13 = (bf16[3,144,1024]{2,1,0:T(8,128)(2,1)}, bf16[3,144,1024]{2,1,0:T(8,128)(2,1)}, u32[]{:S(2)}, u32[]{:S(2)}) collective-permute-start(bf16[3,144,1024]{2,1,0:T(8,128)(2,1)} %get-tuple-element.15), channel_id=1, source_target_pairs={{0,32},{1,33},{2,34},{3,35},{4,36},{5,37},{6,38},{7,39},{8,40},{9,... | collective-permute-start | bytes 2654216 | tf_op jit(solution)/shard_map/ppermute | solution.py:402
  135.8 4.2 %collective-permute-start.14 = (bf16[2,144,1024]{2,1,0:T(8,128)(2,1)}, bf16[2,144,1024]{2,1,0:T(8,128)(2,1)}, u32[]{:S(2)}, u32[]{:S(2)}) collective-permute-start(bf16[2,144,1024]{2,1,0:T(8,128)(2,1)} %get-tuple-element.16), channel_id=1, source_target_pairs={{0,32},{1,33},{2,34},{3,35},{4,36},{5,37},{6,38},{7,39},{8,40},{9,... | collective-permute-start | bytes 1769480 | tf_op jit(solution)/shard_map/ppermute | solution.py:402
  140.1 27.3 %copy-start.2 = (bf16[128,1024]{1,0:T(8,128)(2,1)S(1)}, bf16[128,1024]{1,0:T(8,128)(2,1)}, u32[]{:S(2)}) copy-start(bf16[128,1024]{1,0:T(8,128)(2,1)} %copy-done.1) | copy-start | bytes 786436
Sparse Core Ops, SparseCore 0:
  9.4 118.7 all-gather.2

commit v7 on v6

--- a/solution.py
+++ b/solution.py
@@ -147,6 +147,21 @@
         out_specs=VMEM,
         compiler_params=params(4),
     )(*pieces, after)
+
+
+def stack_kernel(*refs):
+    for n, ref in enumerate(refs[:-1]):
+        refs[-1][n] = ref[...]
+
+
+def stack(pieces):
+    return pl.pallas_call(
+        stack_kernel,
+        out_shape=jax.ShapeDtypeStruct((len(pieces),) + pieces[0].shape, BF),
+        in_specs=[VMEM] * len(pieces),
+        out_specs=VMEM,
+        compiler_params=params(4),
+    )(*pieces)
 
 
 def attention_kernel(core_ref, own_ref, oth_ref, out_ref):
@@ -202,16 +217,17 @@
 
 
 def middle_kernel(where_ref, ctx_ref, *refs):
-    pieces, refs = refs[:8], refs[8:]
+    sides, refs = (refs[:2], refs[2:4]), refs[4:]
     res_ref, router_ref, ids_ref, hidden_ref, out_ref, gate_ref, target_ref = refs[:7]
     halves, proj = refs[7:]
     own, place = where_ref[0], (where_ref[1], where_ref[2])
-    for n in range(8):
-        core = own if n < 4 else 1 - own
-        for first in range(4):
-            along = (place[0] + jnp.where(core == 0, first, n % 4)) % 4
-            across = (place[1] + jnp.where(core == 0, n % 4, first)) % 4
-            proj[core, along * 4 + across] = pieces[n][first]
+    for side in range(2):
+        core = own if side == 0 else 1 - own
+        for second in range(4):
+            for first in range(4):
+                along = (place[0] + jnp.where(core == 0, first, second)) % 4
+                across = (place[1] + jnp.where(core == 0, second, first)) % 4
+                proj[core, along * 4 + across] = sides[side][second // 2][second % 2, first]
     for h in range(HEADS):
         for c in range(2):
             halves[c * 64 : (c + 1) * 64, h * 128 : (h + 1) * 128] = ctx_ref[h * 2 + c]
@@ -261,7 +277,7 @@
             jax.ShapeDtypeStruct((TOP, tokens), F32),
             jax.ShapeDtypeStruct((TOP, tokens), jnp.int32),
         ),
-        in_specs=[SMEM] + [VMEM] * 12,
+        in_specs=[SMEM] + [VMEM] * 8,
         out_specs=(VMEM,) * 4,
         scratch_shapes=[
             pltpu.VMEM((128, 1024), BF),
@@ -386,7 +402,8 @@
     context = attention(core, heads, oth_keys)
 
     line = line_of(pieces, context)
-    proj_own = [line] + [lax.ppermute(line, ALL, plane_pairs(1, d)) for d in (1, 2, 3)]
+    lines = [line] + [lax.ppermute(line, ALL, plane_pairs(1, d)) for d in (1, 2, 3)]
+    proj_own = [stack(lines[:2]), stack(lines[2:])]
     proj_oth = [lax.ppermute(p, ALL, CORE_SWAP) for p in proj_own]
     context = lax.all_to_all(context, ("zlo", "core"), split_axis=0, concat_axis=0, tiled=True)
 

time: 178 us -> 178 us (level)
  waiting for transfers between devices: 28.7 us -> 33.5 us
  starting transfers between devices: 89.5 us -> 84.9 us
    ppermute x3, waiting for transfers between devices: 0.05 us -> 5 us  [on_device(): lax.ppermute(line, ALL, plane_pairs(1, d))]
    ppermute x4 -> x2, starting transfers between devices: 8.62 us -> 3.84 us  [on_device(): proj_oth = [lax.ppermute(p, ALL, CORE_SWAP) for p in proj_own]]
  transfers between devices with their start and end apart: 19 -> 17, of which waited for: 8 -> 10; matrix products, arithmetic and copies ran while one was open for 1% -> 1% of each run, Pallas kernels for 7% -> 7%
where the time goes in v7:
time: 178 us; the launch traced here: 175 us
  starting transfers between devices  84.9 us (48%)
  waiting for transfers between devices  33.5 us (19%)
  blocking collectives  22.7 us (13%)
  Pallas kernels  19.1 us (11%)
  between operations  13.7 us (8%)
    all_to_all x1, blocking collectives, on_device(): lax.all_to_all(produced.reshape(32, SLOT, 1024), ('core', 'xy'), split_ax...  22.7 us
    all_to_all x1, starting transfers between devices, on_device(): lax.all_to_all(context, ('zlo', 'core'), split_axis=0, concat_axis=0, til...  22.3 us
    all_to_all x1, starting transfers between devices, on_device(): lax.all_to_all(heads, ('zlo', 'core'), split_axis=0, concat_axis=0, tiled...  12.8 us
    all_to_all x1, waiting for transfers between devices, on_device(): lax.all_to_all(heads, ('zlo', 'core'), split_axis=0, concat_axis=0, tiled...  9.84 us
    ppermute x3, starting transfers between devices, on_device(): lax.ppermute(line, ALL, plane_pairs(1, d))  9.68 us
    ppermute x1, starting transfers between devices, on_device(): moved = lax.ppermute(out_proj, ALL, HALF_MOVE)  8.68 us
    ppermute x3, starting transfers between devices, on_device(): lax.ppermute(shard, ALL, plane_pairs(0, d))  8.63 us
    all_to_all x1, starting transfers between devices, on_device(): lax.all_to_all(outgoing.reshape(32, SLOT, 1024), ('core', 'xy'), split_ax...  7.16 us
  transfers between devices with their start and end apart: 17, of which 10 were waited for; matrix products, arithmetic and copies ran while one was open for 1% of the time, Pallas kernels for 7%

profile of v7, /device:TPU:6, one launch (start us, length us, event | category | flops | bytes accessed | tf_op | source)
XLA Modules:
  0.0 175.5 jit_solution(4430585889692677577)
XLA Ops:
  6.5 1.7 shard_map.98
  8.3 0.0 all-gather.3.cloned.1.call-update
  8.3 2.1 %shard_map.91 = bf16[16,192,128]{2,1,0:T(8,128)(2,1)} custom-call(bf16[1,128,1024]{2,1,0:T(8,128)(2,1)} %q_ref.1, bf16[1,128,1024]{2,1,0:T(8,128)(2,1)} %k_ref.1, bf16[1,128,1024]{2,1,0:T(8,128)(2,1)} %v_ref.1), custom_call_target="tpu_custom_call" | custom-call | bytes 20971520 | tf_op jit(solution)/shard_map/pallas_call | solution.py:112
  10.4 0.0 copy-start.3
  10.4 0.0 copy-start.4
  10.4 0.0 copy-start.5
  10.5 12.8 %all-to-all-start = ((bf16[16,192,128]{2,1,0:T(8,128)(2,1)}), bf16[16,192,128]{2,1,0:T(8,128)(2,1)S(1)}, u32[]{:S(2)}, u32[]{:S(2)}) async-start(bf16[16,192,128]{2,1,0:T(8,128)(2,1)} %shard_map.91), calls=%async_computation | async-start | bytes 1572864 | tf_op jit(solution)/shard_map/all_to_all | solution.py:400
  23.2 8.7 %collective-permute-start = (bf16[32,1024]{1,0:T(8,128)(2,1)}, bf16[32,1024]{1,0:T(8,128)(2,1)S(1)}, u32[]{:S(2)}, u32[]{:S(2)}) collective-permute-start(bf16[32,1024]{1,0:T(8,128)(2,1)} %param.13), channel_id=1, source_target_pairs={{0,464},{1,465},{2,466},{3,467},{4,468},{5,469},{6,470},{7,471},{8... | collective-permute-start | bytes 196616 | tf_op jit(solution)/shard_map/ppermute | solution.py:395
  31.9 2.2 %collective-permute-done = bf16[32,1024]{1,0:T(8,128)(2,1)S(1)} collective-permute-done((bf16[32,1024]{1,0:T(8,128)(2,1)}, bf16[32,1024]{1,0:T(8,128)(2,1)S(1)}, u32[]{:S(2)}, u32[]{:S(2)}) %collective-permute-start) | collective-permute-done | bytes 65568 | tf_op jit(solution)/shard_map/ppermute | solution.py:395
  34.1 0.8 broadcast_select_fusion.refs_0_
  35.0 2.4 %collective-permute-start.3 = (bf16[32,1024]{1,0:T(8,128)(2,1)S(1)}, bf16[32,1024]{1,0:T(8,128)(2,1)S(1)}, u32[]{:S(2)}, u32[]{:S(2)}) collective-permute-start(bf16[32,1024]{1,0:T(8,128)(2,1)S(1)} %broadcast_select_fusion.refs_0_), channel_id=1, source_target_pairs={{0,4},{1,5},{2,6},{3,7},{4,8},{5,9},{6,10},{7,11},{8,12},{9,13},{1... | collective-permute-start | bytes 196616 | tf_op jit(solution)/shard_map/ppermute | solution.py:397
  37.4 4.3 %collective-permute-start.2 = (bf16[32,1024]{1,0:T(8,128)(2,1)S(1)}, bf16[32,1024]{1,0:T(8,128)(2,1)S(1)}, u32[]{:S(2)}, u32[]{:S(2)}) collective-permute-start(bf16[32,1024]{1,0:T(8,128)(2,1)S(1)} %broadcast_select_fusion.refs_0_), channel_id=1, source_target_pairs={{0,8},{1,9},{2,10},{3,11},{4,12},{5,13},{6,14},{7,15},{8,0},{9,1},... | collective-permute-start | bytes 196616 | tf_op jit(solution)/shard_map/ppermute | solution.py:397
  41.7 1.9 %collective-permute-start.1 = (bf16[32,1024]{1,0:T(8,128)(2,1)S(1)}, bf16[32,1024]{1,0:T(8,128)(2,1)S(1)}, u32[]{:S(2)}, u32[]{:S(2)}) collective-permute-start(bf16[32,1024]{1,0:T(8,128)(2,1)S(1)} %broadcast_select_fusion.refs_0_), channel_id=1, source_target_pairs={{0,12},{1,13},{2,14},{3,15},{4,0},{5,1},{6,2},{7,3},{8,4},{9,5},{1... | collective-permute-start | bytes 196616 | tf_op jit(solution)/shard_map/ppermute | solution.py:397
  43.6 0.0 collective-permute-done.3.refs_3_
  43.6 1.4 collective-permute-done.2.refs_2_
  45.0 4.0 %collective-permute-done.1.refs_1_ = bf16[32,1024]{1,0:T(8,128)(2,1)S(1)} collective-permute-done((bf16[32,1024]{1,0:T(8,128)(2,1)S(1)}, bf16[32,1024]{1,0:T(8,128)(2,1)S(1)}, u32[]{:S(2)}, u32[]{:S(2)}) %collective-permute-start.1) | collective-permute-done | bytes 65568 | tf_op jit(solution)/shard_map/ppermute | solution.py:397
  49.1 9.8 %all-to-all-done.heads_ref.own_ref = bf16[16,192,128]{2,1,0:T(8,128)(2,1)S(1)} async-done(((bf16[16,192,128]{2,1,0:T(8,128)(2,1)}), bf16[16,192,128]{2,1,0:T(8,128)(2,1)S(1)}, u32[]{:S(2)}, u32[]{:S(2)}) %all-to-all-start) | async-done | bytes 786464 | tf_op jit(solution)/shard_map/all_to_all | solution.py:400
  58.9 5.5 %collective-permute-start.4 = (bf16[16,128,128]{2,1,0:T(8,128)(2,1)S(1)}, bf16[16,128,128]{2,1,0:T(8,128)(2,1)S(1)}, u32[]{:S(2)}, u32[]{:S(2)}) collective-permute-start(bf16[16,128,128]{2,1,0:T(8,128)(2,1)S(1)} %shard_map.92), channel_id=1, source_target_pairs={{0,32},{1,33},{2,34},{3,35},{4,36},{5,37},{6,38},{7,39},{8,40},{9,... | collective-permute-start | bytes 1572872 | tf_op jit(solution)/shard_map/ppermute | solution.py:401
  64.5 1.5 collective-permute-done.4.oth_ref
  66.0 3.2 %shard_map.93.refs_4_ = bf16[16,64,128]{2,1,0:T(8,128)(2,1)} custom-call(s32[1]{0:T(128)} %bitcast.core_ref, bf16[16,192,128]{2,1,0:T(8,128)(2,1)S(1)} %all-to-all-done.heads_ref.own_ref, bf16[16,128,128]{2,1,0:T(8,128)(2,1)S(1)} %collective-permute-done.4.oth_ref), custom_call_target="tpu_custom_call" | custom-call | flops 671088640 | bytes 2097152 | tf_op jit(solution)/shard_map/pallas_call | solution.py:207
  69.2 22.3 %all-to-all-start.1 = ((bf16[16,64,128]{2,1,0:T(8,128)(2,1)}), bf16[16,64,128]{2,1,0:T(8,128)(2,1)S(1)}, u32[]{:S(2)}, u32[]{:S(2)}) async-start(bf16[16,64,128]{2,1,0:T(8,128)(2,1)} %shard_map.93.refs_4_), calls=%async_computation.1 | async-start | bytes 524288 | tf_op jit(solution)/shard_map/all_to_all | solution.py:408
  91.5 4.4 %collective-permute-start.5 = (bf16[4,32,1024]{2,1,0:T(8,128)(2,1)S(1)}, bf16[4,32,1024]{2,1,0:T(8,128)(2,1)S(1)}, u32[]{:S(2)}, u32[]{:S(2)}) collective-permute-start(bf16[4,32,1024]{2,1,0:T(8,128)(2,1)S(1)} %shard_map.94.refs_0_), channel_id=1, source_target_pairs={{0,3},{1,0},{2,1},{3,2},{4,7},{5,4},{6,5},{7,6},{8,11},{9,8},{10,9... | collective-permute-start | bytes 786440 | tf_op jit(solution)/shard_map/ppermute | solution.py:405
  95.9 1.9 %collective-permute-start.7 = (bf16[4,32,1024]{2,1,0:T(8,128)(2,1)S(1)}, bf16[4,32,1024]{2,1,0:T(8,128)(2,1)S(1)}, u32[]{:S(2)}, u32[]{:S(2)}) collective-permute-start(bf16[4,32,1024]{2,1,0:T(8,128)(2,1)S(1)} %shard_map.94.refs_0_), channel_id=1, source_target_pairs={{0,1},{1,2},{2,3},{3,0},{4,5},{5,6},{6,7},{7,4},{8,9},{9,10},{10,1... | collective-permute-start | bytes 786440 | tf_op jit(solution)/shard_map/ppermute | solution.py:405
  97.9 3.4 %collective-permute-start.6 = (bf16[4,32,1024]{2,1,0:T(8,128)(2,1)S(1)}, bf16[4,32,1024]{2,1,0:T(8,128)(2,1)S(1)}, u32[]{:S(2)}, u32[]{:S(2)}) collective-permute-start(bf16[4,32,1024]{2,1,0:T(8,128)(2,1)S(1)} %shard_map.94.refs_0_), channel_id=1, source_target_pairs={{0,2},{1,3},{2,0},{3,1},{4,6},{5,7},{6,4},{7,5},{8,10},{9,11},{10,... | collective-permute-start | bytes 786440 | tf_op jit(solution)/shard_map/ppermute | solution.py:405
  101.2 0.0 collective-permute-done.5.refs_1_
  101.3 1.9 %collective-permute-start.8 = (bf16[2,4,32,1024]{3,2,1,0:T(8,128)(2,1)S(1)}, bf16[2,4,32,1024]{3,2,1,0:T(8,128)(2,1)S(1)}, u32[]{:S(2)}, u32[]{:S(2)}) collective-permute-start(bf16[2,4,32,1024]{3,2,1,0:T(8,128)(2,1)S(1)} %shard_map.95.refs_0_), channel_id=1, source_target_pairs={{0,32},{1,33},{2,34},{3,35},{4,36},{5,37},{6,38},{7,39},{8,40},{9,... | collective-permute-start | bytes 1572872 | tf_op jit(solution)/shard_map/ppermute | solution.py:407
  103.2 5.0 %collective-permute-done.7.refs_1_ = bf16[4,32,1024]{2,1,0:T(8,128)(2,1)S(1)} collective-permute-done((bf16[4,32,1024]{2,1,0:T(8,128)(2,1)S(1)}, bf16[4,32,1024]{2,1,0:T(8,128)(2,1)S(1)}, u32[]{:S(2)}, u32[]{:S(2)}) %collective-permute-start.7) | collective-permute-done | bytes 262176 | tf_op jit(solution)/shard_map/ppermute | solution.py:405
  108.3 1.9 %collective-permute-start.9 = (bf16[2,4,32,1024]{3,2,1,0:T(8,128)(2,1)S(1)}, bf16[2,4,32,1024]{3,2,1,0:T(8,128)(2,1)S(1)}, u32[]{:S(2)}, u32[]{:S(2)}) collective-permute-start(bf16[2,4,32,1024]{3,2,1,0:T(8,128)(2,1)S(1)} %shard_map.96.refs_1_), channel_id=1, source_target_pairs={{0,32},{1,33},{2,34},{3,35},{4,36},{5,37},{6,38},{7,39},{8,40},{9,... | collective-permute-start | bytes 1572872 | tf_op jit(solution)/shard_map/ppermute | solution.py:407
  110.2 0.1 pad_add_fusion.where_ref
  110.3 0.0 collective-permute-done.8.refs_2_
  110.3 1.8 %collective-permute-done.9.refs_3_ = bf16[2,4,32,1024]{3,2,1,0:T(8,128)(2,1)S(1)} collective-permute-done((bf16[2,4,32,1024]{3,2,1,0:T(8,128)(2,1)S(1)}, bf16[2,4,32,1024]{3,2,1,0:T(8,128)(2,1)S(1)}, u32[]{:S(2)}, u32[]{:S(2)}) %collective-permute-start.9) | collective-permute-done | bytes 524320 | tf_op jit(solution)/shard_map/ppermute | solution.py:407
  112.1 0.0 all-to-all-done.1.ctx_ref
  112.1 2.9 %shard_map.97 = (bf16[128,1024]{1,0:T(8,128)(2,1)S(1)}, bf16[512,1024]{1,0:T(8,128)(2,1)}, f32[2,128]{1,0:T(2,128)S(1)}, s32[2,128]{1,0:T(2,128)S(1)}) custom-call(s32[3]{0:T(128)S(1)} %pad_add_fusion.where_ref, bf16[16,64,128]{2,1,0:T(8,128)(2,1)S(1)} %all-to-all-done.1.ctx_ref, bf16[2,4,32,1024]{3,2,1,0:T(8,128)(2,1)S(1)} %shard_map.95.refs_0_, ...), custom_call_target="tpu_custom_call" | custom-call | flops 419430400 | bytes 4194304 | tf_op jit(solution)/shard_map/pallas_call | solution.py:272
  114.9 0.7 copy-done.1
  115.6 7.2 %all-to-all-start.2 = ((bf16[32,16,1024]{2,1,0:T(8,128)(2,1)}), bf16[32,16,1024]{2,1,0:T(8,128)(2,1)S(1)}, u32[]{:S(2)}, u32[]{:S(2)}) async-start(bf16[32,16,1024]{2,1,0:T(8,128)(2,1)} %bitcast.5), calls=%async_computation.2 | async-start | bytes 2097152 | tf_op jit(solution)/shard_map/all_to_all | solution.py:415
  122.8 5.6 %all-gather.3.cloned.1.call-done = bf16[2304,1024]{1,0:T(8,128)(2,1)} async-done(((bf16[144,1024]{1,0:T(8,128)(2,1)}), bf16[2304,1024]{1,0:T(8,128)(2,1)}) %all-gather.3.cloned.1.call-update) | async-done | bytes 4718608 | tf_op jit(solution)/shard_map/all_gather | solution.py:393
  128.4 3.2 %shard_map.100 = (bf16[3,144,1024]{2,1,0:T(8,128)(2,1)}, bf16[3,144,1024]{2,1,0:T(8,128)(2,1)}, bf16[2,144,1024]{2,1,0:T(8,128)(2,1)}) custom-call(s32[1]{0:T(128)} %bitcast.core_ref, bf16[16,144,1024]{2,1,0:T(8,128)(2,1)} %bitcast.11, s32[2,128]{1,0:T(2,128)S(1)} %get-tuple-element.13.after_ref.target_ref), custom_call_target="tpu_custom_call" | custom-call | bytes 8388608 | tf_op jit(solution)/shard_map/pallas_call | solution.py:310
  131.6 1.9 %collective-permute-start.10 = (bf16[3,144,1024]{2,1,0:T(8,128)(2,1)}, bf16[3,144,1024]{2,1,0:T(8,128)(2,1)}, u32[]{:S(2)}, u32[]{:S(2)}) collective-permute-start(bf16[3,144,1024]{2,1,0:T(8,128)(2,1)} %get-tuple-element.14), channel_id=1, source_target_pairs={{0,32},{1,33},{2,34},{3,35},{4,36},{5,37},{6,38},{7,39},{8,40},{9,... | collective-permute-start | bytes 2654216 | tf_op jit(solution)/shard_map/ppermute | solution.py:419
  133.6 2.4 %collective-permute-start.11 = (bf16[3,144,1024]{2,1,0:T(8,128)(2,1)}, bf16[3,144,1024]{2,1,0:T(8,128)(2,1)}, u32[]{:S(2)}, u32[]{:S(2)}) collective-permute-start(bf16[3,144,1024]{2,1,0:T(8,128)(2,1)} %get-tuple-element.15), channel_id=1, source_target_pairs={{0,32},{1,33},{2,34},{3,35},{4,36},{5,37},{6,38},{7,39},{8,40},{9,... | collective-permute-start | bytes 2654216 | tf_op jit(solution)/shard_map/ppermute | solution.py:419
  136.0 1.9 %collective-permute-start.12 = (bf16[2,144,1024]{2,1,0:T(8,128)(2,1)}, bf16[2,144,1024]{2,1,0:T(8,128)(2,1)}, u32[]{:S(2)}, u32[]{:S(2)}) collective-permute-start(bf16[2,144,1024]{2,1,0:T(8,128)(2,1)} %get-tuple-element.16), channel_id=1, source_target_pairs={{0,32},{1,33},{2,34},{3,35},{4,36},{5,37},{6,38},{7,39},{8,40},{9,... | collective-permute-start | bytes 1769480 | tf_op jit(solution)/shard_map/ppermute | solution.py:419
  137.9 0.2 shard_map.99.own_ref
  138.1 0.3 all-to-all-done.2
  138.4 1.9 %collective-permute-done.12.refs_2_ = bf16[2,144,1024]{2,1,0:T(8,128)(2,1)} collective-permute-done((bf16[2,144,1024]{2,1,0:T(8,128)(2,1)}, bf16[2,144,1024]{2,1,0:T(8,128)(2,1)}, u32[]{:S(2)}, u32[]{:S(2)}) %collective-permute-start.12) | collective-permute-done | bytes 589856 | tf_op jit(solution)/shard_map/ppermute | solution.py:419
  140.2 0.0 collective-permute-done.10.refs_0_
  140.2 0.0 collective-permute-done.11.refs_1_
  140.2 4.5 %shard_map.101 = bf16[512,1024]{1,0:T(8,128)(2,1)S(1)} custom-call(s32[1]{0:T(128)} %bitcast.core_ref, bf16[512,1024]{1,0:T(8,128)(2,1)S(1)} %bitcast.14, bf16[8,144,1024]{2,1,0:T(8,128)(2,1)S(1)} %shard_map.99.own_ref, bf16[3,144,1024]{2,1,0:T(8,128)(2,1)} %collective-permute-done.10.refs_0_, bf16[3,144,1024]{2,1,0:T(8,128)(2,1)} %collective-permute-done.11.refs_1_, ...), custom_call_target="tpu_custom_call" | custom-call | flops 2415919104 | bytes 7340032 | tf_op jit(solution)/shard_map/pallas_call | solution.py:344
  144.7 22.7 %all_to_all.20 = bf16[32,16,1024]{2,1,0:T(8,128)(2,1)S(1)} all-to-all(bf16[32,16,1024]{2,1,0:T(8,128)(2,1)S(1)} %bitcast.15), channel_id=1, replica_groups=mesh['zlo'=8,'core'=2,'zhi'=2,'xy'=16] {'core','xy'}, dimensions={0} | all-to-all | bytes 2097152 | tf_op jit(solution)/shard_map/all_to_all | solution.py:422
  167.4 1.2 shard_map.102
  (14 shorter events, 0.1 us)
Async XLA Ops:
  6.5 121.9 %all-gather.3.cloned.1.call-start = ((), (), s32[]{:S(2)}) async-start(), calls=%async_computation.4 | async-start | bytes 5013504 | tf_op jit(solution)/shard_map/all_gather | solution.py:393
  10.4 101.7 %copy-start.3 = (bf16[1,128,1024]{2,1,0:T(8,128)(2,1)S(1)}, bf16[1,128,1024]{2,1,0:T(8,128)(2,1)}, u32[]{:S(2)}) copy-start(bf16[1,128,1024]{2,1,0:T(8,128)(2,1)} %refs_4_.1) | copy-start | bytes 786436
  10.4 101.6 %copy-start.4 = (bf16[1024,32]{0,1:T(8,128)(2,1)S(1)}, bf16[1024,32]{0,1:T(8,128)(2,1)}, u32[]{:S(2)}) copy-start(bf16[1024,32]{0,1:T(8,128)(2,1)} %param.14) | copy-start | bytes 196612
  10.4 101.6 %copy-start.5 = (s32[1,128,2]{1,2,0:T(2,128)S(1)}, s32[1,128,2]{1,2,0:T(2,128)}, u32[]{:S(2)}) copy-start(s32[1,128,2]{1,2,0:T(2,128)} %param.15) | copy-start | bytes 3076
  10.5 48.4 %all-to-all-start = ((bf16[16,192,128]{2,1,0:T(8,128)(2,1)}), bf16[16,192,128]{2,1,0:T(8,128)(2,1)S(1)}, u32[]{:S(2)}, u32[]{:S(2)}) async-start(bf16[16,192,128]{2,1,0:T(8,128)(2,1)} %shard_map.91), calls=%async_computation | async-start | bytes 1572864 | tf_op jit(solution)/shard_map/all_to_all | solution.py:400
  23.2 10.9 %collective-permute-start = (bf16[32,1024]{1,0:T(8,128)(2,1)}, bf16[32,1024]{1,0:T(8,128)(2,1)S(1)}, u32[]{:S(2)}, u32[]{:S(2)}) collective-permute-start(bf16[32,1024]{1,0:T(8,128)(2,1)} %param.13), channel_id=1, source_target_pairs={{0,464},{1,465},{2,466},{3,467},{4,468},{5,469},{6,470},{7,471},{8... | collective-permute-start | bytes 196616 | tf_op jit(solution)/shard_map/ppermute | solution.py:395
  35.0 8.7 %collective-permute-start.3 = (bf16[32,1024]{1,0:T(8,128)(2,1)S(1)}, bf16[32,1024]{1,0:T(8,128)(2,1)S(1)}, u32[]{:S(2)}, u32[]{:S(2)}) collective-permute-start(bf16[32,1024]{1,0:T(8,128)(2,1)S(1)} %broadcast_select_fusion.refs_0_), channel_id=1, source_target_pairs={{0,4},{1,5},{2,6},{3,7},{4,8},{5,9},{6,10},{7,11},{8,12},{9,13},{1... | collective-permute-start | bytes 196616 | tf_op jit(solution)/shard_map/ppermute | solution.py:397
  37.4 7.7 %collective-permute-start.2 = (bf16[32,1024]{1,0:T(8,128)(2,1)S(1)}, bf16[32,1024]{1,0:T(8,128)(2,1)S(1)}, u32[]{:S(2)}, u32[]{:S(2)}) collective-permute-start(bf16[32,1024]{1,0:T(8,128)(2,1)S(1)} %broadcast_select_fusion.refs_0_), channel_id=1, source_target_pairs={{0,8},{1,9},{2,10},{3,11},{4,12},{5,13},{6,14},{7,15},{8,0},{9,1},... | collective-permute-start | bytes 196616 | tf_op jit(solution)/shard_map/ppermute | solution.py:397
  41.7 7.4 %collective-permute-start.1 = (bf16[32,1024]{1,0:T(8,128)(2,1)S(1)}, bf16[32,1024]{1,0:T(8,128)(2,1)S(1)}, u32[]{:S(2)}, u32[]{:S(2)}) collective-permute-start(bf16[32,1024]{1,0:T(8,128)(2,1)S(1)} %broadcast_select_fusion.refs_0_), channel_id=1, source_target_pairs={{0,12},{1,13},{2,14},{3,15},{4,0},{5,1},{6,2},{7,3},{8,4},{9,5},{1... | collective-permute-start | bytes 196616 | tf_op jit(solution)/shard_map/ppermute | solution.py:397
  58.9 7.0 %collective-permute-start.4 = (bf16[16,128,128]{2,1,0:T(8,128)(2,1)S(1)}, bf16[16,128,128]{2,1,0:T(8,128)(2,1)S(1)}, u32[]{:S(2)}, u32[]{:S(2)}) collective-permute-start(bf16[16,128,128]{2,1,0:T(8,128)(2,1)S(1)} %shard_map.92), channel_id=1, source_target_pairs={{0,32},{1,33},{2,34},{3,35},{4,36},{5,37},{6,38},{7,39},{8,40},{9,... | collective-permute-start | bytes 1572872 | tf_op jit(solution)/shard_map/ppermute | solution.py:401
  69.2 42.9 %all-to-all-start.1 = ((bf16[16,64,128]{2,1,0:T(8,128)(2,1)}), bf16[16,64,128]{2,1,0:T(8,128)(2,1)S(1)}, u32[]{:S(2)}, u32[]{:S(2)}) async-start(bf16[16,64,128]{2,1,0:T(8,128)(2,1)} %shard_map.93.refs_4_), calls=%async_computation.1 | async-start | bytes 524288 | tf_op jit(solution)/shard_map/all_to_all | solution.py:408
  91.5 9.7 %collective-permute-start.5 = (bf16[4,32,1024]{2,1,0:T(8,128)(2,1)S(1)}, bf16[4,32,1024]{2,1,0:T(8,128)(2,1)S(1)}, u32[]{:S(2)}, u32[]{:S(2)}) collective-permute-start(bf16[4,32,1024]{2,1,0:T(8,128)(2,1)S(1)} %shard_map.94.refs_0_), channel_id=1, source_target_pairs={{0,3},{1,0},{2,1},{3,2},{4,7},{5,4},{6,5},{7,6},{8,11},{9,8},{10,9... | collective-permute-start | bytes 786440 | tf_op jit(solution)/shard_map/ppermute | solution.py:405
  95.9 12.3 %collective-permute-start.7 = (bf16[4,32,1024]{2,1,0:T(8,128)(2,1)S(1)}, bf16[4,32,1024]{2,1,0:T(8,128)(2,1)S(1)}, u32[]{:S(2)}, u32[]{:S(2)}) collective-permute-start(bf16[4,32,1024]{2,1,0:T(8,128)(2,1)S(1)} %shard_map.94.refs_0_), channel_id=1, source_target_pairs={{0,1},{1,2},{2,3},{3,0},{4,5},{5,6},{6,7},{7,4},{8,9},{9,10},{10,1... | collective-permute-start | bytes 786440 | tf_op jit(solution)/shard_map/ppermute | solution.py:405
  97.9 10.4 %collective-permute-start.6 = (bf16[4,32,1024]{2,1,0:T(8,128)(2,1)S(1)}, bf16[4,32,1024]{2,1,0:T(8,128)(2,1)S(1)}, u32[]{:S(2)}, u32[]{:S(2)}) collective-permute-start(bf16[4,32,1024]{2,1,0:T(8,128)(2,1)S(1)} %shard_map.94.refs_0_), channel_id=1, source_target_pairs={{0,2},{1,3},{2,0},{3,1},{4,6},{5,7},{6,4},{7,5},{8,10},{9,11},{10,... | collective-permute-start | bytes 786440 | tf_op jit(solution)/shard_map/ppermute | solution.py:405
  101.3 9.0 %collective-permute-start.8 = (bf16[2,4,32,1024]{3,2,1,0:T(8,128)(2,1)S(1)}, bf16[2,4,32,1024]{3,2,1,0:T(8,128)(2,1)S(1)}, u32[]{:S(2)}, u32[]{:S(2)}) collective-permute-start(bf16[2,4,32,1024]{3,2,1,0:T(8,128)(2,1)S(1)} %shard_map.95.refs_0_), channel_id=1, source_target_pairs={{0,32},{1,33},{2,34},{3,35},{4,36},{5,37},{6,38},{7,39},{8,40},{9,... | collective-permute-start | bytes 1572872 | tf_op jit(solution)/shard_map/ppermute | solution.py:407
  108.3 3.8 %collective-permute-start.9 = (bf16[2,4,32,1024]{3,2,1,0:T(8,128)(2,1)S(1)}, bf16[2,4,32,1024]{3,2,1,0:T(8,128)(2,1)S(1)}, u32[]{:S(2)}, u32[]{:S(2)}) collective-permute-start(bf16[2,4,32,1024]{3,2,1,0:T(8,128)(2,1)S(1)} %shard_map.96.refs_1_), channel_id=1, source_target_pairs={{0,32},{1,33},{2,34},{3,35},{4,36},{5,37},{6,38},{7,39},{8,40},{9,... | collective-permute-start | bytes 1572872 | tf_op jit(solution)/shard_map/ppermute | solution.py:407
  114.9 0.7 copy-start.1
  115.6 22.7 %all-to-all-start.2 = ((bf16[32,16,1024]{2,1,0:T(8,128)(2,1)}), bf16[32,16,1024]{2,1,0:T(8,128)(2,1)S(1)}, u32[]{:S(2)}, u32[]{:S(2)}) async-start(bf16[32,16,1024]{2,1,0:T(8,128)(2,1)} %bitcast.5), calls=%async_computation.2 | async-start | bytes 2097152 | tf_op jit(solution)/shard_map/all_to_all | solution.py:415
  128.4 9.5 %copy-start = (bf16[2304,1024]{1,0:T(8,128)(2,1)S(1)}, bf16[2304,1024]{1,0:T(8,128)(2,1)}, u32[]{:S(2)}) copy-start(bf16[2304,1024]{1,0:T(8,128)(2,1)} %all-gather.3.cloned.1.call-done) | copy-start | bytes 14155780
  131.6 8.6 %collective-permute-start.10 = (bf16[3,144,1024]{2,1,0:T(8,128)(2,1)}, bf16[3,144,1024]{2,1,0:T(8,128)(2,1)}, u32[]{:S(2)}, u32[]{:S(2)}) collective-permute-start(bf16[3,144,1024]{2,1,0:T(8,128)(2,1)} %get-tuple-element.14), channel_id=1, source_target_pairs={{0,32},{1,33},{2,34},{3,35},{4,36},{5,37},{6,38},{7,39},{8,40},{9,... | collective-permute-start | bytes 2654216 | tf_op jit(solution)/shard_map/ppermute | solution.py:419
  133.6 6.7 %collective-permute-start.11 = (bf16[3,144,1024]{2,1,0:T(8,128)(2,1)}, bf16[3,144,1024]{2,1,0:T(8,128)(2,1)}, u32[]{:S(2)}, u32[]{:S(2)}) collective-permute-start(bf16[3,144,1024]{2,1,0:T(8,128)(2,1)} %get-tuple-element.15), channel_id=1, source_target_pairs={{0,32},{1,33},{2,34},{3,35},{4,36},{5,37},{6,38},{7,39},{8,40},{9,... | collective-permute-start | bytes 2654216 | tf_op jit(solution)/shard_map/ppermute | solution.py:419
  136.0 4.2 %collective-permute-start.12 = (bf16[2,144,1024]{2,1,0:T(8,128)(2,1)}, bf16[2,144,1024]{2,1,0:T(8,128)(2,1)}, u32[]{:S(2)}, u32[]{:S(2)}) collective-permute-start(bf16[2,144,1024]{2,1,0:T(8,128)(2,1)} %get-tuple-element.16), channel_id=1, source_target_pairs={{0,32},{1,33},{2,34},{3,35},{4,36},{5,37},{6,38},{7,39},{8,40},{9,... | collective-permute-start | bytes 1769480 | tf_op jit(solution)/shard_map/ppermute | solution.py:419
  140.2 27.2 %copy-start.2 = (bf16[128,1024]{1,0:T(8,128)(2,1)S(1)}, bf16[128,1024]{1,0:T(8,128)(2,1)}, u32[]{:S(2)}) copy-start(bf16[128,1024]{1,0:T(8,128)(2,1)} %copy-done.1) | copy-start | bytes 786436
Sparse Core Ops, SparseCore 0:
  9.4 118.9 all-gather.2
